TPU v7x, 512 devices: a whole 4x8x8 slice. The times are simulated.
512 devices in a mesh: row: 64 (over z, x, core), col: 8 (over y).
Axes of the slice: x: 4, y: 8, z: 8, core: 2. Of those that a mesh axis runs over, the one named last changes fastest.
Arguments:
- front_in: float32 [32768, 4096], P('row', 'col')
- child_block: float32 [32768, 2048], P('row', 'col'), may hold values from -6 to 6
- child_rows: int32 [32768], P('row'), may hold values from 0 to 32767, as said below
- live_counts: int32 [64, 64], P('row'), may hold values from 0 to 8, as said below
- column_map: int32 [2048], P('col'), may hold values from 0 to 4095, as said below
Outputs:
- parent_front: float32 [32768, 4096], P('row', 'col')
- factor_rows: float32 [512, 4096], P(None, 'col')
Inputs may be any that keep to these rules, and one draw needn't show every extreme that they name: `child_rows`: child row i of each row block (0 <= i < 512) goes to a parent row of row block i // 8, that is into rows (i // 8) * 512 to (i // 8 + 1) * 512 - 1; parent rows may repeat. Each row of live_counts holds both 0 and 8. `column_map`: the child columns held by column block c map to distinct parent columns of the same block, c * 512 to (c + 1) * 512 - 1.
All inputs are finite; a program needn't handle non-finite values.
Results may differ from a plain program's by a relative error of at most 0.00029.
Values sent between devices are 32-bit elements; how exact they have to be, the bound alone decides.
No kernel may reach another device: no remote copies, remote signals or barrier semaphores. Data moves between devices by JAX's collectives and lax.ppermute only.
A program may use at most 64 MiB of HBM per device.

v0:
```python
import math

import jax
import jax.numpy as jnp
from jax import lax
from jax.sharding import PartitionSpec as P

PANEL = 256


def swapped(shard, axis, apart):
    return lax.ppermute(shard, axis, [(i, i ^ 1 << apart) for i in range(lax.axis_size(axis))])


def from_root(shard, axis, root):
    mine = lax.axis_index(axis) == root
    return lax.psum(jnp.where(mine, shard, jnp.zeros_like(shard)), axis)


def factor_panel(panel_cols, highest):
    gram_matrix = jnp.dot(panel_cols.T, panel_cols, precision=highest)
    for bit_index in range(lax.axis_size("row").bit_length() - 1):
        partner = swapped(gram_matrix, "row", bit_index)
        gram_matrix = gram_matrix + partner
    upper_factor = jnp.linalg.cholesky(gram_matrix).T
    basis_cols = jax.scipy.linalg.solve_triangular(upper_factor.T, panel_cols.T, lower=True).T
    return (upper_factor, basis_cols)


def on_device(front_in, child_block, child_rows, live_counts, column_map):
    highest = lax.Precision.HIGHEST
    rows_dev, cols_dev = front_in.shape
    owners = lax.axis_size("row")
    capacity = child_block.shape[0] // owners
    child_width = child_block.shape[1]
    slot_index = jnp.arange(capacity, dtype=jnp.int32)
    live_mask = (slot_index[None, :] < live_counts[0][:, None]).astype(jnp.float32)
    payload = child_block.reshape(owners, capacity, child_width) * live_mask[:, :, None]
    targets = child_rows.reshape(owners, capacity)
    arrived, arrived_rows = (
        lax.all_to_all(payload, "row", split_axis=0, concat_axis=0, tiled=True),
        lax.all_to_all(targets, "row", split_axis=0, concat_axis=0, tiled=True),
    )
    local_cols = column_map % cols_dev
    one_hot = (local_cols[:, None] == jnp.arange(cols_dev, dtype=jnp.int32)[None, :]).astype(
        jnp.float32
    )
    placed = jnp.dot(arrived.reshape(owners * capacity, child_width), one_hot, precision=highest)
    parent_front = front_in.at[arrived_rows.reshape(owners * capacity) % rows_dev].add(placed)
    global_cols = lax.axis_index("col") * cols_dev + jnp.arange(cols_dev, dtype=jnp.int32)
    root_rows = math.sqrt(rows_dev * owners)
    blocks = []
    for panel_index in range(2):
        first_col = panel_index * PANEL
        last_col = first_col + PANEL
        upper_factor, basis_cols = factor_panel(parent_front[:, first_col:last_col], highest)
        basis_cols = from_root(basis_cols, "col", 0)
        product = lax.psum(jnp.dot(basis_cols.T, parent_front, precision=highest), "row")
        trailing = (global_cols >= last_col)[None, :]
        in_panel = ((global_cols >= first_col) & (global_cols < last_col))[None, :]
        coupled = jnp.where(trailing, product, jnp.zeros_like(product))
        parent_front = parent_front - jnp.dot(basis_cols, coupled, precision=highest)
        widths = ((0, 0), (first_col, cols_dev - last_col))
        parent_front = jnp.where(in_panel, jnp.pad(basis_cols * root_rows, widths), parent_front)
        blocks.append(jnp.where(in_panel, jnp.pad(upper_factor, widths), coupled) / root_rows)
    return (parent_front, jnp.concatenate(blocks, axis=0))


def solution(mesh):
    return jax.shard_map(
        on_device,
        mesh=mesh,
        in_specs=(P("row", "col"), P("row", "col"), P("row"), P("row", None), P("col")),
        out_specs=(P("row", "col"), P(None, "col")),
        check_vma=False,
    )
```

profile of v0, /device:TPU:1, one launch (start us, length us, event | category | flops | bytes accessed | tf_op | source)
XLA Modules:
  0.0 877.0 jit_solution(3618747720132949880)
XLA Ops:
  8.6 14.8 %all-to-all-start = ((s32[64,1,8]{2,1,0:T(1,128)}), s32[64,1,8]{2,1,0:T(1,128)S(1)}, u32[]{:S(2)}, u32[]{:S(2)}) async-start(s32[64,1,8]{2,1,0:T(1,128)} %bitcast), calls=%async_computation | async-start | bytes 65536 | tf_op jit(solution)/shard_map/all_to_all | solution.py:42
  25.1 7.6 all-to-all-done
  39.2 16.3 %all-to-all-done.1 = f32[64,8,256]{2,1,0:T(8,128)S(1)} async-done(((f32[64,8,256]{2,1,0:T(8,128)}), f32[64,8,256]{2,1,0:T(8,128)S(1)}, u32[]{:S(2)}, u32[]{:S(2)}) %all-to-all-start.1) | async-done | bytes 524320 | tf_op jit(solution)/shard_map/all_to_all | solution.py:41
  67.8 6.3 collective-permute-done.1
  78.8 5.4 collective-permute-done.2
  96.2 11.2 %collective-permute-done.4 = f32[256,256]{0,1:T(8,128)S(1)} collective-permute-done((f32[256,256]{0,1:T(8,128)S(1)}, f32[256,256]{0,1:T(8,128)S(1)}, u32[]{:S(2)}, u32[]{:S(2)}) %collective-permute-start.4) | collective-permute-done | bytes 262176 | tf_op jit(solution)/shard_map/ppermute | solution.py:12
  112.8 14.1 %collective-permute-done.5 = f32[256,256]{0,1:T(8,128)S(1)} collective-permute-done((f32[256,256]{0,1:T(8,128)S(1)}, f32[256,256]{0,1:T(8,128)S(1)}, u32[]{:S(2)}, u32[]{:S(2)}) %collective-permute-start.5) | collective-permute-done | bytes 262176 | tf_op jit(solution)/shard_map/ppermute | solution.py:12
  127.1 11.7 %cholesky.130 = f32[128,128]{1,0:T(8,128)S(1)} custom-call(f32[128,128]{1,0:T(8,128)S(1)} %cholesky.194), custom_call_target="Cholesky" | custom-call | tf_op jit(solution)/shard_map/jit(cholesky)/cholesky | solution.py:25
  138.9 9.8 %custom-call.13 = f32[1,128,128]{1,2,0:T(8,128)S(1)} custom-call(f32[1,128,128]{2,1,0:T(8,128)S(1)} %get-tuple-element.57), custom_call_target="InvertDiagBlocksLowerTriangular" | custom-call | tf_op jit(solution)/shard_map/jit(cholesky)/cholesky | solution.py:25
  149.4 11.7 %cholesky.147 = f32[128,128]{1,0:T(8,128)S(1)} custom-call(f32[128,128]{1,0:T(8,128)S(1)} %slice_subtract_fusion.1), custom_call_target="Cholesky" | custom-call | tf_op jit(solution)/shard_map/jit(cholesky)/cholesky | solution.py:25
  168.0 19.7 %custom-call.14 = f32[2,128,128]{1,2,0:T(8,128)S(1)} custom-call(f32[2,128,128]{2,1,0:T(8,128)S(1)} %get-tuple-element.18), custom_call_target="InvertDiagBlocksLowerTriangular" | custom-call | tf_op jit(solution)/shard_map/jit(_solve_triangular)/triangular_solve | solution.py:26
  190.2 70.7 %all-reduce.10.cloned.1.call-done = f32[512,256]{1,0:T(8,128)} async-done(((f32[512,256]{1,0:T(8,128)}), f32[512,256]{1,0:T(8,128)}) %all-reduce.10.cloned.1.call-update) | async-done | bytes 524304 | tf_op jit(solution)/shard_map/psum | solution.py:17
  265.6 194.4 %all-reduce.12.cloned.1.call-done = f32[256,512]{0,1:T(8,128)} async-done(((f32[256,512]{0,1:T(8,128)}), f32[256,512]{0,1:T(8,128)}) %all-reduce.12.cloned.1.call-update) | async-done | bytes 524304 | tf_op jit(solution)/shard_map/psum | solution.py:58
  471.9 6.6 collective-permute-done.7
  482.6 5.9 collective-permute-done.8
  490.4 5.6 collective-permute-done.9
  499.8 12.5 %collective-permute-done.10 = f32[256,256]{0,1:T(8,128)S(1)} collective-permute-done((f32[256,256]{0,1:T(8,128)S(1)}, f32[256,256]{0,1:T(8,128)S(1)}, u32[]{:S(2)}, u32[]{:S(2)}) %collective-permute-start.10) | collective-permute-done | bytes 262176 | tf_op jit(solution)/shard_map/ppermute | solution.py:12
  516.7 14.4 %collective-permute-done.11 = f32[256,256]{0,1:T(8,128)S(1)} collective-permute-done((f32[256,256]{0,1:T(8,128)S(1)}, f32[256,256]{0,1:T(8,128)S(1)}, u32[]{:S(2)}, u32[]{:S(2)}) %collective-permute-start.11) | collective-permute-done | bytes 262176 | tf_op jit(solution)/shard_map/ppermute | solution.py:12
  531.3 11.7 %cholesky.164 = f32[128,128]{1,0:T(8,128)S(1)} custom-call(f32[128,128]{1,0:T(8,128)S(1)} %cholesky.197), custom_call_target="Cholesky" | custom-call | tf_op jit(solution)/shard_map/jit(cholesky)/cholesky | solution.py:25
  543.1 9.8 %custom-call.15 = f32[1,128,128]{1,2,0:T(8,128)S(1)} custom-call(f32[1,128,128]{2,1,0:T(8,128)S(1)} %get-tuple-element.53), custom_call_target="InvertDiagBlocksLowerTriangular" | custom-call | tf_op jit(solution)/shard_map/jit(cholesky)/cholesky | solution.py:25
  553.6 11.7 %cholesky.181 = f32[128,128]{1,0:T(8,128)S(1)} custom-call(f32[128,128]{1,0:T(8,128)S(1)} %slice_subtract_fusion), custom_call_target="Cholesky" | custom-call | tf_op jit(solution)/shard_map/jit(cholesky)/cholesky | solution.py:25
  572.2 19.7 %custom-call.16 = f32[2,128,128]{1,2,0:T(8,128)S(1)} custom-call(f32[2,128,128]{2,1,0:T(8,128)S(1)} %get-tuple-element.19), custom_call_target="InvertDiagBlocksLowerTriangular" | custom-call | tf_op jit(solution)/shard_map/jit(_solve_triangular)/triangular_solve | solution.py:26
  594.3 71.3 %all-reduce.14.cloned.1.call-done = f32[512,256]{1,0:T(8,128)} async-done(((f32[512,256]{1,0:T(8,128)}), f32[512,256]{1,0:T(8,128)}) %all-reduce.14.cloned.1.call-update) | async-done | bytes 524304 | tf_op jit(solution)/shard_map/psum | solution.py:17
  672.2 192.1 %all-reduce.16.cloned.1.call-done = f32[256,512]{0,1:T(8,128)} async-done(((f32[256,512]{0,1:T(8,128)}), f32[256,512]{0,1:T(8,128)}) %all-reduce.16.cloned.1.call-update) | async-done | bytes 524304 | tf_op jit(solution)/shard_map/psum | solution.py:58
  (137 shorter events, 112.8 us)
Async XLA Ops:
  7.2 17.0 %copy-start.6 = (f32[512,256]{1,0:T(8,128)S(1)}, f32[512,256]{1,0:T(8,128)}, u32[]{:S(2)}) copy-start(f32[512,256]{1,0:T(8,128)} %param.9) | copy-start | bytes 1572868
  8.6 24.1 %all-to-all-start = ((s32[64,1,8]{2,1,0:T(1,128)}), s32[64,1,8]{2,1,0:T(1,128)S(1)}, u32[]{:S(2)}, u32[]{:S(2)}) async-start(s32[64,1,8]{2,1,0:T(1,128)} %bitcast), calls=%async_computation | async-start | bytes 65536 | tf_op jit(solution)/shard_map/all_to_all | solution.py:42
  32.8 4.9 copy-start.8
  32.8 22.7 %all-to-all-start.1 = ((f32[64,8,256]{2,1,0:T(8,128)}), f32[64,8,256]{2,1,0:T(8,128)S(1)}, u32[]{:S(2)}, u32[]{:S(2)}) async-start(f32[64,8,256]{2,1,0:T(8,128)} %bitcast_multiply_fusion), calls=%async_computation.1 | async-start | bytes 1048576 | tf_op jit(solution)/shard_map/all_to_all | solution.py:41
  37.7 18.5 %copy-start = (f32[512,512]{1,0:T(8,128)S(1)}, f32[512,512]{1,0:T(8,128)}, u32[]{:S(2)}) copy-start(f32[512,512]{1,0:T(8,128)} %param.8) | copy-start | bytes 3145732
  37.7 223.2 %all-reduce.10.cloned.1.call-start = ((), (), s32[]{:S(2)}) async-start(), calls=%async_computation.2 | async-start | bytes 1048576 | tf_op jit(solution)/shard_map/psum | solution.py:17
  61.2 3.5 collective-permute-start
  64.7 9.4 %collective-permute-start.1 = (f32[256,256]{0,1:T(8,128)S(1)}, f32[256,256]{0,1:T(8,128)S(1)}, u32[]{:S(2)}, u32[]{:S(2)}) collective-permute-start(f32[256,256]{0,1:T(8,128)S(1)} %add.125), channel_id=1, source_target_pairs={{0,16},{8,24},{16,0},{24,8},{32,48},{40,56},{48,32},{56,40},{64,80... | collective-permute-start | bytes 786440 | tf_op jit(solution)/shard_map/ppermute | solution.py:12
  74.1 10.0 %collective-permute-start.2 = (f32[256,256]{0,1:T(8,128)S(1)}, f32[256,256]{0,1:T(8,128)S(1)}, u32[]{:S(2)}, u32[]{:S(2)}) collective-permute-start(f32[256,256]{0,1:T(8,128)S(1)} %add.126), channel_id=1, source_target_pairs={{0,32},{8,40},{16,48},{24,56},{32,0},{40,8},{48,16},{56,24},{64,96... | collective-permute-start | bytes 786440 | tf_op jit(solution)/shard_map/ppermute | solution.py:12
  84.2 7.6 collective-permute-start.3
  91.8 15.6 %collective-permute-start.4 = (f32[256,256]{0,1:T(8,128)S(1)}, f32[256,256]{0,1:T(8,128)S(1)}, u32[]{:S(2)}, u32[]{:S(2)}) collective-permute-start(f32[256,256]{0,1:T(8,128)S(1)} %add.128), channel_id=1, source_target_pairs={{0,128},{8,136},{16,144},{24,152},{32,160},{40,168},{48,176},{56,1... | collective-permute-start | bytes 786440 | tf_op jit(solution)/shard_map/ppermute | solution.py:12
  107.5 19.4 %collective-permute-start.5 = (f32[256,256]{0,1:T(8,128)S(1)}, f32[256,256]{0,1:T(8,128)S(1)}, u32[]{:S(2)}, u32[]{:S(2)}) collective-permute-start(f32[256,256]{0,1:T(8,128)S(1)} %add.129), channel_id=1, source_target_pairs={{0,256},{8,264},{16,272},{24,280},{32,288},{40,296},{48,304},{56,3... | collective-permute-start | bytes 786440 | tf_op jit(solution)/shard_map/ppermute | solution.py:12
  190.1 269.9 %all-reduce.12.cloned.1.call-start = ((), (), s32[]{:S(2)}) async-start(), calls=%async_computation.3 | async-start | bytes 1048576 | tf_op jit(solution)/shard_map/psum | solution.py:58
  264.5 1.0 copy-start.2
  264.5 401.2 %all-reduce.14.cloned.1.call-start = ((), (), s32[]{:S(2)}) async-start(), calls=%async_computation.4 | async-start | bytes 1048576 | tf_op jit(solution)/shard_map/psum | solution.py:17
  463.2 5.8 collective-permute-start.6
  469.0 9.4 %collective-permute-start.7 = (f32[256,256]{0,1:T(8,128)S(1)}, f32[256,256]{0,1:T(8,128)S(1)}, u32[]{:S(2)}, u32[]{:S(2)}) collective-permute-start(f32[256,256]{0,1:T(8,128)S(1)} %add.131), channel_id=1, source_target_pairs={{0,16},{8,24},{16,0},{24,8},{32,48},{40,56},{48,32},{56,40},{64,80... | collective-permute-start | bytes 786440 | tf_op jit(solution)/shard_map/ppermute | solution.py:12
  478.5 10.0 %collective-permute-start.8 = (f32[256,256]{0,1:T(8,128)S(1)}, f32[256,256]{0,1:T(8,128)S(1)}, u32[]{:S(2)}, u32[]{:S(2)}) collective-permute-start(f32[256,256]{0,1:T(8,128)S(1)} %add.132), channel_id=1, source_target_pairs={{0,32},{8,40},{16,48},{24,56},{32,0},{40,8},{48,16},{56,24},{64,96... | collective-permute-start | bytes 786440 | tf_op jit(solution)/shard_map/ppermute | solution.py:12
  488.5 7.6 collective-permute-start.9
  496.1 16.2 %collective-permute-start.10 = (f32[256,256]{0,1:T(8,128)S(1)}, f32[256,256]{0,1:T(8,128)S(1)}, u32[]{:S(2)}, u32[]{:S(2)}) collective-permute-start(f32[256,256]{0,1:T(8,128)S(1)} %add.134), channel_id=1, source_target_pairs={{0,128},{8,136},{16,144},{24,152},{32,160},{40,168},{48,176},{56,1... | collective-permute-start | bytes 786440 | tf_op jit(solution)/shard_map/ppermute | solution.py:12
  512.3 18.8 %collective-permute-start.11 = (f32[256,256]{0,1:T(8,128)S(1)}, f32[256,256]{0,1:T(8,128)S(1)}, u32[]{:S(2)}, u32[]{:S(2)}) collective-permute-start(f32[256,256]{0,1:T(8,128)S(1)} %add.135), channel_id=1, source_target_pairs={{0,256},{8,264},{16,272},{24,280},{32,288},{40,296},{48,304},{56,3... | collective-permute-start | bytes 786440 | tf_op jit(solution)/shard_map/ppermute | solution.py:12
  594.3 270.0 %all-reduce.16.cloned.1.call-start = ((), (), s32[]{:S(2)}) async-start(), calls=%async_computation.5 | async-start | bytes 1048576 | tf_op jit(solution)/shard_map/psum | solution.py:58
  864.3 1.3 copy-start.5
  865.8 1.3 copy-start.4
  (4 other events, 3.5 us)
Sparse Core Ops, SparseCore 0:
  190.2 70.5 all-reduce.9
  265.3 194.6 all-reduce.11
  594.4 71.2 all-reduce.13
  669.6 194.7 all-reduce.15
where the time goes:
time: 884 us; the launch traced here: 877 us
  waiting for transfers between devices  641 us (73%)
  other arithmetic  119 us (13%)
  starting transfers between devices  64 us (7%)
  matrix products  19.2 us (2%)
  between operations  17.2 us (2%)
  local copies, waits for them, and re-layouts  15.2 us (2%)
    psum x2, waiting for transfers between devices, on_device(): lax.psum(jnp.dot(basis_cols.T, parent_front, precision=highest), 'row')  387 us
    psum x2, waiting for transfers between devices, from_root(): return lax.psum(jnp.where(mine, shard, jnp.zeros_like(shard)), axis)  142 us
    ppermute x12, waiting for transfers between devices, swapped(): lax.ppermute(shard, axis, [(i, i ^ 1 << apart) for i in range(lax.axis_si...  88.7 us
    another operation x13, other arithmetic, factor_panel(): upper_factor = jnp.linalg.cholesky(gram_matrix).T  68.6 us
    ppermute x12, starting transfers between devices, swapped(): lax.ppermute(shard, axis, [(i, i ^ 1 << apart) for i in range(lax.axis_si...  44.1 us
    another operation x3, other arithmetic, factor_panel(): jax.scipy.linalg.solve_triangular(upper_factor.T, panel_cols.T, lower=True)  39.4 us
  transfers between devices with their start and end apart: 18, of which 18 were waited for; matrix products, arithmetic and copies ran while one was open for 1% of the time, Pallas kernels for 0%

commit v1 on v0

v1 whole, which is shorter than its diff:
```python
import math

import jax
import jax.numpy as jnp
from jax import lax
from jax.experimental import pallas as pl
from jax.experimental.pallas import tpu as pltpu
from jax.sharding import Mesh, PartitionSpec as P

PANELS = 512
BLOCK = 128
SUB = 32
ROW = ("z", "x", "core")
VMEM = pl.BlockSpec(memory_space=pltpu.VMEM)


def dot(a, b, ca=1, cb=0):
    return lax.dot_general(
        a,
        b,
        (((ca,), (cb,)), ((), ())),
        precision=lax.Precision.HIGHEST,
        preferred_element_type=jnp.float32,
    )


def dot_fast(a, b, ca=1, cb=0):
    return lax.dot_general(
        a, b, (((ca,), (cb,)), ((), ())), preferred_element_type=jnp.float32
    )


def split3(a):
    hi = a.astype(jnp.bfloat16)
    rest = a - hi.astype(jnp.float32)
    mid = rest.astype(jnp.bfloat16)
    low = (rest - mid.astype(jnp.float32)).astype(jnp.bfloat16)
    return hi, mid, low


def call(kernel, out_shape, name, flops, *args):
    return pl.pallas_call(
        kernel,
        out_shape=out_shape,
        in_specs=[VMEM] * len(args),
        out_specs=jax.tree.map(lambda _: VMEM, out_shape),
        name=name,
        compiler_params=pltpu.CompilerParams(vmem_limit_bytes=24 << 20),
        cost_estimate=pl.CostEstimate(flops=flops, bytes_accessed=4 << 20, transcendentals=0),
    )(*args)


def f32(*shape):
    return jax.ShapeDtypeStruct(shape, jnp.float32)


def place_kernel(front_ref, arrived_ref, rows_ref, cols_ref, out_ref):
    height, width = front_ref.shape
    count, child_width = arrived_ref.shape
    col_hot = (
        lax.broadcasted_iota(jnp.int32, (width, child_width), 0) == cols_ref[...]
    ).astype(jnp.float32).astype(jnp.bfloat16)
    row_hot = (
        lax.broadcasted_iota(jnp.int32, (height, count), 0) == rows_ref[...]
    ).astype(jnp.float32).astype(jnp.bfloat16)
    total = front_ref[...]
    for term in split3(arrived_ref[...]):
        spread = dot_fast(term, col_hot, 1, 1).astype(jnp.bfloat16)
        total = total + dot_fast(row_hot, spread)
    out_ref[...] = total


def gram_kernel(a_ref, b_ref, out_ref):
    out_ref[...] = dot(a_ref[...], b_ref[...], 0, 0)


def factor_diagonal(block):
    done = []
    rest = block
    for sub in range(BLOCK // SUB):
        groups = [rest[8 * g : 8 * g + 8, :] for g in range(SUB // 8)]
        for j in range(SUB):
            column = SUB * sub + j
            own, at = divmod(j, 8)
            row = groups[own][at : at + 1, :]
            scale = lax.rsqrt(row[:, column : column + 1])
            scaled = row * scale
            for g in range(own, SUB // 8):
                factor = groups[g][:, column : column + 1] * scale
                updated = groups[g] - factor * scaled
                if g == own:
                    index = lax.broadcasted_iota(jnp.int32, updated.shape, 0)
                    kept = jnp.where(index == at, jnp.broadcast_to(scaled, updated.shape), groups[g])
                    updated = jnp.where(index > at, updated, kept)
                groups[g] = updated
        rows = jnp.concatenate(groups, axis=0)
        done.append(rows)
        if sub + 1 < BLOCK // SUB:
            rest = rest[SUB:, :] - dot(rows[:, SUB * (sub + 1) : BLOCK], rows, 0, 0)
    return jnp.concatenate(done, axis=0)


def eye(size):
    shape = (size, size)
    return (
        lax.broadcasted_iota(jnp.int32, shape, 0) == lax.broadcasted_iota(jnp.int32, shape, 1)
    ).astype(jnp.float32)


def factor_kernel(k, gram_ref, *refs):
    above, out_ref = refs[:-1], refs[-1]
    n = gram_ref.shape[0]
    rows = slice(k * BLOCK, (k + 1) * BLOCK)
    low, high = k * BLOCK, n + (k + 1) * BLOCK
    identity = eye(BLOCK)
    pad = [jnp.zeros((BLOCK, low), jnp.float32)] if k else []
    work = jnp.concatenate([gram_ref[rows, low:]] + pad + [identity], axis=1)
    for ref in above:
        work = work - dot(ref[:, rows], ref[:, low:high], 0, 0)
    diagonal = factor_diagonal(jnp.concatenate([work[:, :BLOCK], identity], axis=1))
    out_ref[:, low:high] = dot(diagonal[:, BLOCK:], work)
    out_ref[:, rows] = diagonal[:, :BLOCK]
    if k:
        out_ref[:, :low] = jnp.zeros((BLOCK, low), jnp.float32)
    if high < 2 * n:
        out_ref[:, high:] = jnp.zeros((BLOCK, 2 * n - high), jnp.float32)


def final_kernel(root_rows, front_ref, panel_ref, sums_ref, is_root_ref, *refs):
    blocks, (out_ref, factor_ref) = refs[:-2], refs[-2:]
    n = panel_ref.shape[1]
    inverse = jnp.concatenate([ref[:, n:] for ref in blocks], axis=0)
    basis = dot(panel_ref[...], inverse, 1, 1)
    coupled = dot(inverse, sums_ref[...])
    is_root = is_root_ref[0, 0] == 1
    out_ref[...] = jnp.where(
        is_root, basis * root_rows, front_ref[...] - dot(basis, coupled)
    )
    upper = jnp.concatenate([ref[:, :n] for ref in blocks], axis=0)
    factor_ref[...] = jnp.where(is_root, upper, coupled) * (1.0 / root_rows)


def exchange(blocks, axis):
    return lax.all_to_all(blocks, axis, split_axis=0, concat_axis=0, tiled=True)


def scatter_sum(x):
    for axis in ("core", "x", "z"):
        n = lax.axis_size(axis)
        x = jnp.sum(exchange(x.reshape(n, x.shape[0] // n, x.shape[1]), axis), axis=0)
    return x


def gathered(x, axis):
    n = lax.axis_size(axis)
    return exchange(jnp.broadcast_to(x[None], (n,) + x.shape), axis).reshape(
        n * x.shape[0], x.shape[1]
    )


def gather_rows(x):
    for axis in ("z", "x", "core"):
        x = gathered(x, axis)
    return x


def share_from_root(x):
    n = lax.axis_size("col")
    return exchange(x.reshape(n, x.shape[0] // n, x.shape[1]), "col")[0]


def on_device(front_in, child_block, child_rows, live_counts, column_map):
    rows_dev, cols_dev = front_in.shape
    owners = lax.axis_size(ROW)
    count, child_width = child_block.shape
    capacity = count // owners
    slots = jnp.arange(capacity, dtype=jnp.int32)
    live = slots[None, :] < live_counts[0][:, None]
    targets = jnp.where(live, child_rows.reshape(owners, capacity) % rows_dev, -1)
    arrived = exchange(child_block.reshape(owners, capacity, child_width), ROW)
    arrived_rows = exchange(targets.reshape(owners, 1, capacity), ROW)
    arrived = arrived.reshape(count, child_width)
    arrived_rows = arrived_rows.reshape(1, count)
    local_cols = (column_map % cols_dev).reshape(1, child_width)
    front = call(
        place_kernel, f32(rows_dev, cols_dev), "place", 2 << 30,
        front_in, arrived, arrived_rows, local_cols,
    )

    gram_part = call(gram_kernel, f32(PANELS, PANELS), "gram", 2 << 30, front, front)
    gram_share = scatter_sum(gram_part)
    gram_share = exchange(
        jnp.broadcast_to(gram_share[None], (lax.axis_size("col"),) + gram_share.shape), "col"
    )[0]
    gram = gather_rows(gram_share)

    panel = gathered(share_from_root(front), "col")
    sums = call(gram_kernel, f32(PANELS, cols_dev), "products", 2 << 30, panel, front)
    sums = gather_rows(scatter_sum(sums))

    blocks = []
    for k in range(PANELS // BLOCK):
        blocks.append(
            call(
                lambda *refs, k=k: factor_kernel(k, *refs),
                f32(BLOCK, 2 * PANELS), f"factor{k}", 10 << 30, gram, *blocks,
            )
        )

    is_root = (lax.axis_index("col") == 0).astype(jnp.int32).reshape(1, 1)
    return call(
        lambda *refs: final_kernel(math.sqrt(rows_dev * owners), *refs),
        (f32(rows_dev, cols_dev), f32(PANELS, cols_dev)), "final", 6 << 30,
        front, panel, sums, is_root, *blocks,
    )


def solution(mesh):
    row, col = mesh.shape["row"], mesh.shape["col"]
    fine = Mesh(mesh.devices.reshape(8, 4, row // 32, col), ROW + ("col",))
    return jax.shard_map(
        on_device,
        mesh=fine,
        in_specs=(P(ROW, "col"), P(ROW, "col"), P(ROW), P(ROW, None), P("col")),
        out_specs=(P(ROW, "col"), P(None, "col")),
        check_vma=False,
    )
```

time: 884 us -> 283 us (0.32)
  waiting for transfers between devices: 641 us -> 54.6 us
  other arithmetic: 119 us -> 3.23 us
  blocking collectives: 0 us -> 110 us
  Pallas kernels: 0 us -> 65.9 us
  starting transfers between devices: 64 us -> 36.8 us
  matrix products: 19.2 us -> 0 us
  between operations: 17.2 us -> 0.88 us
    psum x4 -> x0, waiting for transfers between devices: 529 us -> none  [the longest x2 387 us: on_device(): lax.psum(jnp.dot(basis_cols.T, parent_front, precision=highest), 'row')]
    all_to_all x0 -> x8, blocking collectives: none -> 110 us  [exchange(): return lax.all_to_all(blocks, axis, split_axis=0, concat_axis=0, tiled=True)]
    another operation x16 -> x0, other arithmetic: 108 us -> none  [the longest x13 68.6 us: factor_panel(): upper_factor = jnp.linalg.cholesky(gram_matrix).T]
    ppermute x12 -> x0, waiting for transfers between devices: 88.7 us -> none  [swapped(): lax.ppermute(shard, axis, [(i, i ^ 1 << apart) for i in range(lax.axis_si...]
    pallas_call x0 -> x8, Pallas kernels: none -> 65.9 us  [call(): pl.pallas_call(kernel, out_shape=out_shape, in_specs=[VMEM] * len(args),...]
    ppermute x12 -> x0, starting transfers between devices: 44.1 us -> none  [swapped(): lax.ppermute(shard, axis, [(i, i ^ 1 << apart) for i in range(lax.axis_si...]
    all_to_all x2 -> x9, waiting for transfers between devices: 23.9 us -> 54.6 us  [exchange(): return lax.all_to_all(blocks, axis, split_axis=0, concat_axis=0, tiled=True)]
    all_to_all x2 -> x9, starting transfers between devices: 19.7 us -> 36.8 us  [exchange(): return lax.all_to_all(blocks, axis, split_axis=0, concat_axis=0, tiled=True)]
  transfers between devices with their start and end apart: 18 -> 9, of which waited for: 18 -> 5; matrix products, arithmetic and copies ran while one was open for 1% -> 1% of each run, Pallas kernels for 0% -> 19%
where the time goes in v1:
time: 283 us; the launch traced here: 282 us
  blocking collectives  110 us (39%)
  Pallas kernels  65.9 us (23%)
  waiting for transfers between devices  54.6 us (19%)
  starting transfers between devices  36.8 us (13%)
  local copies, waits for them, and re-layouts  10.3 us (4%)
  other arithmetic  3.23 us (1%)
    all_to_all x8, blocking collectives, exchange(): return lax.all_to_all(blocks, axis, split_axis=0, concat_axis=0, tiled=True)  110 us
    pallas_call x8, Pallas kernels, call(): pl.pallas_call(kernel, out_shape=out_shape, in_specs=[VMEM] * len(args),...  65.9 us
    all_to_all x9, waiting for transfers between devices, exchange(): return lax.all_to_all(blocks, axis, split_axis=0, concat_axis=0, tiled=True)  54.6 us
    all_to_all x9, starting transfers between devices, exchange(): return lax.all_to_all(blocks, axis, split_axis=0, concat_axis=0, tiled=True)  36.8 us
  transfers between devices with their start and end apart: 9, of which 5 were waited for; matrix products, arithmetic and copies ran while one was open for 1% of the time, Pallas kernels for 19%

profile of v1, /device:TPU:1, one launch (start us, length us, event | category | flops | bytes accessed | tf_op | source)
XLA Modules:
  0.0 281.8 jit_solution(12815170427156232803)
XLA Ops:
  2.2 24.0 %all_to_all.85 = s32[64,1,8]{2,1,0:T(1,128)S(1)} all-to-all(s32[64,1,8]{2,1,0:T(1,128)S(1)} %bitcast.42), channel_id=1, replica_groups=mesh['z'=8,'x'=4,'core'=2,'col'=8] {'z','x','core'}, dimensions={0} | all-to-all | bytes 4096 | tf_op jit(solution)/shard_map/all_to_all | solution.py:144
  26.2 4.9 %all-to-all-start = ((f32[64,8,256]{2,1,0:T(8,128)}), f32[64,8,256]{2,1,0:T(8,128)S(1)}, u32[]{:S(2)}, u32[]{:S(2)}) async-start(f32[64,8,256]{2,1,0:T(8,128)} %bitcast.40), calls=%async_computation | async-start | bytes 1048576 | tf_op jit(solution)/shard_map/all_to_all | solution.py:144
  32.5 16.5 %all-to-all-done = f32[64,8,256]{2,1,0:T(8,128)S(1)} async-done(((f32[64,8,256]{2,1,0:T(8,128)}), f32[64,8,256]{2,1,0:T(8,128)S(1)}, u32[]{:S(2)}, u32[]{:S(2)}) %all-to-all-start) | async-done | bytes 524320 | tf_op jit(solution)/shard_map/all_to_all | solution.py:144
  55.0 4.6 %all_to_all.86 = f32[2,256,512]{2,1,0:T(8,128)S(1)} all-to-all(f32[2,256,512]{2,1,0:T(8,128)S(1)} %bitcast.32), channel_id=1, replica_groups=mesh['z'=8,'x'=4,'core'=2,'col'=8] {'core'}, dimensions={0} | all-to-all | bytes 2097152 | tf_op jit(solution)/shard_map/all_to_all | solution.py:144
  59.7 12.4 %all_to_all.87 = f32[4,64,512]{2,1,0:T(8,128)S(1)} all-to-all(f32[4,64,512]{2,1,0:T(8,128)S(1)} %bitcast.37), channel_id=1, replica_groups=mesh['z'=8,'x'=4,'core'=2,'col'=8] {'x'}, dimensions={0} | all-to-all | bytes 1048576 | tf_op jit(solution)/shard_map/all_to_all | solution.py:144
  72.1 11.0 %all_to_all.88 = f32[8,8,512]{2,1,0:T(8,128)S(1)} all-to-all(f32[8,8,512]{2,1,0:T(8,128)S(1)} %bitcast.41), channel_id=1, replica_groups=mesh['z'=8,'x'=4,'core'=2,'col'=8] {'z'}, dimensions={0} | all-to-all | bytes 262144 | tf_op jit(solution)/shard_map/all_to_all | solution.py:144
  83.1 14.5 %all_to_all.89 = f32[8,8,512]{2,1,0:T(8,128)S(1)} all-to-all(f32[8,8,512]{2,1,0:T(8,128)S(1)} %broadcast_in_dim.67), channel_id=1, replica_groups=mesh['z'=8,'x'=4,'core'=2,'col'=8] {'col'}, dimensions={0} | all-to-all | bytes 262144 | tf_op jit(solution)/shard_map/all_to_all | solution.py:144
  97.6 3.6 %all-to-all-start.2 = ((f32[8,64,512]{2,1,0:T(8,128)}), f32[8,64,512]{2,1,0:T(8,128)S(1)}, u32[]{:S(2)}, u32[]{:S(2)}) async-start(f32[8,64,512]{2,1,0:T(8,128)} %bitcast.5), calls=%async_computation.2 | async-start | bytes 2097152 | tf_op jit(solution)/shard_map/all_to_all | solution.py:144
  101.2 25.7 %all-to-all-done.2 = f32[8,64,512]{2,1,0:T(8,128)S(1)} async-done(((f32[8,64,512]{2,1,0:T(8,128)}), f32[8,64,512]{2,1,0:T(8,128)S(1)}, u32[]{:S(2)}, u32[]{:S(2)}) %all-to-all-start.2) | async-done | bytes 1048608 | tf_op jit(solution)/shard_map/all_to_all | solution.py:144
  130.9 7.8 %all-to-all-done.14 = f32[8,8,512]{2,1,0:T(8,128)S(1)} async-done(((f32[8,8,512]{2,1,0:T(8,128)}), f32[8,8,512]{2,1,0:T(8,128)S(1)}, u32[]{:S(2)}, u32[]{:S(2)}) %all-to-all-start.14) | async-done | bytes 131104 | tf_op jit(solution)/shard_map/all_to_all | solution.py:144
  138.9 25.3 %all_to_all.90 = f32[8,64,512]{2,1,0:T(8,128)S(1)} all-to-all(f32[8,64,512]{2,1,0:T(8,128)S(1)} %broadcast_in_dim.61), channel_id=1, replica_groups=mesh['z'=8,'x'=4,'core'=2,'col'=8] {'col'}, dimensions={0} | all-to-all | bytes 2097152 | tf_op jit(solution)/shard_map/all_to_all | solution.py:144
  165.1 3.5 %all-to-all-start.15 = ((f32[4,64,512]{2,1,0:T(8,128)}), f32[4,64,512]{2,1,0:T(8,128)S(1)}, u32[]{:S(2)}, u32[]{:S(2)}) async-start(f32[4,64,512]{2,1,0:T(8,128)} %broadcast_in_dim.71), calls=%async_computation.15 | async-start | bytes 1048576 | tf_op jit(solution)/shard_map/all_to_all | solution.py:144
  171.6 3.8 %all-to-all-done.15 = f32[4,64,512]{2,1,0:T(8,128)S(1)} async-done(((f32[4,64,512]{2,1,0:T(8,128)}), f32[4,64,512]{2,1,0:T(8,128)S(1)}, u32[]{:S(2)}, u32[]{:S(2)}) %all-to-all-start.15) | async-done | bytes 524320 | tf_op jit(solution)/shard_map/all_to_all | solution.py:144
  176.2 12.2 %all_to_all.91 = f32[2,256,512]{2,1,0:T(8,128)S(1)} all-to-all(f32[2,256,512]{2,1,0:T(8,128)S(1)} %bitcast.31), channel_id=1, replica_groups=mesh['z'=8,'x'=4,'core'=2,'col'=8] {'core'}, dimensions={0} | all-to-all | bytes 2097152 | tf_op jit(solution)/shard_map/all_to_all | solution.py:144
  189.6 3.9 %all-to-all-start.16 = ((f32[2,256,512]{2,1,0:T(8,128)}), f32[2,256,512]{2,1,0:T(8,128)S(1)}, u32[]{:S(2)}, u32[]{:S(2)}) async-start(f32[2,256,512]{2,1,0:T(8,128)} %broadcast_in_dim.73), calls=%async_computation.16 | async-start | bytes 2097152 | tf_op jit(solution)/shard_map/all_to_all | solution.py:144
  198.8 11.8 %factor0.1.refs_1_.refs_4_ = f32[128,1024]{1,0:T(8,128)S(1)} custom-call(f32[512,512]{1,0:T(8,128)S(1)} %bitcast.26), custom_call_target="tpu_custom_call" | custom-call | flops 10737418240 | bytes 4194304 | tf_op jit(solution)/shard_map/factor0/pallas_call | solution.py:42
  211.3 3.6 %all-to-all-start.6 = ((f32[8,8,512]{2,1,0:T(8,128)}), f32[8,8,512]{2,1,0:T(8,128)S(1)}, u32[]{:S(2)}, u32[]{:S(2)}) async-start(f32[8,8,512]{2,1,0:T(8,128)} %bitcast.10), calls=%async_computation.6 | async-start | bytes 262144 | tf_op jit(solution)/shard_map/all_to_all | solution.py:144
  214.8 12.2 %factor1.1.refs_2_.refs_5_ = f32[128,1024]{1,0:T(8,128)S(1)} custom-call(f32[512,512]{1,0:T(8,128)S(1)} %bitcast.27, f32[128,1024]{1,0:T(8,128)S(1)} %factor0.1.refs_1_.refs_4_), custom_call_target="tpu_custom_call" | custom-call | flops 10737418240 | bytes 4194304 | tf_op jit(solution)/shard_map/factor1/pallas_call | solution.py:42
  227.8 6.4 %all-to-all-start.7 = ((f32[8,8,512]{2,1,0:T(8,128)}), f32[8,8,512]{2,1,0:T(8,128)S(1)}, u32[]{:S(2)}, u32[]{:S(2)}) async-start(f32[8,8,512]{2,1,0:T(8,128)} %broadcast_in_dim.62), calls=%async_computation.7 | async-start | bytes 262144 | tf_op jit(solution)/shard_map/all_to_all | solution.py:144
  234.1 12.5 %factor2.1.refs_3_.refs_6_ = f32[128,1024]{1,0:T(8,128)S(1)} custom-call(f32[512,512]{1,0:T(8,128)S(1)} %bitcast.28, f32[128,1024]{1,0:T(8,128)S(1)} %factor0.1.refs_1_.refs_4_, f32[128,1024]{1,0:T(8,128)S(1)} %factor1.1.refs_2_.refs_5_), custom_call_target="tpu_custom_call" | custom-call | flops 10737418240 | bytes 4194304 | tf_op jit(solution)/shard_map/factor2/pallas_call | solution.py:42
  248.3 4.2 %all-to-all-start.8 = ((f32[4,64,512]{2,1,0:T(8,128)}), f32[4,64,512]{2,1,0:T(8,128)}, u32[]{:S(2)}, u32[]{:S(2)}) async-start(f32[4,64,512]{2,1,0:T(8,128)} %broadcast_in_dim.64), calls=%async_computation.8 | async-start | bytes 1048576 | tf_op jit(solution)/shard_map/all_to_all | solution.py:144
  253.5 12.7 %factor3.1.refs_7_ = f32[128,1024]{1,0:T(8,128)S(1)} custom-call(f32[512,512]{1,0:T(8,128)S(1)} %bitcast.29, f32[128,1024]{1,0:T(8,128)S(1)} %factor0.1.refs_1_.refs_4_, f32[128,1024]{1,0:T(8,128)S(1)} %factor1.1.refs_2_.refs_5_, f32[128,1024]{1,0:T(8,128)S(1)} %copy-done.2), custom_call_target="tpu_custom_call" | custom-call | flops 10737418240 | bytes 4194304 | tf_op jit(solution)/shard_map/factor3/pallas_call | solution.py:42
  268.3 5.9 %all_to_all.92 = f32[2,256,512]{2,1,0:T(8,128)S(1)} all-to-all(f32[2,256,512]{2,1,0:T(8,128)S(1)} %broadcast_in_dim.66), channel_id=1, replica_groups=mesh['z'=8,'x'=4,'core'=2,'col'=8] {'core'}, dimensions={0} | all-to-all | bytes 2097152 | tf_op jit(solution)/shard_map/all_to_all | solution.py:144
  274.2 7.6 %final.1 = (f32[512,512]{1,0:T(8,128)}, f32[512,512]{1,0:T(8,128)}) custom-call(f32[512,512]{1,0:T(8,128)} %place.1.b_ref.a_ref.refs_0_, f32[512,512]{1,0:T(8,128)S(1)} %bitcast.25, f32[512,512]{1,0:T(8,128)S(1)} %bitcast.30, s32[1,1]{1,0:T(1,128)} %bitcast.14.refs_3_, f32[128,1024]{1,0:T(8,128)S(1)} %factor0.1.refs_1_.refs_4_, ...), custom_call_target="tpu_custom_call" | custom-call | flops 6442450944 | bytes 4194304 | tf_op jit(solution)/shard_map/final/pallas_call | solution.py:42
  (50 shorter events, 30.4 us)
Async XLA Ops:
  0.6 48.3 %copy-start = (f32[512,512]{1,0:T(8,128)S(1)}, f32[512,512]{1,0:T(8,128)}, u32[]{:S(2)}) copy-start(f32[512,512]{1,0:T(8,128)} %front_ref.1) | copy-start | bytes 3145732
  26.2 4.9 %copy-start.8 = (s32[256]{0:T(256)S(1)}, s32[256]{0:T(256)}, u32[]{:S(2)}) copy-start(s32[256]{0:T(256)} %param.9) | copy-start | bytes 3076
  26.2 22.7 %all-to-all-start = ((f32[64,8,256]{2,1,0:T(8,128)}), f32[64,8,256]{2,1,0:T(8,128)S(1)}, u32[]{:S(2)}, u32[]{:S(2)}) async-start(f32[64,8,256]{2,1,0:T(8,128)} %bitcast.40), calls=%async_computation | async-start | bytes 1048576 | tf_op jit(solution)/shard_map/all_to_all | solution.py:144
  97.6 29.2 %all-to-all-start.2 = ((f32[8,64,512]{2,1,0:T(8,128)}), f32[8,64,512]{2,1,0:T(8,128)S(1)}, u32[]{:S(2)}, u32[]{:S(2)}) async-start(f32[8,64,512]{2,1,0:T(8,128)} %bitcast.5), calls=%async_computation.2 | async-start | bytes 2097152 | tf_op jit(solution)/shard_map/all_to_all | solution.py:144
  127.5 11.2 %all-to-all-start.14 = ((f32[8,8,512]{2,1,0:T(8,128)}), f32[8,8,512]{2,1,0:T(8,128)S(1)}, u32[]{:S(2)}, u32[]{:S(2)}) async-start(f32[8,8,512]{2,1,0:T(8,128)} %broadcast_in_dim.69), calls=%async_computation.14 | async-start | bytes 262144 | tf_op jit(solution)/shard_map/all_to_all | solution.py:144
  165.1 10.4 %all-to-all-start.15 = ((f32[4,64,512]{2,1,0:T(8,128)}), f32[4,64,512]{2,1,0:T(8,128)S(1)}, u32[]{:S(2)}, u32[]{:S(2)}) async-start(f32[4,64,512]{2,1,0:T(8,128)} %broadcast_in_dim.71), calls=%async_computation.15 | async-start | bytes 1048576 | tf_op jit(solution)/shard_map/all_to_all | solution.py:144
  175.4 0.8 copy-start.6
  176.2 12.2 %copy-start.7 = (f32[4,64,512]{2,1,0:T(8,128)S(1)}, f32[4,64,512]{2,1,0:T(8,128)}, u32[]{:S(2)}) copy-start(f32[4,64,512]{2,1,0:T(8,128)} %copy-done.6) | copy-start | bytes 1572868
  189.6 5.7 %all-to-all-start.16 = ((f32[2,256,512]{2,1,0:T(8,128)}), f32[2,256,512]{2,1,0:T(8,128)S(1)}, u32[]{:S(2)}, u32[]{:S(2)}) async-start(f32[2,256,512]{2,1,0:T(8,128)} %broadcast_in_dim.73), calls=%async_computation.16 | async-start | bytes 2097152 | tf_op jit(solution)/shard_map/all_to_all | solution.py:144
  195.3 15.3 %all-to-all-start.5 = ((f32[4,64,512]{2,1,0:T(8,128)}), f32[4,64,512]{2,1,0:T(8,128)S(1)}, u32[]{:S(2)}, u32[]{:S(2)}) async-start(f32[4,64,512]{2,1,0:T(8,128)} %bitcast.36), calls=%async_computation.5 | async-start | bytes 1048576 | tf_op jit(solution)/shard_map/all_to_all | solution.py:144
  211.3 15.8 %all-to-all-start.6 = ((f32[8,8,512]{2,1,0:T(8,128)}), f32[8,8,512]{2,1,0:T(8,128)S(1)}, u32[]{:S(2)}, u32[]{:S(2)}) async-start(f32[8,8,512]{2,1,0:T(8,128)} %bitcast.10), calls=%async_computation.6 | async-start | bytes 262144 | tf_op jit(solution)/shard_map/all_to_all | solution.py:144
  227.8 19.7 %all-to-all-start.7 = ((f32[8,8,512]{2,1,0:T(8,128)}), f32[8,8,512]{2,1,0:T(8,128)S(1)}, u32[]{:S(2)}, u32[]{:S(2)}) async-start(f32[8,8,512]{2,1,0:T(8,128)} %broadcast_in_dim.62), calls=%async_computation.7 | async-start | bytes 262144 | tf_op jit(solution)/shard_map/all_to_all | solution.py:144
  246.6 0.8 copy-start.1
  248.3 18.8 %all-to-all-start.8 = ((f32[4,64,512]{2,1,0:T(8,128)}), f32[4,64,512]{2,1,0:T(8,128)}, u32[]{:S(2)}, u32[]{:S(2)}) async-start(f32[4,64,512]{2,1,0:T(8,128)} %broadcast_in_dim.64), calls=%async_computation.8 | async-start | bytes 1048576 | tf_op jit(solution)/shard_map/all_to_all | solution.py:144
  252.5 1.0 copy-start.2
  266.3 0.8 copy-start.4
  268.3 5.9 %copy-start.3 = (f32[128,1024]{1,0:T(8,128)S(1)}, f32[128,1024]{1,0:T(8,128)}, u32[]{:S(2)}) copy-start(f32[128,1024]{1,0:T(8,128)} %copy-done.1) | copy-start | bytes 1572868
  268.3 5.9 %copy-start.5 = (f32[128,1024]{1,0:T(8,128)S(1)}, f32[128,1024]{1,0:T(8,128)}, u32[]{:S(2)}) copy-start(f32[128,1024]{1,0:T(8,128)} %copy-done.4) | copy-start | bytes 1572868

commit v2 on v1

--- a/solution.py
+++ b/solution.py
@@ -54,23 +54,43 @@
     return jax.ShapeDtypeStruct(shape, jnp.float32)
 
 
-def place_kernel(front_ref, arrived_ref, rows_ref, cols_ref, out_ref):
+def place_kernel(front_ref, arrived_ref, cols_ref, out_ref):
     height, width = front_ref.shape
-    count, child_width = arrived_ref.shape
+    count = arrived_ref.shape[0]
+    child_width = cols_ref.shape[1]
     col_hot = (
         lax.broadcasted_iota(jnp.int32, (width, child_width), 0) == cols_ref[...]
     ).astype(jnp.float32).astype(jnp.bfloat16)
+    targets = arrived_ref[:, child_width : child_width + 1].astype(jnp.int32)
     row_hot = (
-        lax.broadcasted_iota(jnp.int32, (height, count), 0) == rows_ref[...]
+        lax.broadcasted_iota(jnp.int32, (count, height), 1) == targets
     ).astype(jnp.float32).astype(jnp.bfloat16)
     total = front_ref[...]
-    for term in split3(arrived_ref[...]):
+    for term in split3(arrived_ref[:, :child_width]):
         spread = dot_fast(term, col_hot, 1, 1).astype(jnp.bfloat16)
-        total = total + dot_fast(row_hot, spread)
+        total = total + dot_fast(row_hot, spread, 0, 0)
     out_ref[...] = total
 
 
-def gram_kernel(a_ref, b_ref, out_ref):
+def gram_place(i, j):
+    if i < 2:
+        return (2 * j + i) * BLOCK
+    return (2 * PANELS // BLOCK + 2 * (j - 2) + i - 2) * BLOCK
+
+
+def gram_kernel(panel_ref, out_ref):
+    half = PANELS // 2
+    for first in range(2):
+        cols = slice(half * first, PANELS)
+        product = dot(panel_ref[:, half * first : half * (first + 1)], panel_ref[:, cols], 0, 0)
+        for i in range(2):
+            for j in range(2 * first, PANELS // BLOCK):
+                at = gram_place(2 * first + i, j)
+                left = (j - 2 * first) * BLOCK
+                out_ref[at : at + BLOCK, :] = product[i * BLOCK : (i + 1) * BLOCK, left : left + BLOCK]
+
+
+def product_kernel(a_ref, b_ref, out_ref):
     out_ref[...] = dot(a_ref[...], b_ref[...], 0, 0)
 
 
@@ -109,12 +129,14 @@
 
 def factor_kernel(k, gram_ref, *refs):
     above, out_ref = refs[:-1], refs[-1]
-    n = gram_ref.shape[0]
+    n = PANELS
     rows = slice(k * BLOCK, (k + 1) * BLOCK)
     low, high = k * BLOCK, n + (k + 1) * BLOCK
     identity = eye(BLOCK)
     pad = [jnp.zeros((BLOCK, low), jnp.float32)] if k else []
-    work = jnp.concatenate([gram_ref[rows, low:]] + pad + [identity], axis=1)
+    starts = [gram_place(k, j) for j in range(k, n // BLOCK)]
+    gram = [gram_ref[at : at + BLOCK, :] for at in starts]
+    work = jnp.concatenate(gram + pad + [identity], axis=1)
     for ref in above:
         work = work - dot(ref[:, rows], ref[:, low:high], 0, 0)
     diagonal = factor_diagonal(jnp.concatenate([work[:, :BLOCK], identity], axis=1))
@@ -145,28 +167,33 @@
 
 
 def scatter_sum(x):
-    for axis in ("core", "x", "z"):
-        n = lax.axis_size(axis)
+    for axis, n in (("core", 2), (("z", "x"), 32)):
         x = jnp.sum(exchange(x.reshape(n, x.shape[0] // n, x.shape[1]), axis), axis=0)
     return x
 
 
-def gathered(x, axis):
-    n = lax.axis_size(axis)
-    return exchange(jnp.broadcast_to(x[None], (n,) + x.shape), axis).reshape(
-        n * x.shape[0], x.shape[1]
-    )
+def repeated(x, n):
+    return jnp.broadcast_to(x[None], (n,) + x.shape)
 
 
 def gather_rows(x):
-    for axis in ("z", "x", "core"):
-        x = gathered(x, axis)
-    return x
-
-
-def share_from_root(x):
+    chips = lax.axis_size(("z", "x"))
+    own = exchange(repeated(x, chips), ("z", "x")).reshape(chips * x.shape[0], x.shape[1])
+    other = lax.ppermute(own, "core", [(0, 1), (1, 0)])
+    return jnp.where(
+        lax.axis_index("core") == 0,
+        jnp.concatenate([own, other], axis=0),
+        jnp.concatenate([other, own], axis=0),
+    )
+
+
+def from_root(x):
     n = lax.axis_size("col")
-    return exchange(x.reshape(n, x.shape[0] // n, x.shape[1]), "col")[0]
+    shares = x.reshape(n, x.shape[0] // n, x.shape[1])
+    mine = jnp.where(lax.axis_index("col") == 0, shares[0], 0.0)
+    for k in range(1, n):
+        mine = mine + lax.ppermute(shares[k], "col", [(0, k)])
+    return lax.all_gather(mine, "col", tiled=True)
 
 
 def on_device(front_in, child_block, child_rows, live_counts, column_map):
@@ -177,25 +204,26 @@
     slots = jnp.arange(capacity, dtype=jnp.int32)
     live = slots[None, :] < live_counts[0][:, None]
     targets = jnp.where(live, child_rows.reshape(owners, capacity) % rows_dev, -1)
-    arrived = exchange(child_block.reshape(owners, capacity, child_width), ROW)
-    arrived_rows = exchange(targets.reshape(owners, 1, capacity), ROW)
-    arrived = arrived.reshape(count, child_width)
-    arrived_rows = arrived_rows.reshape(1, count)
+    sent = jnp.concatenate(
+        [
+            child_block.reshape(owners, capacity, child_width),
+            jnp.broadcast_to(targets.astype(jnp.float32)[:, :, None], (owners, capacity, 128)),
+        ],
+        axis=2,
+    )
+    arrived = exchange(sent, ROW).reshape(count, child_width + 128)
     local_cols = (column_map % cols_dev).reshape(1, child_width)
     front = call(
-        place_kernel, f32(rows_dev, cols_dev), "place", 2 << 30,
-        front_in, arrived, arrived_rows, local_cols,
-    )
-
-    gram_part = call(gram_kernel, f32(PANELS, PANELS), "gram", 2 << 30, front, front)
+        place_kernel, f32(rows_dev, cols_dev), "place", 2 << 30, front_in, arrived, local_cols
+    )
+
+    gram_part = call(gram_kernel, f32(3 * PANELS, BLOCK), "gram", 2 << 30, front)
     gram_share = scatter_sum(gram_part)
-    gram_share = exchange(
-        jnp.broadcast_to(gram_share[None], (lax.axis_size("col"),) + gram_share.shape), "col"
-    )[0]
+    gram_share = exchange(repeated(gram_share, lax.axis_size("col")), "col")[0]
     gram = gather_rows(gram_share)
 
-    panel = gathered(share_from_root(front), "col")
-    sums = call(gram_kernel, f32(PANELS, cols_dev), "products", 2 << 30, panel, front)
+    panel = from_root(front)
+    sums = call(product_kernel, f32(PANELS, cols_dev), "products", 2 << 30, panel, front)
     sums = gather_rows(scatter_sum(sums))
 
     blocks = []

time: 283 us -> 216 us (0.76)
  blocking collectives: 110 us -> 36.6 us
  starting transfers between devices: 36.8 us -> 52.4 us
  waiting for transfers between devices: 54.6 us -> 39.4 us
  between operations: 0.88 us -> 14.4 us
  local copies, waits for them, and re-layouts: 10.3 us -> 3.81 us
  Pallas kernels: 65.9 us -> 60.7 us
  other arithmetic: 3.23 us -> 7.22 us
    all_to_all x8 -> x4, blocking collectives: 110 us -> 36.6 us  [exchange(): return lax.all_to_all(blocks, axis, split_axis=0, concat_axis=0, tiled=True)]
    ppermute x0 -> x9, starting transfers between devices: none -> 22.8 us  [the longest x7 12.7 us: from_root(): mine = mine + lax.ppermute(shares[k], 'col', [(0, k)])]
    all_to_all x9 -> x4, waiting for transfers between devices: 54.6 us -> 39.3 us  [exchange(): return lax.all_to_all(blocks, axis, split_axis=0, concat_axis=0, tiled=True)]
    all_to_all x9 -> x4, starting transfers between devices: 36.8 us -> 29.6 us  [exchange(): return lax.all_to_all(blocks, axis, split_axis=0, concat_axis=0, tiled=True)]
    pallas_call x8, Pallas kernels: 65.9 us -> 60.7 us  [call(): pl.pallas_call(kernel, out_shape=out_shape, in_specs=[VMEM] * len(args),...]
    broadcast_in_dim x10 -> x5, local copies, waits for them, and re-layouts: 5.46 us -> 1.02 us  [the longest x4 0.9 us: repeated(): return jnp.broadcast_to(x[None], (n,) + x.shape)]
  transfers between devices with their start and end apart: 9 -> 14, of which waited for: 5 -> 3; matrix products, arithmetic and copies ran while one was open for 1% -> 2% of each run, Pallas kernels for 19% -> 25%
where the time goes in v2:
time: 216 us; the launch traced here: 215 us
  Pallas kernels  60.7 us (28%)
  starting transfers between devices  52.4 us (24%)
  waiting for transfers between devices  39.4 us (18%)
  blocking collectives  36.6 us (17%)
  between operations  14.4 us (7%)
  other arithmetic  7.22 us (3%)
  local copies, waits for them, and re-layouts  3.81 us (2%)
    pallas_call x8, Pallas kernels, call(): pl.pallas_call(kernel, out_shape=out_shape, in_specs=[VMEM] * len(args),...  60.7 us
    all_to_all x4, waiting for transfers between devices, exchange(): return lax.all_to_all(blocks, axis, split_axis=0, concat_axis=0, tiled=True)  39.3 us
    all_to_all x4, blocking collectives, exchange(): return lax.all_to_all(blocks, axis, split_axis=0, concat_axis=0, tiled=True)  36.6 us
    all_to_all x4, starting transfers between devices, exchange(): return lax.all_to_all(blocks, axis, split_axis=0, concat_axis=0, tiled=True)  29.6 us
    ppermute x7, starting transfers between devices, from_root(): mine = mine + lax.ppermute(shares[k], 'col', [(0, k)])  12.7 us
    ppermute x2, starting transfers between devices, gather_rows(): other = lax.ppermute(own, 'core', [(0, 1), (1, 0)])  10.1 us
  transfers between devices with their start and end apart: 14, of which 3 were waited for; matrix products, arithmetic and copies ran while one was open for 2% of the time, Pallas kernels for 25%

profile of v2, /device:TPU:1, one launch (start us, length us, event | category | flops | bytes accessed | tf_op | source)
XLA Modules:
  0.0 214.5 jit_solution(10529518940865165764)
XLA Ops:
  8.8 2.0 pad_maximum_fusion
  10.8 15.0 %all-to-all-start = ((f32[64,8,384]{2,1,0:T(8,128)}), f32[64,8,384]{2,1,0:T(8,128)S(1)}, u32[]{:S(2)}, u32[]{:S(2)}) async-start(f32[64,8,384]{2,1,0:T(8,128)} %pad_maximum_fusion), calls=%async_computation | async-start | bytes 1572864 | tf_op jit(solution)/shard_map/all_to_all | solution.py:166
  25.8 22.7 %all-to-all-done = f32[64,8,384]{2,1,0:T(8,128)S(1)} async-done(((f32[64,8,384]{2,1,0:T(8,128)}), f32[64,8,384]{2,1,0:T(8,128)S(1)}, u32[]{:S(2)}, u32[]{:S(2)}) %all-to-all-start) | async-done | bytes 786464 | tf_op jit(solution)/shard_map/all_to_all | solution.py:166
  48.5 1.7 place.1.b_ref.panel_ref.refs_0_
  50.3 3.2 %collective-permute-start = (f32[64,512]{1,0:T(8,128)S(1)}, f32[64,512]{1,0:T(8,128)S(1)}, u32[]{:S(2)}, u32[]{:S(2)}) collective-permute-start(f32[64,512]{1,0:T(8,128)S(1)} %get-tuple-element.2), channel_id=1, source_target_pairs={{0,1},{8,9},{16,17},{24,25},{32,33},{40,41},{48,49},{56,57},{64,65... | collective-permute-start | bytes 393224 | tf_op jit(solution)/shard_map/ppermute | solution.py:195
  53.5 2.6 %collective-permute-start.6 = (f32[64,512]{1,0:T(8,128)S(1)}, f32[64,512]{1,0:T(8,128)S(1)}, u32[]{:S(2)}, u32[]{:S(2)}) collective-permute-start(f32[64,512]{1,0:T(8,128)S(1)} %get-tuple-element.3), channel_id=1, source_target_pairs={{0,7},{8,15},{16,23},{24,31},{32,39},{40,47},{48,55},{56,63},{64,7... | collective-permute-start | bytes 393224 | tf_op jit(solution)/shard_map/ppermute | solution.py:195
  63.1 1.5 gram.1
  64.6 5.2 %all_to_all.40 = f32[2,768,128]{2,1,0:T(8,128)S(1)} all-to-all(f32[2,768,128]{2,1,0:T(8,128)S(1)} %bitcast.15), channel_id=1, replica_groups=mesh['z'=8,'x'=4,'core'=2,'col'=8] {'core'}, dimensions={0} | all-to-all | bytes 1572864 | tf_op jit(solution)/shard_map/all_to_all | solution.py:166
  70.7 4.8 %all-to-all-start.5 = ((f32[32,24,128]{2,1,0:T(8,128)}), f32[32,24,128]{2,1,0:T(8,128)S(1)}, u32[]{:S(2)}, u32[]{:S(2)}) async-start(f32[32,24,128]{2,1,0:T(8,128)} %bitcast.9), calls=%async_computation.5 | async-start | bytes 786432 | tf_op jit(solution)/shard_map/all_to_all | solution.py:166
  76.4 13.0 %all-to-all-done.5 = f32[32,24,128]{2,1,0:T(8,128)S(1)} async-done(((f32[32,24,128]{2,1,0:T(8,128)}), f32[32,24,128]{2,1,0:T(8,128)S(1)}, u32[]{:S(2)}, u32[]{:S(2)}) %all-to-all-start.5) | async-done | bytes 393248 | tf_op jit(solution)/shard_map/all_to_all | solution.py:166
  89.4 10.8 %all_to_all.41 = f32[8,24,128]{2,1,0:T(8,128)S(1)} all-to-all(f32[8,24,128]{2,1,0:T(8,128)S(1)} %broadcast_in_dim.38), channel_id=1, replica_groups=mesh['z'=8,'x'=4,'core'=2,'col'=8] {'col'}, dimensions={0} | all-to-all | bytes 196608 | tf_op jit(solution)/shard_map/all_to_all | solution.py:166
  100.3 16.4 %all_to_all.42 = f32[32,24,128]{2,1,0:T(8,128)S(1)} all-to-all(f32[32,24,128]{2,1,0:T(8,128)S(1)} %broadcast_in_dim.40), channel_id=1, replica_groups=mesh['z'=8,'x'=4,'core'=2,'col'=8] {'z','x'}, dimensions={0} | all-to-all | bytes 786432 | tf_op jit(solution)/shard_map/all_to_all | solution.py:166
  116.6 7.1 %collective-permute-start.8 = (f32[768,128]{1,0:T(8,128)S(1)}, f32[768,128]{1,0:T(8,128)}, u32[]{:S(2)}, u32[]{:S(2)}) collective-permute-start(f32[768,128]{1,0:T(8,128)S(1)} %bitcast.17), channel_id=1, source_target_pairs={{0,8},{8,0},{1,9},{9,1},{2,10},{10,2},{3,11},{11,3},{4,12},{12,4},... | collective-permute-start | bytes 1179656 | tf_op jit(solution)/shard_map/ppermute | solution.py:182
  125.0 1.8 products.1
  126.8 4.2 %all_to_all.43 = f32[2,256,512]{2,1,0:T(8,128)S(1)} all-to-all(f32[2,256,512]{2,1,0:T(8,128)S(1)} %bitcast.13), channel_id=1, replica_groups=mesh['z'=8,'x'=4,'core'=2,'col'=8] {'core'}, dimensions={0} | all-to-all | bytes 2097152 | tf_op jit(solution)/shard_map/all_to_all | solution.py:166
  131.9 3.9 %all-to-all-start.2 = ((f32[32,8,512]{2,1,0:T(8,128)}), f32[32,8,512]{2,1,0:T(8,128)S(1)}, u32[]{:S(2)}, u32[]{:S(2)}) async-start(f32[32,8,512]{2,1,0:T(8,128)} %bitcast.5), calls=%async_computation.2 | async-start | bytes 1048576 | tf_op jit(solution)/shard_map/all_to_all | solution.py:166
  137.1 11.8 %factor0.1.refs_1_.refs_4_ = f32[128,1024]{1,0:T(8,128)S(1)} custom-call(f32[1536,128]{1,0:T(8,128)S(1)} %maximum_select_fusion.1.refs_0_), custom_call_target="tpu_custom_call" | custom-call | flops 10737418240 | bytes 4194304 | tf_op jit(solution)/shard_map/factor0/pallas_call | solution.py:42
  148.9 3.6 %all-to-all-done.2 = f32[32,8,512]{2,1,0:T(8,128)S(1)} async-done(((f32[32,8,512]{2,1,0:T(8,128)}), f32[32,8,512]{2,1,0:T(8,128)S(1)}, u32[]{:S(2)}, u32[]{:S(2)}) %all-to-all-start.2) | async-done | bytes 524320 | tf_op jit(solution)/shard_map/all_to_all | solution.py:166
  153.4 5.9 %all-to-all-start.3 = ((f32[32,8,512]{2,1,0:T(8,128)}), f32[32,8,512]{2,1,0:T(8,128)}, u32[]{:S(2)}, u32[]{:S(2)}) async-start(f32[32,8,512]{2,1,0:T(8,128)} %broadcast_in_dim.37), calls=%async_computation.3 | async-start | bytes 1048576 | tf_op jit(solution)/shard_map/all_to_all | solution.py:166
  159.3 12.2 %factor1.1.refs_2_.refs_5_ = f32[128,1024]{1,0:T(8,128)S(1)} custom-call(f32[1536,128]{1,0:T(8,128)S(1)} %maximum_select_fusion.1.refs_0_, f32[128,1024]{1,0:T(8,128)S(1)} %factor0.1.refs_1_.refs_4_), custom_call_target="tpu_custom_call" | custom-call | flops 10737418240 | bytes 4194304 | tf_op jit(solution)/shard_map/factor1/pallas_call | solution.py:42
  171.5 12.5 %factor2.1.refs_3_.refs_6_ = f32[128,1024]{1,0:T(8,128)S(1)} custom-call(f32[1536,128]{1,0:T(8,128)S(1)} %maximum_select_fusion.1.refs_0_, f32[128,1024]{1,0:T(8,128)S(1)} %factor0.1.refs_1_.refs_4_, f32[128,1024]{1,0:T(8,128)S(1)} %factor1.1.refs_2_.refs_5_), custom_call_target="tpu_custom_call" | custom-call | flops 10737418240 | bytes 4194304 | tf_op jit(solution)/shard_map/factor2/pallas_call | solution.py:42
  184.1 3.0 %collective-permute-start.7 = (f32[256,512]{1,0:T(8,128)}, f32[256,512]{1,0:T(8,128)S(1)}, u32[]{:S(2)}, u32[]{:S(2)}) collective-permute-start(f32[256,512]{1,0:T(8,128)} %bitcast.6), channel_id=1, source_target_pairs={{0,8},{8,0},{1,9},{9,1},{2,10},{10,2},{3,11},{11,3},{4,12},{12,4},... | collective-permute-start | bytes 1572872 | tf_op jit(solution)/shard_map/ppermute | solution.py:182
  187.1 12.7 %factor3.1.refs_7_ = f32[128,1024]{1,0:T(8,128)S(1)} custom-call(f32[1536,128]{1,0:T(8,128)S(1)} %maximum_select_fusion.1.refs_0_, f32[128,1024]{1,0:T(8,128)S(1)} %factor0.1.refs_1_.refs_4_, f32[128,1024]{1,0:T(8,128)S(1)} %factor1.1.refs_2_.refs_5_, f32[128,1024]{1,0:T(8,128)S(1)} %factor2.1.refs_3_.refs_6_), custom_call_target="tpu_custom_call" | custom-call | flops 10737418240 | bytes 4194304 | tf_op jit(solution)/shard_map/factor3/pallas_call | solution.py:42
  201.3 6.4 %final.1 = (f32[512,512]{1,0:T(8,128)}, f32[512,512]{1,0:T(8,128)}) custom-call(f32[512,512]{1,0:T(8,128)S(1)} %place.1.b_ref.panel_ref.refs_0_, f32[512,512]{1,0:T(8,128)S(1)} %copy-done.2, f32[512,512]{1,0:T(8,128)S(1)} %maximum_select_fusion.refs_2_, s32[1,1]{1,0:T(1,128)} %bitcast.7.refs_3_, f32[128,1024]{1,0:T(8,128)S(1)} %factor0.1.refs_1_.refs_4_, ...), custom_call_target="tpu_custom_call" | custom-call | flops 6442450944 | bytes 4194304 | tf_op jit(solution)/shard_map/final/pallas_call | solution.py:42
  (44 shorter events, 16.1 us)
Async XLA Ops:
  7.9 0.7 copy-start.4
  10.8 15.0 %copy-start.3 = (s32[256]{0:T(256)S(1)}, s32[256]{0:T(256)}, u32[]{:S(2)}) copy-start(s32[256]{0:T(256)} %param.9) | copy-start | bytes 3076
  10.8 37.7 %copy-start = (f32[512,512]{1,0:T(8,128)S(1)}, f32[512,512]{1,0:T(8,128)}, u32[]{:S(2)}) copy-start(f32[512,512]{1,0:T(8,128)} %front_ref.1) | copy-start | bytes 3145732
  10.8 37.7 %all-to-all-start = ((f32[64,8,384]{2,1,0:T(8,128)}), f32[64,8,384]{2,1,0:T(8,128)S(1)}, u32[]{:S(2)}, u32[]{:S(2)}) async-start(f32[64,8,384]{2,1,0:T(8,128)} %pad_maximum_fusion), calls=%async_computation | async-start | bytes 1572864 | tf_op jit(solution)/shard_map/all_to_all | solution.py:166
  50.3 10.2 %collective-permute-start = (f32[64,512]{1,0:T(8,128)S(1)}, f32[64,512]{1,0:T(8,128)S(1)}, u32[]{:S(2)}, u32[]{:S(2)}) collective-permute-start(f32[64,512]{1,0:T(8,128)S(1)} %get-tuple-element.2), channel_id=1, source_target_pairs={{0,1},{8,9},{16,17},{24,25},{32,33},{40,41},{48,49},{56,57},{64,65... | collective-permute-start | bytes 393224 | tf_op jit(solution)/shard_map/ppermute | solution.py:195
  53.5 8.3 %collective-permute-start.6 = (f32[64,512]{1,0:T(8,128)S(1)}, f32[64,512]{1,0:T(8,128)S(1)}, u32[]{:S(2)}, u32[]{:S(2)}) collective-permute-start(f32[64,512]{1,0:T(8,128)S(1)} %get-tuple-element.3), channel_id=1, source_target_pairs={{0,7},{8,15},{16,23},{24,31},{32,39},{40,47},{48,55},{56,63},{64,7... | collective-permute-start | bytes 393224 | tf_op jit(solution)/shard_map/ppermute | solution.py:195
  56.1 19.5 %collective-permute-start.5 = (f32[64,512]{1,0:T(8,128)S(1)}, f32[64,512]{1,0:T(8,128)S(1)}, u32[]{:S(2)}, u32[]{:S(2)}) collective-permute-start(f32[64,512]{1,0:T(8,128)S(1)} %get-tuple-element.4), channel_id=1, source_target_pairs={{0,6},{8,14},{16,22},{24,30},{32,38},{40,46},{48,54},{56,62},{64,7... | collective-permute-start | bytes 393224 | tf_op jit(solution)/shard_map/ppermute | solution.py:195
  57.5 18.0 %collective-permute-start.4 = (f32[64,512]{1,0:T(8,128)S(1)}, f32[64,512]{1,0:T(8,128)S(1)}, u32[]{:S(2)}, u32[]{:S(2)}) collective-permute-start(f32[64,512]{1,0:T(8,128)S(1)} %get-tuple-element.5), channel_id=1, source_target_pairs={{0,5},{8,13},{16,21},{24,29},{32,37},{40,45},{48,53},{56,61},{64,6... | collective-permute-start | bytes 393224 | tf_op jit(solution)/shard_map/ppermute | solution.py:195
  59.0 16.6 %collective-permute-start.3 = (f32[64,512]{1,0:T(8,128)S(1)}, f32[64,512]{1,0:T(8,128)S(1)}, u32[]{:S(2)}, u32[]{:S(2)}) collective-permute-start(f32[64,512]{1,0:T(8,128)S(1)} %get-tuple-element.6), channel_id=1, source_target_pairs={{0,4},{8,12},{16,20},{24,28},{32,36},{40,44},{48,52},{56,60},{64,6... | collective-permute-start | bytes 393224 | tf_op jit(solution)/shard_map/ppermute | solution.py:195
  60.5 15.1 %collective-permute-start.2 = (f32[64,512]{1,0:T(8,128)S(1)}, f32[64,512]{1,0:T(8,128)S(1)}, u32[]{:S(2)}, u32[]{:S(2)}) collective-permute-start(f32[64,512]{1,0:T(8,128)S(1)} %get-tuple-element.7), channel_id=1, source_target_pairs={{0,3},{8,11},{16,19},{24,27},{32,35},{40,43},{48,51},{56,59},{64,6... | collective-permute-start | bytes 393224 | tf_op jit(solution)/shard_map/ppermute | solution.py:195
  61.8 13.8 %collective-permute-start.1 = (f32[64,512]{1,0:T(8,128)S(1)}, f32[64,512]{1,0:T(8,128)S(1)}, u32[]{:S(2)}, u32[]{:S(2)}) collective-permute-start(f32[64,512]{1,0:T(8,128)S(1)} %get-tuple-element.8), channel_id=1, source_target_pairs={{0,2},{8,10},{16,18},{24,26},{32,34},{40,42},{48,50},{56,58},{64,6... | collective-permute-start | bytes 393224 | tf_op jit(solution)/shard_map/ppermute | solution.py:195
  70.7 18.7 %all-to-all-start.5 = ((f32[32,24,128]{2,1,0:T(8,128)}), f32[32,24,128]{2,1,0:T(8,128)S(1)}, u32[]{:S(2)}, u32[]{:S(2)}) async-start(f32[32,24,128]{2,1,0:T(8,128)} %bitcast.9), calls=%async_computation.5 | async-start | bytes 786432 | tf_op jit(solution)/shard_map/all_to_all | solution.py:166
  75.5 48.3 %all-gather.2.cloned.1.call-start = ((), (), s32[]{:S(2)}) async-start(), calls=%async_computation.8 | async-start | bytes 1179648 | tf_op jit(solution)/shard_map/all_gather | solution.py:196
  116.6 19.2 %collective-permute-start.8 = (f32[768,128]{1,0:T(8,128)S(1)}, f32[768,128]{1,0:T(8,128)}, u32[]{:S(2)}, u32[]{:S(2)}) collective-permute-start(f32[768,128]{1,0:T(8,128)S(1)} %bitcast.17), channel_id=1, source_target_pairs={{0,8},{8,0},{1,9},{9,1},{2,10},{10,2},{3,11},{11,3},{4,12},{12,4},... | collective-permute-start | bytes 1179656 | tf_op jit(solution)/shard_map/ppermute | solution.py:182
  123.8 1.2 copy-start.1
  131.9 20.5 %all-to-all-start.2 = ((f32[32,8,512]{2,1,0:T(8,128)}), f32[32,8,512]{2,1,0:T(8,128)S(1)}, u32[]{:S(2)}, u32[]{:S(2)}) async-start(f32[32,8,512]{2,1,0:T(8,128)} %bitcast.5), calls=%async_computation.2 | async-start | bytes 1048576 | tf_op jit(solution)/shard_map/all_to_all | solution.py:166
  153.4 30.7 %all-to-all-start.3 = ((f32[32,8,512]{2,1,0:T(8,128)}), f32[32,8,512]{2,1,0:T(8,128)}, u32[]{:S(2)}, u32[]{:S(2)}) async-start(f32[32,8,512]{2,1,0:T(8,128)} %broadcast_in_dim.37), calls=%async_computation.3 | async-start | bytes 1048576 | tf_op jit(solution)/shard_map/all_to_all | solution.py:166
  184.1 15.8 %collective-permute-start.7 = (f32[256,512]{1,0:T(8,128)}, f32[256,512]{1,0:T(8,128)S(1)}, u32[]{:S(2)}, u32[]{:S(2)}) collective-permute-start(f32[256,512]{1,0:T(8,128)} %bitcast.6), channel_id=1, source_target_pairs={{0,8},{8,0},{1,9},{9,1},{2,10},{10,2},{3,11},{11,3},{4,12},{12,4},... | collective-permute-start | bytes 1572872 | tf_op jit(solution)/shard_map/ppermute | solution.py:182
  199.8 1.5 copy-start.2
Sparse Core Ops, SparseCore 0:
  79.0 33.3 all-gather.1

commit v3 on v2

v3 whole, which is shorter than its diff:
```python
import math

import jax
import jax.numpy as jnp
from jax import lax
from jax.experimental import pallas as pl
from jax.experimental.pallas import tpu as pltpu
from jax.sharding import Mesh, PartitionSpec as P

PANELS = 512
BLOCK = 128
SUB = 64
PIECES = 2
ROW = ("z", "x", "core")
VMEM = pl.BlockSpec(memory_space=pltpu.VMEM)
SMEM = pl.BlockSpec(memory_space=pltpu.SMEM)


def dot_fast(a, b, ca=1, cb=0):
    return lax.dot_general(
        a, b, (((ca,), (cb,)), ((), ())), preferred_element_type=jnp.float32
    )


def dot(a, b, ca=1, cb=0):
    return lax.dot_general(
        a,
        b,
        (((ca,), (cb,)), ((), ())),
        precision=lax.Precision.HIGHEST,
        preferred_element_type=jnp.float32,
    )


def split3(a):
    hi = a.astype(jnp.bfloat16)
    rest = a - hi.astype(jnp.float32)
    mid = rest.astype(jnp.bfloat16)
    low = (rest - mid.astype(jnp.float32)).astype(jnp.bfloat16)
    return hi, mid, low


def f32(*shape):
    return jax.ShapeDtypeStruct(shape, jnp.float32)


def call(kernel, out_shape, name, flops, *args, scalars=(), scratch=()):
    return pl.pallas_call(
        kernel,
        out_shape=out_shape,
        in_specs=[SMEM] * len(scalars) + [VMEM] * len(args),
        out_specs=jax.tree.map(lambda _: VMEM, out_shape),
        scratch_shapes=scratch,
        name=name,
        compiler_params=pltpu.CompilerParams(vmem_limit_bytes=14 << 20),
        cost_estimate=pl.CostEstimate(flops=flops, bytes_accessed=4 << 20, transcendentals=0),
    )(*[s.reshape(1, 1) for s in scalars], *args)


def iota(shape, axis):
    return lax.broadcasted_iota(jnp.int32, shape, axis)


def hot(mask):
    return mask.astype(jnp.float32).astype(jnp.bfloat16)


def eye(size):
    return (iota((size, size), 0) == iota((size, size), 1)).astype(jnp.float32)


def pack_kernel(height, capacity, child_ref, rows_ref, live_ref, out_ref):
    count, width = child_ref.shape
    owners = live_ref.shape[1]
    lanes = rows_ref.shape[1]
    out_ref[:, :width] = child_ref[...]
    live = jnp.broadcast_to(live_ref[...].astype(jnp.float32), (count, owners))
    owner = lax.div(iota((count, owners), 0), jnp.int32(capacity))
    live = jnp.sum(jnp.where(owner == iota((count, owners), 1), live, 0.0), axis=1, keepdims=True)
    slot = lax.rem(iota((count, 1), 0), jnp.int32(capacity)).astype(jnp.float32)
    local = lax.rem(rows_ref[...], jnp.int32(height)).astype(jnp.float32)
    identity = eye(lanes)
    rows = jnp.concatenate(
        [
            jnp.sum(jnp.broadcast_to(local[g : g + 1, :], (lanes, lanes)) * identity, axis=1, keepdims=True)
            for g in range(count // lanes)
        ],
        axis=0,
    )
    targets = jnp.where(slot < live, rows, -1.0)
    out_ref[:, width:] = jnp.broadcast_to(targets, (count, BLOCK))


def placed(front, rows, targets, cols):
    height, width = front.shape
    count, child_width = rows.shape
    col_hot = hot(iota((width, child_width), 0) == cols)
    row_hot = hot(iota((count, height), 1) == targets)
    total = front
    for term in split3(rows):
        spread = dot_fast(term, col_hot, 1, 1).astype(jnp.bfloat16)
        total = total + dot_fast(row_hot, spread, 0, 0)
    return total


def place_kernel(front_ref, arrived_ref, cols_ref, out_ref, shares_ref):
    child_width = cols_ref.shape[1]
    rows = arrived_ref[:, :child_width]
    targets = arrived_ref[:, child_width : child_width + 1].astype(jnp.int32)
    out_ref[...] = placed(front_ref[...], rows, targets, cols_ref[...])
    parts, height = shares_ref.shape[0], shares_ref.shape[1] // 2
    for k in range(parts):
        for h in range(2):
            shares_ref[k, h * height : (h + 1) * height, :] = rows[
                k * height : (k + 1) * height, h * BLOCK : (h + 1) * BLOCK
            ]


def place_panel_kernel(front_ref, shares_ref, cols_ref, arrived_ref, out_ref):
    parts, height = shares_ref.shape[0], shares_ref.shape[1] // 2
    child_width = 2 * BLOCK
    rows = jnp.concatenate(
        [
            jnp.concatenate([shares_ref[k, :height, :], shares_ref[k, height:, :]], axis=1)
            for k in range(parts)
        ],
        axis=0,
    )
    cols = jnp.concatenate([cols_ref[0:1, :], cols_ref[1:2, :]], axis=1).astype(jnp.int32)
    targets = arrived_ref[:, child_width : child_width + 1].astype(jnp.int32)
    out_ref[...] = placed(front_ref[...], rows, targets, cols)


def halves(core_ref, whole_ref, keep_ref, send_ref):
    height = keep_ref.shape[0]
    core = core_ref[0, 0]
    keep_ref[...] = whole_ref[pl.ds(pl.multiple_of(core * height, height), height), :]
    send_ref[...] = whole_ref[pl.ds(pl.multiple_of((1 - core) * height, height), height), :]


def gram_place(i, j):
    if i < 2:
        return (2 * j + i) * BLOCK
    return (2 * PANELS // BLOCK + 2 * (j - 2) + i - 2) * BLOCK


def gram_kernel(core_ref, panel_ref, keep_ref, send_ref, whole_ref):
    half = PANELS // 2
    for first in range(2):
        cols = slice(half * first, PANELS)
        product = dot(panel_ref[:, half * first : half * (first + 1)], panel_ref[:, cols], 0, 0)
        for i in range(2):
            for j in range(2 * first, PANELS // BLOCK):
                at = gram_place(2 * first + i, j)
                left = (j - 2 * first) * BLOCK
                whole_ref[at : at + BLOCK, :] = product[i * BLOCK : (i + 1) * BLOCK, left : left + BLOCK]
    halves(core_ref, whole_ref, keep_ref, send_ref)


def product_kernel(core_ref, panel_ref, front_ref, keep_ref, send_ref, whole_ref):
    whole_ref[...] = dot(panel_ref[...], front_ref[...], 0, 0)
    halves(core_ref, whole_ref, keep_ref, send_ref)


def factor_diagonal(block):
    width = block.shape[1]
    done = []
    rest = block
    at_narrow, at_wide = iota((8, BLOCK), 0), iota((8, width), 0)
    count = SUB // 8
    for sub in range(BLOCK // SUB):
        groups = [rest[8 * g : 8 * g + 8, :] for g in range(count)]
        for p in range(count):
            first = SUB * sub + 8 * p
            spread = {
                (g, k): jnp.broadcast_to(groups[g][:, first + k : first + k + 1], (8, BLOCK))
                for g in range(p, count)
                for k in range(8)
            }
            for j in range(8):
                scale = lax.rsqrt(jnp.broadcast_to(spread[p, j][j : j + 1, :], (8, BLOCK)))
                factor = {g: spread[g, j] * scale for g in range(p, count)}
                factor[p] = jnp.where(at_narrow > j, factor[p], 0.0)
                for k in range(j + 1, 8):
                    pivot = jnp.broadcast_to(spread[p, k][j : j + 1, :], (8, BLOCK)) * scale
                    for g in range(p, count):
                        spread[g, k] = spread[g, k] - factor[g] * pivot
                wide = jnp.concatenate([scale] * (width // BLOCK), axis=1)
                row = jnp.broadcast_to(groups[p][j : j + 1, :], (8, width)) * wide
                for g in range(p, count):
                    updated = groups[g] - jnp.concatenate([factor[g]] * (width // BLOCK), axis=1) * row
                    groups[g] = jnp.where(at_wide == j, row, updated) if g == p else updated
        rows = jnp.concatenate(groups, axis=0)
        done.append(rows)
        if sub + 1 < BLOCK // SUB:
            rest = rest[SUB:, :] - dot(rows[:, SUB * (sub + 1) : BLOCK], rows, 0, 0)
    return jnp.concatenate(done, axis=0)


def in_order(core_ref, own, other):
    first = core_ref[0, 0] == 0
    return jnp.concatenate(
        [jnp.where(first, own, other), jnp.where(first, other, own)], axis=0
    )


def factor_kernel(piece, core_ref, own_ref, other_ref, *refs):
    above, out_ref = refs[:-1], refs[-1]
    n = PANELS
    per = n // BLOCK // PIECES
    gram = in_order(core_ref, own_ref[...], other_ref[...])
    identity = eye(BLOCK)

    def rows_of(block):
        at = block % per * BLOCK
        return (*above, out_ref)[block // per], slice(at, at + BLOCK)

    for k in range(piece * per, (piece + 1) * per):
        _, rows = rows_of(k)
        low, high = k * BLOCK, n + (k + 1) * BLOCK
        starts = [gram_place(k, j) for j in range(k, n // BLOCK)]
        pad = [jnp.zeros((BLOCK, low), jnp.float32)] if k else []
        work = jnp.concatenate([gram[at : at + BLOCK, :] for at in starts] + pad + [identity], axis=1)
        for upper in range(k):
            ref, at = rows_of(upper)
            work = work - dot(ref[at, low : low + BLOCK], ref[at, low:high], 0, 0)
        diagonal = factor_diagonal(jnp.concatenate([work[:, :BLOCK], identity], axis=1))
        out_ref[rows, low:high] = dot(diagonal[:, BLOCK:], work)
        out_ref[rows, low : low + BLOCK] = diagonal[:, :BLOCK]
        if k:
            out_ref[rows, :low] = jnp.zeros((BLOCK, low), jnp.float32)
        if high < 2 * n:
            out_ref[rows, high:] = jnp.zeros((BLOCK, 2 * n - high), jnp.float32)


def inverse_rows(blocks, i):
    per = blocks[0].shape[0]
    ref, at = blocks[i * BLOCK // per], i * BLOCK % per
    return ref[at : at + BLOCK, PANELS : PANELS + (i + 1) * BLOCK]


def basis_kernel(panel_ref, *refs):
    blocks, out_ref = refs[:-1], refs[-1]
    for i in range(PANELS // BLOCK):
        upto = (i + 1) * BLOCK
        out_ref[:, i * BLOCK : upto] = dot(panel_ref[:, :upto], inverse_rows(blocks, i), 1, 1)


def final_kernel(root_rows, core_ref, root_ref, front_ref, basis_ref, own_ref, other_ref, *refs):
    blocks, (out_ref, factor_ref) = refs[:-2], refs[-2:]
    sums = in_order(core_ref, own_ref[...], other_ref[...])
    coupled = jnp.concatenate(
        [dot(inverse_rows(blocks, i), sums[: (i + 1) * BLOCK, :]) for i in range(PANELS // BLOCK)],
        axis=0,
    )
    is_root = root_ref[0, 0] == 1
    basis = basis_ref[...]
    basis_hi, basis_mid, _ = split3(basis)
    coupled_hi, coupled_mid, _ = split3(coupled)
    update = dot_fast(basis_mid, coupled_hi) + dot_fast(basis_hi, coupled_mid)
    update = update + dot_fast(basis_hi, coupled_hi)
    out_ref[...] = jnp.where(is_root, basis * root_rows, front_ref[...] - update)
    upper = jnp.concatenate([ref[:, :PANELS] for ref in blocks], axis=0)
    factor_ref[...] = jnp.where(is_root, upper, coupled) * (1.0 / root_rows)


def exchange(blocks, axis):
    return lax.all_to_all(blocks, axis, split_axis=0, concat_axis=0, tiled=True)


def repeated(x, n):
    return jnp.broadcast_to(x[None], (n,) + x.shape)


def swapped(x):
    return lax.ppermute(x, "core", [(0, 1), (1, 0)])


def chip_share(x):
    n = lax.axis_size(("z", "x"))
    return jnp.sum(exchange(x.reshape(n, x.shape[0] // n, x.shape[1]), ("z", "x")), axis=0)


def all_shares(x):
    n = lax.axis_size(("z", "x"))
    return exchange(repeated(x, n), ("z", "x")).reshape(n * x.shape[0], x.shape[1])


def share_of_root(shares):
    mine = jnp.where(lax.axis_index("col") == 0, shares[0], 0.0)
    for k in range(1, lax.axis_size("col")):
        mine = mine + lax.ppermute(shares[k], "col", [(0, k)])
    return mine


def on_device(front_in, child_block, child_rows, live_counts, column_map):
    rows_dev, cols_dev = front_in.shape
    owners, parts = lax.axis_size(ROW), lax.axis_size("col")
    count, child_width = child_block.shape
    capacity = count // owners
    core = lax.axis_index("core").astype(jnp.int32)
    is_root = (lax.axis_index("col") == 0).astype(jnp.int32)
    halved = (f32(3 * PANELS // 2, BLOCK),) * 2
    local_cols = column_map % cols_dev

    sent = call(
        lambda *refs: pack_kernel(rows_dev, capacity, *refs),
        f32(count, child_width + BLOCK), "pack", 1 << 20,
        child_block, child_rows.reshape(count // BLOCK, BLOCK), live_counts,
    )
    arrived = exchange(sent.reshape(owners, capacity, child_width + BLOCK), ROW)
    arrived = arrived.reshape(count, child_width + BLOCK)
    front_share = share_of_root(front_in.reshape(parts, rows_dev // parts, cols_dev))
    arrived, front_share = lax.optimization_barrier((arrived, front_share))
    panel_front = lax.all_gather(front_share, "col", tiled=True)

    front, shares = call(
        place_kernel, (f32(rows_dev, cols_dev), f32(parts, 2 * count // parts, BLOCK)),
        "place", 2 << 30, front_in, arrived, local_cols.reshape(1, child_width),
    )
    keep, send = call(
        gram_kernel, halved, "gram", 2 << 30, front, scalars=(core,),
        scratch=[pltpu.VMEM((3 * PANELS, BLOCK), jnp.float32)],
    )
    half, shares = lax.optimization_barrier((keep + swapped(send), shares))
    gram_share = chip_share(half)

    rows_of_share = 2 * count // parts
    to_all = jnp.concatenate(
        [
            share_of_root(shares),
            gram_share,
            local_cols.astype(jnp.float32).reshape(child_width // BLOCK, BLOCK),
            jnp.zeros((8 - child_width // BLOCK, BLOCK), jnp.float32),
        ],
        axis=0,
    )
    from_all = exchange(repeated(to_all, parts), "col")
    gram_end = rows_of_share + gram_share.shape[0]
    own_gram = all_shares(from_all[0, rows_of_share:gram_end])
    other_gram = swapped(own_gram)

    panel = call(
        place_panel_kernel, f32(rows_dev, PANELS), "place_panel", 2 << 30,
        panel_front, from_all[:, :rows_of_share], from_all[0, gram_end:], arrived,
    )
    keep, send = call(
        product_kernel, (f32(PANELS // 2, cols_dev),) * 2, "products", 2 << 30, panel, front,
        scalars=(core,), scratch=[pltpu.VMEM((PANELS, cols_dev), jnp.float32)],
    )
    sums_share = chip_share(keep + swapped(send))

    blocks = []
    for piece in range(PIECES):
        blocks.append(
            call(
                lambda *refs, piece=piece: factor_kernel(piece, *refs),
                f32(PANELS // PIECES, 2 * PANELS), f"factor{piece}", 10 << 30,
                own_gram, other_gram, *blocks, scalars=(core,),
            )
        )
        if piece == 0:
            sums_share, blocks[0] = lax.optimization_barrier((sums_share, blocks[0]))
            own_sums = all_shares(sums_share)
    own_sums, blocks[1] = lax.optimization_barrier((own_sums, blocks[1]))
    other_sums = swapped(own_sums)
    basis = call(basis_kernel, f32(rows_dev, PANELS), "basis", 2 << 30, panel, *blocks)
    return call(
        lambda *refs: final_kernel(math.sqrt(rows_dev * owners), *refs),
        (f32(rows_dev, cols_dev), f32(PANELS, cols_dev)), "final", 4 << 30,
        front, basis, own_sums, other_sums, *blocks, scalars=(core, is_root),
    )


def solution(mesh):
    row, col = mesh.shape["row"], mesh.shape["col"]
    fine = Mesh(mesh.devices.reshape(8, 4, row // 32, col), ROW + ("col",))
    return jax.shard_map(
        on_device,
        mesh=fine,
        in_specs=(P(ROW, "col"), P(ROW, "col"), P(ROW), P(ROW, None), P("col")),
        out_specs=(P(ROW, "col"), P(None, "col")),
        check_vma=False,
    )
```

time: 216 us -> 195 us (0.903)
  Pallas kernels: 60.7 us -> 32.3 us
  starting transfers between devices: 52.4 us -> 80.6 us
  waiting for transfers between devices: 39.4 us -> 24.6 us
  blocking collectives: 36.6 us -> 28.4 us
  local copies, waits for them, and re-layouts: 3.81 us -> 11.2 us
  other arithmetic: 7.22 us -> 2.61 us
    pallas_call x8 -> x9, Pallas kernels: 60.7 us -> 32.3 us  [call(): pl.pallas_call(kernel, out_shape=out_shape, in_specs=[SMEM] * len(scalars...]
    all_to_all x4 -> x5, waiting for transfers between devices: 39.3 us -> 13.8 us  [exchange(): return lax.all_to_all(blocks, axis, split_axis=0, concat_axis=0, tiled=True)]
    ppermute x9 -> x18, starting transfers between devices: 22.8 us -> 45.2 us  [the longest x14 25.5 us: share_of_root(): mine = mine + lax.ppermute(shares[k], 'col', [(0, k)])]
    all_to_all x4 -> x1, blocking collectives: 36.6 us -> 28.4 us  [exchange(): return lax.all_to_all(blocks, axis, split_axis=0, concat_axis=0, tiled=True)]
    unnamed x10 -> x32, local copies, waits for them, and re-layouts: 1.95 us -> 9.26 us
    ppermute x9 -> x18, waiting for transfers between devices: 0.02 us -> 7.12 us  [the longest x14 5.78 us: share_of_root(): mine = mine + lax.ppermute(shares[k], 'col', [(0, k)])]
    all_to_all x4 -> x5, starting transfers between devices: 29.6 us -> 35.3 us  [exchange(): return lax.all_to_all(blocks, axis, split_axis=0, concat_axis=0, tiled=True)]
    all_gather x1, waiting for transfers between devices: 0.02 us -> 3.72 us  [on_device(): panel_front = lax.all_gather(front_share, 'col', tiled=True)]
  transfers between devices with their start and end apart: 14 -> 24, of which waited for: 3 -> 9; matrix products, arithmetic and copies ran while one was open for 2% -> 1% of each run, Pallas kernels for 25% -> 13%
where the time goes in v3:
time: 195 us; the launch traced here: 194 us
  starting transfers between devices  80.6 us (41%)
  Pallas kernels  32.3 us (17%)
  blocking collectives  28.4 us (15%)
  waiting for transfers between devices  24.6 us (13%)
  between operations  14.6 us (7%)
  local copies, waits for them, and re-layouts  11.2 us (6%)
  other arithmetic  2.61 us (1%)
    all_to_all x5, starting transfers between devices, exchange(): return lax.all_to_all(blocks, axis, split_axis=0, concat_axis=0, tiled=True)  35.3 us
    pallas_call x9, Pallas kernels, call(): pl.pallas_call(kernel, out_shape=out_shape, in_specs=[SMEM] * len(scalars...  32.3 us
    all_to_all x1, blocking collectives, exchange(): return lax.all_to_all(blocks, axis, split_axis=0, concat_axis=0, tiled=True)  28.4 us
    ppermute x14, starting transfers between devices, share_of_root(): mine = mine + lax.ppermute(shares[k], 'col', [(0, k)])  25.5 us
    ppermute x4, starting transfers between devices, swapped(): return lax.ppermute(x, 'core', [(0, 1), (1, 0)])  19.7 us
    all_to_all x5, waiting for transfers between devices, exchange(): return lax.all_to_all(blocks, axis, split_axis=0, concat_axis=0, tiled=True)  13.8 us
    unnamed x32, local copies, waits for them, and re-layouts  9.26 us
    ppermute x14, waiting for transfers between devices, share_of_root(): mine = mine + lax.ppermute(shares[k], 'col', [(0, k)])  5.78 us
  transfers between devices with their start and end apart: 24, of which 9 were waited for; matrix products, arithmetic and copies ran while one was open for 1% of the time, Pallas kernels for 13%

profile of v3, /device:TPU:1, one launch (start us, length us, event | category | flops | bytes accessed | tf_op | source)
XLA Modules:
  0.0 194.2 jit_solution(15999238919717157444)
XLA Ops:
  10.8 15.0 %all-to-all-start = ((f32[64,8,384]{2,1,0:T(8,128)}), f32[64,8,384]{2,1,0:T(8,128)S(1)}, u32[]{:S(2)}, u32[]{:S(2)}) async-start(f32[64,8,384]{2,1,0:T(8,128)} %bitcast.3), calls=%async_computation | async-start | bytes 1572864 | tf_op jit(solution)/shard_map/all_to_all | solution.py:268
  25.8 3.2 %collective-permute-start = (f32[64,512]{1,0:T(8,128)S(1)}, f32[64,512]{1,0:T(8,128)S(1)}, u32[]{:S(2)}, u32[]{:S(2)}) collective-permute-start(f32[64,512]{1,0:T(8,128)S(1)} %get-tuple-element.32), channel_id=1, source_target_pairs={{0,1},{8,9},{16,17},{24,25},{32,33},{40,41},{48,49},{56,57},{64,65... | collective-permute-start | bytes 393224 | tf_op jit(solution)/shard_map/ppermute | solution.py:292
  29.0 3.3 %collective-permute-start.5 = (f32[64,512]{1,0:T(8,128)S(1)}, f32[64,512]{1,0:T(8,128)S(1)}, u32[]{:S(2)}, u32[]{:S(2)}) collective-permute-start(f32[64,512]{1,0:T(8,128)S(1)} %get-tuple-element.33), channel_id=1, source_target_pairs={{0,6},{8,14},{16,22},{24,30},{32,38},{40,46},{48,54},{56,62},{64,7... | collective-permute-start | bytes 393224 | tf_op jit(solution)/shard_map/ppermute | solution.py:292
  40.5 2.8 %collective-permute-done.1 = f32[64,512]{1,0:T(8,128)S(1)} collective-permute-done((f32[64,512]{1,0:T(8,128)S(1)}, f32[64,512]{1,0:T(8,128)S(1)}, u32[]{:S(2)}, u32[]{:S(2)}) %collective-permute-start.1) | collective-permute-done | bytes 131104 | tf_op jit(solution)/shard_map/ppermute | solution.py:292
  44.1 4.4 %all-to-all-done = f32[64,8,384]{2,1,0:T(8,128)S(1)} async-done(((f32[64,8,384]{2,1,0:T(8,128)}), f32[64,8,384]{2,1,0:T(8,128)S(1)}, u32[]{:S(2)}, u32[]{:S(2)}) %all-to-all-start) | async-done | bytes 786464 | tf_op jit(solution)/shard_map/all_to_all | solution.py:268
  51.8 2.9 %collective-permute-start.7 = (f32[768,128]{1,0:T(8,128)S(1)}, f32[768,128]{1,0:T(8,128)S(1)}, u32[]{:S(2)}, u32[]{:S(2)}) collective-permute-start(f32[768,128]{1,0:T(8,128)S(1)} %get-tuple-element.20), channel_id=1, source_target_pairs={{0,8},{8,0},{1,9},{9,1},{2,10},{10,2},{3,11},{11,3},{4,12},{12,4},... | collective-permute-start | bytes 1179656 | tf_op jit(solution)/shard_map/ppermute | solution.py:276
  56.8 5.4 %all-to-all-start.1 = ((f32[32,24,128]{2,1,0:T(8,128)}), f32[32,24,128]{2,1,0:T(8,128)S(1)}, u32[]{:S(2)}, u32[]{:S(2)}) async-start(f32[32,24,128]{2,1,0:T(8,128)} %bitcast.14), calls=%async_computation.1 | async-start | bytes 786432 | tf_op jit(solution)/shard_map/all_to_all | solution.py:268
  62.3 2.6 %collective-permute-start.8 = (f32[128,128]{1,0:T(8,128)S(1)}, f32[128,128]{1,0:T(8,128)S(1)}, u32[]{:S(2)}, u32[]{:S(2)}) collective-permute-start(f32[128,128]{1,0:T(8,128)S(1)} %get-tuple-element.39), channel_id=1, source_target_pairs={{0,1},{8,9},{16,17},{24,25},{32,33},{40,41},{48,49},{56,57},{64,65... | collective-permute-start | bytes 196616 | tf_op jit(solution)/shard_map/ppermute | solution.py:292
  64.9 2.6 %collective-permute-start.14 = (f32[128,128]{1,0:T(8,128)S(1)}, f32[128,128]{1,0:T(8,128)S(1)}, u32[]{:S(2)}, u32[]{:S(2)}) collective-permute-start(f32[128,128]{1,0:T(8,128)S(1)} %get-tuple-element.40), channel_id=1, source_target_pairs={{0,7},{8,15},{16,23},{24,31},{32,39},{40,47},{48,55},{56,63},{64,7... | collective-permute-start | bytes 196616 | tf_op jit(solution)/shard_map/ppermute | solution.py:292
  76.6 28.4 %all_to_all.30 = f32[8,160,128]{2,1,0:T(8,128)S(1)} all-to-all(f32[8,160,128]{2,1,0:T(8,128)S(1)} %broadcast_in_dim.33), channel_id=1, replica_groups=mesh['z'=8,'x'=4,'core'=2,'col'=8] {'col'}, dimensions={0} | all-to-all | bytes 1310720 | tf_op jit(solution)/shard_map/all_to_all | solution.py:268
  105.7 5.6 %all-to-all-start.4 = ((f32[32,24,128]{2,1,0:T(8,128)}), f32[32,24,128]{2,1,0:T(8,128)S(1)}, u32[]{:S(2)}, u32[]{:S(2)}) async-start(f32[32,24,128]{2,1,0:T(8,128)} %broadcast_in_dim.35), calls=%async_computation.4 | async-start | bytes 786432 | tf_op jit(solution)/shard_map/all_to_all | solution.py:268
  111.4 3.7 %all-gather.2.cloned.1.call-done.front_ref = f32[512,512]{1,0:T(8,128)} async-done(((f32[64,512]{1,0:T(8,128)}), f32[512,512]{1,0:T(8,128)}) %all-gather.2.cloned.1.call-update) | async-done | bytes 1048592 | tf_op jit(solution)/shard_map/all_gather | solution.py:315
  118.1 1.9 products.1
  120.0 4.8 %collective-permute-start.15 = (f32[256,512]{1,0:T(8,128)S(1)}, f32[256,512]{1,0:T(8,128)S(1)}, u32[]{:S(2)}, u32[]{:S(2)}) collective-permute-start(f32[256,512]{1,0:T(8,128)S(1)} %get-tuple-element.25), channel_id=1, source_target_pairs={{0,8},{8,0},{1,9},{9,1},{2,10},{10,2},{3,11},{11,3},{4,12},{12,4},... | collective-permute-start | bytes 1572872 | tf_op jit(solution)/shard_map/ppermute | solution.py:276
  124.8 6.5 %collective-permute-start.16 = (f32[768,128]{1,0:T(8,128)S(1)}, f32[768,128]{1,0:T(8,128)S(1)}, u32[]{:S(2)}, u32[]{:S(2)}) collective-permute-start(f32[768,128]{1,0:T(8,128)S(1)} %bitcast.49), channel_id=1, source_target_pairs={{0,8},{8,0},{1,9},{9,1},{2,10},{10,2},{3,11},{11,3},{4,12},{12,4},... | collective-permute-start | bytes 1179656 | tf_op jit(solution)/shard_map/ppermute | solution.py:276
  132.2 4.1 %all-to-all-start.3 = ((f32[32,8,512]{2,1,0:T(8,128)}), f32[32,8,512]{2,1,0:T(8,128)S(1)}, u32[]{:S(2)}, u32[]{:S(2)}) async-start(f32[32,8,512]{2,1,0:T(8,128)} %add_bitcast_fusion), calls=%async_computation.3 | async-start | bytes 1048576 | tf_op jit(solution)/shard_map/all_to_all | solution.py:268
  136.3 8.8 %factor0.1.refs_3_.refs_0_.refs_6_ = f32[256,1024]{1,0:T(8,128)S(1)} custom-call(s32[1,1]{1,0:T(1,128)} %bitcast.core_ref.refs_0_, f32[768,128]{1,0:T(8,128)S(1)} %bitcast.50, f32[768,128]{1,0:T(8,128)S(1)} %collective-permute-done.16.refs_2_), custom_call_target="tpu_custom_call" | custom-call | flops 10737418240 | bytes 4194304 | tf_op jit(solution)/shard_map/factor0/pallas_call | solution.py:48
  146.1 6.5 %all-to-all-done.3 = f32[32,8,512]{2,1,0:T(8,128)S(1)} async-done(((f32[32,8,512]{2,1,0:T(8,128)}), f32[32,8,512]{2,1,0:T(8,128)S(1)}, u32[]{:S(2)}, u32[]{:S(2)}) %all-to-all-start.3) | async-done | bytes 524320 | tf_op jit(solution)/shard_map/all_to_all | solution.py:268
  153.5 5.3 %all-to-all-start.5 = ((f32[32,8,512]{2,1,0:T(8,128)}), f32[32,8,512]{2,1,0:T(8,128)S(1)}, u32[]{:S(2)}, u32[]{:S(2)}) async-start(f32[32,8,512]{2,1,0:T(8,128)} %broadcast_in_dim.36), calls=%async_computation.5 | async-start | bytes 1048576 | tf_op jit(solution)/shard_map/all_to_all | solution.py:268
  160.0 9.9 %factor1.1.refs_1_.refs_7_ = f32[256,1024]{1,0:T(8,128)S(1)} custom-call(s32[1,1]{1,0:T(1,128)} %bitcast.core_ref.refs_0_, f32[768,128]{1,0:T(8,128)S(1)} %bitcast.51, f32[768,128]{1,0:T(8,128)S(1)} %collective-permute-done.16.refs_2_, f32[256,1024]{1,0:T(8,128)S(1)} %copy-done.6), custom_call_target="tpu_custom_call" | custom-call | flops 10737418240 | bytes 4194304 | tf_op jit(solution)/shard_map/factor1/pallas_call | solution.py:48
  170.9 2.8 %all-to-all-done.5 = f32[32,8,512]{2,1,0:T(8,128)S(1)} async-done(((f32[32,8,512]{2,1,0:T(8,128)}), f32[32,8,512]{2,1,0:T(8,128)S(1)}, u32[]{:S(2)}, u32[]{:S(2)}) %all-to-all-start.5) | async-done | bytes 524320 | tf_op jit(solution)/shard_map/all_to_all | solution.py:268
  173.8 5.6 %collective-permute-start.17 = (f32[256,512]{1,0:T(8,128)S(1)}, f32[256,512]{1,0:T(8,128)S(1)}, u32[]{:S(2)}, u32[]{:S(2)}) collective-permute-start(f32[256,512]{1,0:T(8,128)S(1)} %bitcast.47), channel_id=1, source_target_pairs={{0,8},{8,0},{1,9},{9,1},{2,10},{10,2},{3,11},{11,3},{4,12},{12,4},... | collective-permute-start | bytes 1572872 | tf_op jit(solution)/shard_map/ppermute | solution.py:276
  181.8 2.2 %basis.1.refs_3_ = f32[512,512]{1,0:T(8,128)S(1)} custom-call(f32[512,512]{1,0:T(8,128)S(1)} %place_panel.1.panel_ref, f32[256,1024]{1,0:T(8,128)S(1)} %copy-done.7, f32[256,1024]{1,0:T(8,128)S(1)} %copy-done.10), custom_call_target="tpu_custom_call" | custom-call | flops 2147483648 | bytes 4194304 | tf_op jit(solution)/shard_map/basis/pallas_call | solution.py:48
  184.1 3.3 %final.1 = (f32[512,512]{1,0:T(8,128)}, f32[512,512]{1,0:T(8,128)}) custom-call(s32[1,1]{1,0:T(1,128)} %bitcast.core_ref.refs_0_, s32[1,1]{1,0:T(1,128)} %bitcast.1.refs_1_, f32[512,512]{1,0:T(8,128)S(1)} %copy-done.14, f32[512,512]{1,0:T(8,128)S(1)} %basis.1.refs_3_, f32[256,512]{1,0:T(8,128)S(1)} %bitcast.48, ...), custom_call_target="tpu_custom_call" | custom-call | flops 4294967296 | bytes 4194304 | tf_op jit(solution)/shard_map/final/pallas_call | solution.py:48
  (85 shorter events, 38.0 us)
Async XLA Ops:
  10.8 37.7 %all-to-all-start = ((f32[64,8,384]{2,1,0:T(8,128)}), f32[64,8,384]{2,1,0:T(8,128)S(1)}, u32[]{:S(2)}, u32[]{:S(2)}) async-start(f32[64,8,384]{2,1,0:T(8,128)} %bitcast.3), calls=%async_computation | async-start | bytes 1572864 | tf_op jit(solution)/shard_map/all_to_all | solution.py:268
  25.8 10.8 %collective-permute-start = (f32[64,512]{1,0:T(8,128)S(1)}, f32[64,512]{1,0:T(8,128)S(1)}, u32[]{:S(2)}, u32[]{:S(2)}) collective-permute-start(f32[64,512]{1,0:T(8,128)S(1)} %get-tuple-element.32), channel_id=1, source_target_pairs={{0,1},{8,9},{16,17},{24,25},{32,33},{40,41},{48,49},{56,57},{64,65... | collective-permute-start | bytes 393224 | tf_op jit(solution)/shard_map/ppermute | solution.py:292
  29.0 8.9 %collective-permute-start.5 = (f32[64,512]{1,0:T(8,128)S(1)}, f32[64,512]{1,0:T(8,128)S(1)}, u32[]{:S(2)}, u32[]{:S(2)}) collective-permute-start(f32[64,512]{1,0:T(8,128)S(1)} %get-tuple-element.33), channel_id=1, source_target_pairs={{0,6},{8,14},{16,22},{24,30},{32,38},{40,46},{48,54},{56,62},{64,7... | collective-permute-start | bytes 393224 | tf_op jit(solution)/shard_map/ppermute | solution.py:292
  32.4 6.9 %collective-permute-start.4 = (f32[64,512]{1,0:T(8,128)S(1)}, f32[64,512]{1,0:T(8,128)S(1)}, u32[]{:S(2)}, u32[]{:S(2)}) collective-permute-start(f32[64,512]{1,0:T(8,128)S(1)} %get-tuple-element.34), channel_id=1, source_target_pairs={{0,5},{8,13},{16,21},{24,29},{32,37},{40,45},{48,53},{56,61},{64,6... | collective-permute-start | bytes 393224 | tf_op jit(solution)/shard_map/ppermute | solution.py:292
  33.9 5.5 %collective-permute-start.3 = (f32[64,512]{1,0:T(8,128)S(1)}, f32[64,512]{1,0:T(8,128)S(1)}, u32[]{:S(2)}, u32[]{:S(2)}) collective-permute-start(f32[64,512]{1,0:T(8,128)S(1)} %get-tuple-element.35), channel_id=1, source_target_pairs={{0,4},{8,12},{16,20},{24,28},{32,36},{40,44},{48,52},{56,60},{64,6... | collective-permute-start | bytes 393224 | tf_op jit(solution)/shard_map/ppermute | solution.py:292
  35.3 5.2 %collective-permute-start.2 = (f32[64,512]{1,0:T(8,128)S(1)}, f32[64,512]{1,0:T(8,128)S(1)}, u32[]{:S(2)}, u32[]{:S(2)}) collective-permute-start(f32[64,512]{1,0:T(8,128)S(1)} %get-tuple-element.36), channel_id=1, source_target_pairs={{0,3},{8,11},{16,19},{24,27},{32,35},{40,43},{48,51},{56,59},{64,6... | collective-permute-start | bytes 393224 | tf_op jit(solution)/shard_map/ppermute | solution.py:292
  36.7 6.7 %collective-permute-start.1 = (f32[64,512]{1,0:T(8,128)S(1)}, f32[64,512]{1,0:T(8,128)S(1)}, u32[]{:S(2)}, u32[]{:S(2)}) collective-permute-start(f32[64,512]{1,0:T(8,128)S(1)} %get-tuple-element.37), channel_id=1, source_target_pairs={{0,2},{8,10},{16,18},{24,26},{32,34},{40,42},{48,50},{56,58},{64,6... | collective-permute-start | bytes 393224 | tf_op jit(solution)/shard_map/ppermute | solution.py:292
  38.0 5.4 %collective-permute-start.6 = (f32[64,512]{1,0:T(8,128)S(1)}, f32[64,512]{1,0:T(8,128)S(1)}, u32[]{:S(2)}, u32[]{:S(2)}) collective-permute-start(f32[64,512]{1,0:T(8,128)S(1)} %get-tuple-element.38), channel_id=1, source_target_pairs={{0,7},{8,15},{16,23},{24,31},{32,39},{40,47},{48,55},{56,63},{64,7... | collective-permute-start | bytes 393224 | tf_op jit(solution)/shard_map/ppermute | solution.py:292
  51.8 4.2 %collective-permute-start.7 = (f32[768,128]{1,0:T(8,128)S(1)}, f32[768,128]{1,0:T(8,128)S(1)}, u32[]{:S(2)}, u32[]{:S(2)}) collective-permute-start(f32[768,128]{1,0:T(8,128)S(1)} %get-tuple-element.20), channel_id=1, source_target_pairs={{0,8},{8,0},{1,9},{9,1},{2,10},{10,2},{3,11},{11,3},{4,12},{12,4},... | collective-permute-start | bytes 1179656 | tf_op jit(solution)/shard_map/ppermute | solution.py:276
  56.8 19.6 %all-to-all-start.1 = ((f32[32,24,128]{2,1,0:T(8,128)}), f32[32,24,128]{2,1,0:T(8,128)S(1)}, u32[]{:S(2)}, u32[]{:S(2)}) async-start(f32[32,24,128]{2,1,0:T(8,128)} %bitcast.14), calls=%async_computation.1 | async-start | bytes 786432 | tf_op jit(solution)/shard_map/all_to_all | solution.py:268
  62.2 53.0 %all-gather.2.cloned.1.call-start = ((), (), s32[]{:S(2)}) async-start(), calls=%async_computation.6 | async-start | bytes 1179648 | tf_op jit(solution)/shard_map/all_gather | solution.py:315
  62.3 9.6 %collective-permute-start.8 = (f32[128,128]{1,0:T(8,128)S(1)}, f32[128,128]{1,0:T(8,128)S(1)}, u32[]{:S(2)}, u32[]{:S(2)}) collective-permute-start(f32[128,128]{1,0:T(8,128)S(1)} %get-tuple-element.39), channel_id=1, source_target_pairs={{0,1},{8,9},{16,17},{24,25},{32,33},{40,41},{48,49},{56,57},{64,65... | collective-permute-start | bytes 196616 | tf_op jit(solution)/shard_map/ppermute | solution.py:292
  64.9 8.3 %collective-permute-start.14 = (f32[128,128]{1,0:T(8,128)S(1)}, f32[128,128]{1,0:T(8,128)S(1)}, u32[]{:S(2)}, u32[]{:S(2)}) collective-permute-start(f32[128,128]{1,0:T(8,128)S(1)} %get-tuple-element.40), channel_id=1, source_target_pairs={{0,7},{8,15},{16,23},{24,31},{32,39},{40,47},{48,55},{56,63},{64,7... | collective-permute-start | bytes 196616 | tf_op jit(solution)/shard_map/ppermute | solution.py:292
  67.5 7.1 %collective-permute-start.13 = (f32[128,128]{1,0:T(8,128)S(1)}, f32[128,128]{1,0:T(8,128)S(1)}, u32[]{:S(2)}, u32[]{:S(2)}) collective-permute-start(f32[128,128]{1,0:T(8,128)S(1)} %get-tuple-element.41), channel_id=1, source_target_pairs={{0,6},{8,14},{16,22},{24,30},{32,38},{40,46},{48,54},{56,62},{64,7... | collective-permute-start | bytes 196616 | tf_op jit(solution)/shard_map/ppermute | solution.py:292
  68.9 5.7 %collective-permute-start.12 = (f32[128,128]{1,0:T(8,128)S(1)}, f32[128,128]{1,0:T(8,128)S(1)}, u32[]{:S(2)}, u32[]{:S(2)}) collective-permute-start(f32[128,128]{1,0:T(8,128)S(1)} %get-tuple-element.42), channel_id=1, source_target_pairs={{0,5},{8,13},{16,21},{24,29},{32,37},{40,45},{48,53},{56,61},{64,6... | collective-permute-start | bytes 196616 | tf_op jit(solution)/shard_map/ppermute | solution.py:292
  70.4 4.2 %collective-permute-start.11 = (f32[128,128]{1,0:T(8,128)S(1)}, f32[128,128]{1,0:T(8,128)S(1)}, u32[]{:S(2)}, u32[]{:S(2)}) collective-permute-start(f32[128,128]{1,0:T(8,128)S(1)} %get-tuple-element.43), channel_id=1, source_target_pairs={{0,4},{8,12},{16,20},{24,28},{32,36},{40,44},{48,52},{56,60},{64,6... | collective-permute-start | bytes 196616 | tf_op jit(solution)/shard_map/ppermute | solution.py:292
  71.9 3.0 %collective-permute-start.10 = (f32[128,128]{1,0:T(8,128)S(1)}, f32[128,128]{1,0:T(8,128)S(1)}, u32[]{:S(2)}, u32[]{:S(2)}) collective-permute-start(f32[128,128]{1,0:T(8,128)S(1)} %get-tuple-element.44), channel_id=1, source_target_pairs={{0,3},{8,11},{16,19},{24,27},{32,35},{40,43},{48,51},{56,59},{64,6... | collective-permute-start | bytes 196616 | tf_op jit(solution)/shard_map/ppermute | solution.py:292
  73.2 3.2 %collective-permute-start.9 = (f32[128,128]{1,0:T(8,128)S(1)}, f32[128,128]{1,0:T(8,128)S(1)}, u32[]{:S(2)}, u32[]{:S(2)}) collective-permute-start(f32[128,128]{1,0:T(8,128)S(1)} %get-tuple-element.45), channel_id=1, source_target_pairs={{0,2},{8,10},{16,18},{24,26},{32,34},{40,42},{48,50},{56,58},{64,6... | collective-permute-start | bytes 196616 | tf_op jit(solution)/shard_map/ppermute | solution.py:292
  105.7 19.1 %all-to-all-start.4 = ((f32[32,24,128]{2,1,0:T(8,128)}), f32[32,24,128]{2,1,0:T(8,128)S(1)}, u32[]{:S(2)}, u32[]{:S(2)}) async-start(f32[32,24,128]{2,1,0:T(8,128)} %broadcast_in_dim.35), calls=%async_computation.4 | async-start | bytes 786432 | tf_op jit(solution)/shard_map/all_to_all | solution.py:268
  120.0 11.3 %collective-permute-start.15 = (f32[256,512]{1,0:T(8,128)S(1)}, f32[256,512]{1,0:T(8,128)S(1)}, u32[]{:S(2)}, u32[]{:S(2)}) collective-permute-start(f32[256,512]{1,0:T(8,128)S(1)} %get-tuple-element.25), channel_id=1, source_target_pairs={{0,8},{8,0},{1,9},{9,1},{2,10},{10,2},{3,11},{11,3},{4,12},{12,4},... | collective-permute-start | bytes 1572872 | tf_op jit(solution)/shard_map/ppermute | solution.py:276
  124.8 11.5 %collective-permute-start.16 = (f32[768,128]{1,0:T(8,128)S(1)}, f32[768,128]{1,0:T(8,128)S(1)}, u32[]{:S(2)}, u32[]{:S(2)}) collective-permute-start(f32[768,128]{1,0:T(8,128)S(1)} %bitcast.49), channel_id=1, source_target_pairs={{0,8},{8,0},{1,9},{9,1},{2,10},{10,2},{3,11},{11,3},{4,12},{12,4},... | collective-permute-start | bytes 1179656 | tf_op jit(solution)/shard_map/ppermute | solution.py:276
  132.2 20.4 %all-to-all-start.3 = ((f32[32,8,512]{2,1,0:T(8,128)}), f32[32,8,512]{2,1,0:T(8,128)S(1)}, u32[]{:S(2)}, u32[]{:S(2)}) async-start(f32[32,8,512]{2,1,0:T(8,128)} %add_bitcast_fusion), calls=%async_computation.3 | async-start | bytes 1048576 | tf_op jit(solution)/shard_map/all_to_all | solution.py:268
  153.5 20.2 %all-to-all-start.5 = ((f32[32,8,512]{2,1,0:T(8,128)}), f32[32,8,512]{2,1,0:T(8,128)S(1)}, u32[]{:S(2)}, u32[]{:S(2)}) async-start(f32[32,8,512]{2,1,0:T(8,128)} %broadcast_in_dim.36), calls=%async_computation.5 | async-start | bytes 1048576 | tf_op jit(solution)/shard_map/all_to_all | solution.py:268
  173.8 10.3 %collective-permute-start.17 = (f32[256,512]{1,0:T(8,128)S(1)}, f32[256,512]{1,0:T(8,128)S(1)}, u32[]{:S(2)}, u32[]{:S(2)}) collective-permute-start(f32[256,512]{1,0:T(8,128)S(1)} %bitcast.47), channel_id=1, source_target_pairs={{0,8},{8,0},{1,9},{9,1},{2,10},{10,2},{3,11},{11,3},{4,12},{12,4},... | collective-permute-start | bytes 1572872 | tf_op jit(solution)/shard_map/ppermute | solution.py:276
  (16 other events, 37.0 us)
Sparse Core Ops, SparseCore 0:
  74.7 40.3 all-gather.1

commit v4 on v3

--- a/solution.py
+++ b/solution.py
@@ -44,7 +44,7 @@
     return jax.ShapeDtypeStruct(shape, jnp.float32)
 
 
-def call(kernel, out_shape, name, flops, *args, scalars=(), scratch=()):
+def call(kernel, out_shape, name, flops, *args, scalars=(), scratch=(), vmem=14):
     return pl.pallas_call(
         kernel,
         out_shape=out_shape,
@@ -52,7 +52,7 @@
         out_specs=jax.tree.map(lambda _: VMEM, out_shape),
         scratch_shapes=scratch,
         name=name,
-        compiler_params=pltpu.CompilerParams(vmem_limit_bytes=14 << 20),
+        compiler_params=pltpu.CompilerParams(vmem_limit_bytes=vmem << 20),
         cost_estimate=pl.CostEstimate(flops=flops, bytes_accessed=4 << 20, transcendentals=0),
     )(*[s.reshape(1, 1) for s in scalars], *args)
 
@@ -103,32 +103,29 @@
     return total
 
 
-def place_kernel(front_ref, arrived_ref, cols_ref, out_ref, shares_ref):
-    child_width = cols_ref.shape[1]
-    rows = arrived_ref[:, :child_width]
-    targets = arrived_ref[:, child_width : child_width + 1].astype(jnp.int32)
-    out_ref[...] = placed(front_ref[...], rows, targets, cols_ref[...])
-    parts, height = shares_ref.shape[0], shares_ref.shape[1] // 2
-    for k in range(parts):
-        for h in range(2):
-            shares_ref[k, h * height : (h + 1) * height, :] = rows[
-                k * height : (k + 1) * height, h * BLOCK : (h + 1) * BLOCK
-            ]
-
-
-def place_panel_kernel(front_ref, shares_ref, cols_ref, arrived_ref, out_ref):
-    parts, height = shares_ref.shape[0], shares_ref.shape[1] // 2
-    child_width = 2 * BLOCK
-    rows = jnp.concatenate(
-        [
-            jnp.concatenate([shares_ref[k, :height, :], shares_ref[k, height:, :]], axis=1)
-            for k in range(parts)
-        ],
-        axis=0,
-    )
-    cols = jnp.concatenate([cols_ref[0:1, :], cols_ref[1:2, :]], axis=1).astype(jnp.int32)
-    targets = arrived_ref[:, child_width : child_width + 1].astype(jnp.int32)
-    out_ref[...] = placed(front_ref[...], rows, targets, cols)
+def choose_kernel(root_ref, own_ref, *refs):
+    arrived, out_ref = refs[:-1], refs[-1]
+    total = arrived[0][...]
+    for ref in arrived[1:]:
+        total = total + ref[...]
+    out_ref[...] = jnp.where(root_ref[0, 0] == 1, own_ref[...], total)
+
+
+def add_kernel(a_ref, b_ref, out_ref):
+    out_ref[...] = a_ref[...] + b_ref[...]
+
+
+def fold_kernel(x_ref, out_ref):
+    terms = [x_ref[i] for i in range(x_ref.shape[0])]
+    while len(terms) > 1:
+        terms = [a + b for a, b in zip(terms[::2], terms[1::2])]
+    for i in range(out_ref.shape[0]):
+        out_ref[i] = terms[0]
+
+
+def first_kernel(x_ref, out_ref):
+    for i in range(out_ref.shape[0]):
+        out_ref[i] = x_ref[0]
 
 
 def halves(core_ref, whole_ref, keep_ref, send_ref):
@@ -144,11 +141,21 @@
     return (2 * PANELS // BLOCK + 2 * (j - 2) + i - 2) * BLOCK
 
 
-def gram_kernel(core_ref, panel_ref, keep_ref, send_ref, whole_ref):
+def place_kernel(
+    core_ref, front_ref, arrived_ref, cols_ref, out_ref, keep_ref, send_ref, *refs
+):
+    share_refs, whole_ref = refs[:-1], refs[-1]
+    child_width = cols_ref.shape[1]
+    targets = arrived_ref[:, child_width : child_width + 1].astype(jnp.int32)
+    front = placed(front_ref[...], arrived_ref[:, :child_width], targets, cols_ref[...])
+    out_ref[...] = front
+    height = share_refs[0].shape[0]
+    for k, ref in enumerate(share_refs):
+        ref[...] = front[k * height : (k + 1) * height, :]
     half = PANELS // 2
     for first in range(2):
         cols = slice(half * first, PANELS)
-        product = dot(panel_ref[:, half * first : half * (first + 1)], panel_ref[:, cols], 0, 0)
+        product = dot(front[:, half * first : half * (first + 1)], front[:, cols], 0, 0)
         for i in range(2):
             for j in range(2 * first, PANELS // BLOCK):
                 at = gram_place(2 * first + i, j)
@@ -213,30 +220,36 @@
 
     def rows_of(block):
         at = block % per * BLOCK
-        return (*above, out_ref)[block // per], slice(at, at + BLOCK)
+        start = block // per * per * BLOCK
+        return (*above, out_ref)[block // per], slice(at, at + BLOCK), start
 
     for k in range(piece * per, (piece + 1) * per):
-        _, rows = rows_of(k)
+        _, rows, start = rows_of(k)
         low, high = k * BLOCK, n + (k + 1) * BLOCK
         starts = [gram_place(k, j) for j in range(k, n // BLOCK)]
         pad = [jnp.zeros((BLOCK, low), jnp.float32)] if k else []
         work = jnp.concatenate([gram[at : at + BLOCK, :] for at in starts] + pad + [identity], axis=1)
         for upper in range(k):
-            ref, at = rows_of(upper)
-            work = work - dot(ref[at, low : low + BLOCK], ref[at, low:high], 0, 0)
+            ref, at, shift = rows_of(upper)
+            end = min(high, shift + ref.shape[1])
+            factor = dot(ref[at, low - shift : low - shift + BLOCK], ref[at, low - shift : end - shift], 0, 0)
+            if end < high:
+                factor = jnp.concatenate([factor, jnp.zeros((BLOCK, high - end), jnp.float32)], axis=1)
+            work = work - factor
         diagonal = factor_diagonal(jnp.concatenate([work[:, :BLOCK], identity], axis=1))
-        out_ref[rows, low:high] = dot(diagonal[:, BLOCK:], work)
-        out_ref[rows, low : low + BLOCK] = diagonal[:, :BLOCK]
-        if k:
-            out_ref[rows, :low] = jnp.zeros((BLOCK, low), jnp.float32)
-        if high < 2 * n:
-            out_ref[rows, high:] = jnp.zeros((BLOCK, 2 * n - high), jnp.float32)
+        out_ref[rows, low - start : high - start] = dot(diagonal[:, BLOCK:], work)
+        out_ref[rows, low - start : low - start + BLOCK] = diagonal[:, :BLOCK]
+        if low > start:
+            out_ref[rows, : low - start] = jnp.zeros((BLOCK, low - start), jnp.float32)
+        if high - start < out_ref.shape[1]:
+            out_ref[rows, high - start :] = jnp.zeros((BLOCK, out_ref.shape[1] - high + start), jnp.float32)
 
 
 def inverse_rows(blocks, i):
     per = blocks[0].shape[0]
     ref, at = blocks[i * BLOCK // per], i * BLOCK % per
-    return ref[at : at + BLOCK, PANELS : PANELS + (i + 1) * BLOCK]
+    left = PANELS - i * BLOCK // per * per
+    return ref[at : at + BLOCK, left : left + (i + 1) * BLOCK]
 
 
 def basis_kernel(panel_ref, *refs):
@@ -260,7 +273,16 @@
     update = dot_fast(basis_mid, coupled_hi) + dot_fast(basis_hi, coupled_mid)
     update = update + dot_fast(basis_hi, coupled_hi)
     out_ref[...] = jnp.where(is_root, basis * root_rows, front_ref[...] - update)
-    upper = jnp.concatenate([ref[:, :PANELS] for ref in blocks], axis=0)
+    per = PANELS // PIECES
+    upper = jnp.concatenate(
+        [
+            jnp.concatenate(
+                ([jnp.zeros((per, at), jnp.float32)] if at else []) + [ref[:, : PANELS - at]], axis=1
+            )
+            for ref, at in zip(blocks, range(0, PANELS, per))
+        ],
+        axis=0,
+    )
     factor_ref[...] = jnp.where(is_root, upper, coupled) * (1.0 / root_rows)
 
 
@@ -268,34 +290,30 @@
     return lax.all_to_all(blocks, axis, split_axis=0, concat_axis=0, tiled=True)
 
 
-def repeated(x, n):
-    return jnp.broadcast_to(x[None], (n,) + x.shape)
-
-
 def swapped(x):
     return lax.ppermute(x, "core", [(0, 1), (1, 0)])
 
 
-def chip_share(x):
-    n = lax.axis_size(("z", "x"))
-    return jnp.sum(exchange(x.reshape(n, x.shape[0] // n, x.shape[1]), ("z", "x")), axis=0)
-
-
-def all_shares(x):
-    n = lax.axis_size(("z", "x"))
-    return exchange(repeated(x, n), ("z", "x")).reshape(n * x.shape[0], x.shape[1])
-
-
-def share_of_root(shares):
-    mine = jnp.where(lax.axis_index("col") == 0, shares[0], 0.0)
-    for k in range(1, lax.axis_size("col")):
-        mine = mine + lax.ppermute(shares[k], "col", [(0, k)])
-    return mine
+def summed(a, b):
+    return call(add_kernel, f32(*a.shape), "add", 1 << 20, a, b, vmem=4)
+
+
+def split_rows(x, n):
+    return x.reshape(n, x.shape[0] // n, x.shape[1])
+
+
+def merge_rows(x):
+    return x.reshape(x.shape[0] * x.shape[1], x.shape[2])
+
+
+def folded(x, n):
+    return call(fold_kernel, f32(n, *x.shape[1:]), "fold", 1 << 20, x, vmem=6)
 
 
 def on_device(front_in, child_block, child_rows, live_counts, column_map):
     rows_dev, cols_dev = front_in.shape
     owners, parts = lax.axis_size(ROW), lax.axis_size("col")
+    chips = lax.axis_size(("z", "x"))
     count, child_width = child_block.shape
     capacity = count // owners
     core = lax.axis_index("core").astype(jnp.int32)
@@ -308,60 +326,48 @@
         f32(count, child_width + BLOCK), "pack", 1 << 20,
         child_block, child_rows.reshape(count // BLOCK, BLOCK), live_counts,
     )
-    arrived = exchange(sent.reshape(owners, capacity, child_width + BLOCK), ROW)
-    arrived = arrived.reshape(count, child_width + BLOCK)
-    front_share = share_of_root(front_in.reshape(parts, rows_dev // parts, cols_dev))
-    arrived, front_share = lax.optimization_barrier((arrived, front_share))
-    panel_front = lax.all_gather(front_share, "col", tiled=True)
-
-    front, shares = call(
-        place_kernel, (f32(rows_dev, cols_dev), f32(parts, 2 * count // parts, BLOCK)),
-        "place", 2 << 30, front_in, arrived, local_cols.reshape(1, child_width),
-    )
-    keep, send = call(
-        gram_kernel, halved, "gram", 2 << 30, front, scalars=(core,),
+    arrived = merge_rows(exchange(sent.reshape(owners, capacity, child_width + BLOCK), ROW))
+
+    share = f32(rows_dev // parts, cols_dev)
+    front, keep, send, *shares = call(
+        place_kernel, [f32(rows_dev, cols_dev), *halved] + [share] * parts,
+        "place", 4 << 30, front_in, arrived, local_cols.reshape(1, child_width), scalars=(core,),
         scratch=[pltpu.VMEM((3 * PANELS, BLOCK), jnp.float32)],
     )
-    half, shares = lax.optimization_barrier((keep + swapped(send), shares))
-    gram_share = chip_share(half)
-
-    rows_of_share = 2 * count // parts
-    to_all = jnp.concatenate(
-        [
-            share_of_root(shares),
-            gram_share,
-            local_cols.astype(jnp.float32).reshape(child_width // BLOCK, BLOCK),
-            jnp.zeros((8 - child_width // BLOCK, BLOCK), jnp.float32),
-        ],
-        axis=0,
-    )
-    from_all = exchange(repeated(to_all, parts), "col")
-    gram_end = rows_of_share + gram_share.shape[0]
-    own_gram = all_shares(from_all[0, rows_of_share:gram_end])
+    sent_shares = [lax.ppermute(shares[k], "col", [(0, k)]) for k in range(1, parts)]
+    panel_share = call(
+        choose_kernel, share, "choose", 1 << 20, shares[0], *sent_shares, scalars=(is_root,), vmem=4
+    )
+    panel = lax.all_gather(panel_share, "col", tiled=True)
+
+    half = summed(keep, swapped(send))
+    gram_share = folded(exchange(split_rows(half, chips), ("z", "x")), parts)
+    gram_share = exchange(gram_share, "col")
+    gram_share = call(
+        first_kernel, f32(chips, *gram_share.shape[1:]), "first", 1 << 20, gram_share, vmem=4
+    )
+    own_gram = merge_rows(exchange(gram_share, ("z", "x")))
     other_gram = swapped(own_gram)
 
-    panel = call(
-        place_panel_kernel, f32(rows_dev, PANELS), "place_panel", 2 << 30,
-        panel_front, from_all[:, :rows_of_share], from_all[0, gram_end:], arrived,
-    )
     keep, send = call(
         product_kernel, (f32(PANELS // 2, cols_dev),) * 2, "products", 2 << 30, panel, front,
         scalars=(core,), scratch=[pltpu.VMEM((PANELS, cols_dev), jnp.float32)],
     )
-    sums_share = chip_share(keep + swapped(send))
+    half = summed(keep, swapped(send))
+    sums_share = folded(exchange(split_rows(half, chips), ("z", "x")), chips)
 
     blocks = []
     for piece in range(PIECES):
         blocks.append(
             call(
                 lambda *refs, piece=piece: factor_kernel(piece, *refs),
-                f32(PANELS // PIECES, 2 * PANELS), f"factor{piece}", 10 << 30,
+                f32(PANELS // PIECES, 3 * PANELS // 2), f"factor{piece}", 10 << 30,
                 own_gram, other_gram, *blocks, scalars=(core,),
             )
         )
         if piece == 0:
             sums_share, blocks[0] = lax.optimization_barrier((sums_share, blocks[0]))
-            own_sums = all_shares(sums_share)
+            own_sums = merge_rows(exchange(sums_share, ("z", "x")))
     own_sums, blocks[1] = lax.optimization_barrier((own_sums, blocks[1]))
     other_sums = swapped(own_sums)
     basis = call(basis_kernel, f32(rows_dev, PANELS), "basis", 2 << 30, panel, *blocks)

time: 195 us -> 196 us (level)
  waiting for transfers between devices: 24.6 us -> 43.1 us
  starting transfers between devices: 80.6 us -> 64.3 us
  other arithmetic: 2.61 us -> 0.01 us
  blocking collectives: 28.4 us -> 30.8 us
    all_to_all x5 -> x4, waiting for transfers between devices: 13.8 us -> 36.9 us  [exchange(): return lax.all_to_all(blocks, axis, split_axis=0, concat_axis=0, tiled=True)]
    ppermute x14 -> x7, starting transfers between devices: 25.5 us -> 13.3 us  [on_device(): lax.ppermute(shares[k], 'col', [(0, k)])]
    all_to_all x5 -> x4, starting transfers between devices: 35.3 us -> 29.5 us  [exchange(): return lax.all_to_all(blocks, axis, split_axis=0, concat_axis=0, tiled=True)]
    all_gather x1, waiting for transfers between devices: 3.72 us -> 0.02 us  [on_device(): panel = lax.all_gather(panel_share, 'col', tiled=True)]
    all_to_all x1 -> x2, blocking collectives: 28.4 us -> 30.8 us  [exchange(): return lax.all_to_all(blocks, axis, split_axis=0, concat_axis=0, tiled=True)]
    pallas_call x9 -> x13, Pallas kernels: 32.3 us -> 33.4 us  [call(): pl.pallas_call(kernel, out_shape=out_shape, in_specs=[SMEM] * len(scalars...]
    ppermute x14 -> x7, waiting for transfers between devices: 5.78 us -> 4.78 us  [on_device(): lax.ppermute(shares[k], 'col', [(0, k)])]
    unnamed x32 -> x34, local copies, waits for them, and re-layouts: 9.26 us -> 9.52 us
  transfers between devices with their start and end apart: 24 -> 16, of which waited for: 9 -> 8; matrix products, arithmetic and copies ran while one was open for 1% -> 0% of each run, Pallas kernels for 13% -> 12%
where the time goes in v4:
time: 196 us; the launch traced here: 195 us
  starting transfers between devices  64.3 us (33%)
  waiting for transfers between devices  43.1 us (22%)
  Pallas kernels  33.4 us (17%)
  blocking collectives  30.8 us (16%)
  between operations  14.4 us (7%)
  local copies, waits for them, and re-layouts  9.52 us (5%)
    all_to_all x4, waiting for transfers between devices, exchange(): return lax.all_to_all(blocks, axis, split_axis=0, concat_axis=0, tiled=True)  36.9 us
    pallas_call x13, Pallas kernels, call(): pl.pallas_call(kernel, out_shape=out_shape, in_specs=[SMEM] * len(scalars...  33.4 us
    all_to_all x2, blocking collectives, exchange(): return lax.all_to_all(blocks, axis, split_axis=0, concat_axis=0, tiled=True)  30.8 us
    all_to_all x4, starting transfers between devices, exchange(): return lax.all_to_all(blocks, axis, split_axis=0, concat_axis=0, tiled=True)  29.5 us
    ppermute x4, starting transfers between devices, swapped(): return lax.ppermute(x, 'core', [(0, 1), (1, 0)])  21.4 us
    ppermute x7, starting transfers between devices, on_device(): lax.ppermute(shares[k], 'col', [(0, k)])  13.3 us
    unnamed x34, local copies, waits for them, and re-layouts  9.52 us
    ppermute x7, waiting for transfers between devices, on_device(): lax.ppermute(shares[k], 'col', [(0, k)])  4.78 us
  transfers between devices with their start and end apart: 16, of which 8 were waited for; matrix products, arithmetic and copies ran while one was open for 0% of the time, Pallas kernels for 12%

profile of v4, /device:TPU:1, one launch (start us, length us, event | category | flops | bytes accessed | tf_op | source)
XLA Modules:
  0.0 195.4 jit_solution(5546006607585086608)
XLA Ops:
  10.8 15.0 %all-to-all-start = ((f32[64,8,384]{2,1,0:T(8,128)}), f32[64,8,384]{2,1,0:T(8,128)S(1)}, u32[]{:S(2)}, u32[]{:S(2)}) async-start(f32[64,8,384]{2,1,0:T(8,128)} %bitcast.3), calls=%async_computation | async-start | bytes 1572864 | tf_op jit(solution)/shard_map/all_to_all | solution.py:290
  26.5 22.0 %all-to-all-done = f32[64,8,384]{2,1,0:T(8,128)S(1)} async-done(((f32[64,8,384]{2,1,0:T(8,128)}), f32[64,8,384]{2,1,0:T(8,128)S(1)}, u32[]{:S(2)}, u32[]{:S(2)}) %all-to-all-start) | async-done | bytes 786464 | tf_op jit(solution)/shard_map/all_to_all | solution.py:290
  48.5 3.1 %place.1 = (f32[512,512]{1,0:T(8,128)S(1)}, f32[768,128]{1,0:T(8,128)S(1)}, f32[768,128]{1,0:T(8,128)S(1)}, f32[64,512]{1,0:T(8,128)S(1)}, f32[64,512]{1,0:T(8,1...) custom-call(s32[1,1]{1,0:T(1,128)} %bitcast.core_ref.refs_0_, ...), custom_call_target="tpu_custom_call" | custom-call | flops 4294967296 | bytes 4194304 | tf_op jit(solution)/shard_map/place/pallas_call | solution.py:48
  52.5 3.2 %collective-permute-start = (f32[64,512]{1,0:T(8,128)S(1)}, f32[64,512]{1,0:T(8,128)S(1)}, u32[]{:S(2)}, u32[]{:S(2)}) collective-permute-start(f32[64,512]{1,0:T(8,128)S(1)} %get-tuple-element.21), channel_id=1, source_target_pairs={{0,1},{8,9},{16,17},{24,25},{32,33},{40,41},{48,49},{56,57},{64,65... | collective-permute-start | bytes 393224 | tf_op jit(solution)/shard_map/ppermute | solution.py:337
  55.8 1.7 collective-permute-start.1
  59.1 2.9 %collective-permute-start.3 = (f32[64,512]{1,0:T(8,128)S(1)}, f32[64,512]{1,0:T(8,128)S(1)}, u32[]{:S(2)}, u32[]{:S(2)}) collective-permute-start(f32[64,512]{1,0:T(8,128)S(1)} %get-tuple-element.24), channel_id=1, source_target_pairs={{0,4},{8,12},{16,20},{24,28},{32,36},{40,44},{48,52},{56,60},{64,6... | collective-permute-start | bytes 393224 | tf_op jit(solution)/shard_map/ppermute | solution.py:337
  68.0 2.8 %collective-permute-done.6.refs_6_ = f32[64,512]{1,0:T(8,128)S(1)} collective-permute-done((f32[64,512]{1,0:T(8,128)S(1)}, f32[64,512]{1,0:T(8,128)S(1)}, u32[]{:S(2)}, u32[]{:S(2)}) %collective-permute-start.6) | collective-permute-done | bytes 131104 | tf_op jit(solution)/shard_map/ppermute | solution.py:337
  71.5 3.8 %collective-permute-start.8 = (f32[768,128]{1,0:T(8,128)S(1)}, f32[768,128]{1,0:T(8,128)S(1)}, u32[]{:S(2)}, u32[]{:S(2)}) collective-permute-start(f32[768,128]{1,0:T(8,128)S(1)} %get-tuple-element.31), channel_id=1, source_target_pairs={{0,8},{8,0},{1,9},{9,1},{2,10},{10,2},{3,11},{11,3},{4,12},{12,4},... | collective-permute-start | bytes 1179656 | tf_op jit(solution)/shard_map/ppermute | solution.py:294
  76.7 18.6 %all_to_all.30.x_ref = f32[32,24,128]{2,1,0:T(8,128)S(1)} all-to-all(f32[32,24,128]{2,1,0:T(8,128)S(1)} %bitcast.10), channel_id=1, replica_groups=mesh['z'=8,'x'=4,'core'=2,'col'=8] {'z','x'}, dimensions={0} | all-to-all | bytes 786432 | tf_op jit(solution)/shard_map/all_to_all | solution.py:290
  95.2 12.2 %all_to_all.31.x_ref = f32[8,24,128]{2,1,0:T(8,128)S(1)} all-to-all(f32[8,24,128]{2,1,0:T(8,128)S(1)} %fold.3), channel_id=1, replica_groups=mesh['z'=8,'x'=4,'core'=2,'col'=8] {'col'}, dimensions={0} | all-to-all | bytes 196608 | tf_op jit(solution)/shard_map/all_to_all | solution.py:290
  108.3 5.6 %all-to-all-start.4 = ((f32[32,24,128]{2,1,0:T(8,128)}), f32[32,24,128]{2,1,0:T(8,128)S(1)}, u32[]{:S(2)}, u32[]{:S(2)}) async-start(f32[32,24,128]{2,1,0:T(8,128)} %first.1), calls=%async_computation.4 | async-start | bytes 786432 | tf_op jit(solution)/shard_map/all_to_all | solution.py:290
  115.1 1.9 products.1
  117.0 5.2 %collective-permute-start.7 = (f32[256,512]{1,0:T(8,128)S(1)}, f32[256,512]{1,0:T(8,128)S(1)}, u32[]{:S(2)}, u32[]{:S(2)}) collective-permute-start(f32[256,512]{1,0:T(8,128)S(1)} %get-tuple-element.29), channel_id=1, source_target_pairs={{0,8},{8,0},{1,9},{9,1},{2,10},{10,2},{3,11},{11,3},{4,12},{12,4},... | collective-permute-start | bytes 1572872 | tf_op jit(solution)/shard_map/ppermute | solution.py:294
  122.2 3.1 %all-to-all-done.4 = f32[32,24,128]{2,1,0:T(8,128)S(1)} async-done(((f32[32,24,128]{2,1,0:T(8,128)}), f32[32,24,128]{2,1,0:T(8,128)S(1)}, u32[]{:S(2)}, u32[]{:S(2)}) %all-to-all-start.4) | async-done | bytes 393248 | tf_op jit(solution)/shard_map/all_to_all | solution.py:290
  125.3 7.2 %collective-permute-start.9 = (f32[768,128]{1,0:T(8,128)S(1)}, f32[768,128]{1,0:T(8,128)S(1)}, u32[]{:S(2)}, u32[]{:S(2)}) collective-permute-start(f32[768,128]{1,0:T(8,128)S(1)} %bitcast.14), channel_id=1, source_target_pairs={{0,8},{8,0},{1,9},{9,1},{2,10},{10,2},{3,11},{11,3},{4,12},{12,4},... | collective-permute-start | bytes 1179656 | tf_op jit(solution)/shard_map/ppermute | solution.py:294
  133.3 4.1 %all-to-all-start.1 = ((f32[32,8,512]{2,1,0:T(8,128)}), f32[32,8,512]{2,1,0:T(8,128)S(1)}, u32[]{:S(2)}, u32[]{:S(2)}) async-start(f32[32,8,512]{2,1,0:T(8,128)} %bitcast.6), calls=%async_computation.1 | async-start | bytes 1048576 | tf_op jit(solution)/shard_map/all_to_all | solution.py:290
  137.4 8.8 %factor0.1.refs_3_.refs_0_.refs_6_ = f32[256,768]{1,0:T(8,128)S(1)} custom-call(s32[1,1]{1,0:T(1,128)} %bitcast.core_ref.refs_0_, f32[768,128]{1,0:T(8,128)S(1)} %bitcast.15, f32[768,128]{1,0:T(8,128)S(1)} %collective-permute-done.9.refs_2_), custom_call_target="tpu_custom_call" | custom-call | flops 10737418240 | bytes 4194304 | tf_op jit(solution)/shard_map/factor0/pallas_call | solution.py:48
  146.2 8.2 %all-to-all-done.1.x_ref = f32[32,8,512]{2,1,0:T(8,128)S(1)} async-done(((f32[32,8,512]{2,1,0:T(8,128)}), f32[32,8,512]{2,1,0:T(8,128)S(1)}, u32[]{:S(2)}, u32[]{:S(2)}) %all-to-all-start.1) | async-done | bytes 524320 | tf_op jit(solution)/shard_map/all_to_all | solution.py:290
  155.3 4.9 %all-to-all-start.5 = ((f32[32,8,512]{2,1,0:T(8,128)}), f32[32,8,512]{2,1,0:T(8,128)S(1)}, u32[]{:S(2)}, u32[]{:S(2)}) async-start(f32[32,8,512]{2,1,0:T(8,128)} %fold.2), calls=%async_computation.5 | async-start | bytes 1048576 | tf_op jit(solution)/shard_map/all_to_all | solution.py:290
  161.4 9.5 %factor1.1.refs_1_.refs_7_ = f32[256,768]{1,0:T(8,128)S(1)} custom-call(s32[1,1]{1,0:T(1,128)} %bitcast.core_ref.refs_0_, f32[768,128]{1,0:T(8,128)S(1)} %bitcast.16, f32[768,128]{1,0:T(8,128)S(1)} %collective-permute-done.9.refs_2_, f32[256,768]{1,0:T(8,128)S(1)} %copy-done.7), custom_call_target="tpu_custom_call" | custom-call | flops 10737418240 | bytes 4194304 | tf_op jit(solution)/shard_map/factor1/pallas_call | solution.py:48
  171.8 3.6 %all-to-all-done.5 = f32[32,8,512]{2,1,0:T(8,128)S(1)} async-done(((f32[32,8,512]{2,1,0:T(8,128)}), f32[32,8,512]{2,1,0:T(8,128)S(1)}, u32[]{:S(2)}, u32[]{:S(2)}) %all-to-all-start.5) | async-done | bytes 524320 | tf_op jit(solution)/shard_map/all_to_all | solution.py:290
  175.4 5.3 %collective-permute-start.10 = (f32[256,512]{1,0:T(8,128)S(1)}, f32[256,512]{1,0:T(8,128)S(1)}, u32[]{:S(2)}, u32[]{:S(2)}) collective-permute-start(f32[256,512]{1,0:T(8,128)S(1)} %bitcast.12), channel_id=1, source_target_pairs={{0,8},{8,0},{1,9},{9,1},{2,10},{10,2},{3,11},{11,3},{4,12},{12,4},... | collective-permute-start | bytes 1572872 | tf_op jit(solution)/shard_map/ppermute | solution.py:294
  183.0 2.2 %basis.1.refs_3_ = f32[512,512]{1,0:T(8,128)S(1)} custom-call(f32[512,512]{1,0:T(8,128)S(1)} %copy-done.5, f32[256,768]{1,0:T(8,128)S(1)} %copy-done.8, f32[256,768]{1,0:T(8,128)S(1)} %copy-done.11), custom_call_target="tpu_custom_call" | custom-call | flops 2147483648 | bytes 4194304 | tf_op jit(solution)/shard_map/basis/pallas_call | solution.py:48
  185.2 3.4 %final.1 = (f32[512,512]{1,0:T(8,128)}, f32[512,512]{1,0:T(8,128)}) custom-call(s32[1,1]{1,0:T(1,128)} %bitcast.core_ref.refs_0_, s32[1,1]{1,0:T(1,128)} %bitcast.1.root_ref.refs_1_, f32[512,512]{1,0:T(8,128)S(1)} %copy-done.15, f32[512,512]{1,0:T(8,128)S(1)} %basis.1.refs_3_, f32[256,512]{1,0:T(8,128)S(1)} %bitcast.13, ...), custom_call_target="tpu_custom_call" | custom-call | flops 4294967296 | bytes 4194304 | tf_op jit(solution)/shard_map/final/pallas_call | solution.py:48
  (59 shorter events, 23.0 us)
Async XLA Ops:
  10.7 37.7 %copy-start.3 = (f32[512,512]{1,0:T(8,128)S(1)}, f32[512,512]{1,0:T(8,128)}, u32[]{:S(2)}) copy-start(f32[512,512]{1,0:T(8,128)} %front_ref.1) | copy-start | bytes 3145732
  10.8 37.7 %all-to-all-start = ((f32[64,8,384]{2,1,0:T(8,128)}), f32[64,8,384]{2,1,0:T(8,128)S(1)}, u32[]{:S(2)}, u32[]{:S(2)}) async-start(f32[64,8,384]{2,1,0:T(8,128)} %bitcast.3), calls=%async_computation | async-start | bytes 1572864 | tf_op jit(solution)/shard_map/all_to_all | solution.py:290
  25.7 88.1 %all-gather.2.cloned.1.call-start = ((), (), s32[]{:S(2)}) async-start(), calls=%async_computation.6 | async-start | bytes 1179648 | tf_op jit(solution)/shard_map/all_gather | solution.py:341
  52.5 10.8 %collective-permute-start = (f32[64,512]{1,0:T(8,128)S(1)}, f32[64,512]{1,0:T(8,128)S(1)}, u32[]{:S(2)}, u32[]{:S(2)}) collective-permute-start(f32[64,512]{1,0:T(8,128)S(1)} %get-tuple-element.21), channel_id=1, source_target_pairs={{0,1},{8,9},{16,17},{24,25},{32,33},{40,41},{48,49},{56,57},{64,65... | collective-permute-start | bytes 393224 | tf_op jit(solution)/shard_map/ppermute | solution.py:337
  55.8 8.9 %collective-permute-start.1 = (f32[64,512]{1,0:T(8,128)S(1)}, f32[64,512]{1,0:T(8,128)S(1)}, u32[]{:S(2)}, u32[]{:S(2)}) collective-permute-start(f32[64,512]{1,0:T(8,128)S(1)} %get-tuple-element.22), channel_id=1, source_target_pairs={{0,2},{8,10},{16,18},{24,26},{32,34},{40,42},{48,50},{56,58},{64,6... | collective-permute-start | bytes 393224 | tf_op jit(solution)/shard_map/ppermute | solution.py:337
  57.4 8.5 %collective-permute-start.2 = (f32[64,512]{1,0:T(8,128)S(1)}, f32[64,512]{1,0:T(8,128)S(1)}, u32[]{:S(2)}, u32[]{:S(2)}) collective-permute-start(f32[64,512]{1,0:T(8,128)S(1)} %get-tuple-element.23), channel_id=1, source_target_pairs={{0,3},{8,11},{16,19},{24,27},{32,35},{40,43},{48,51},{56,59},{64,6... | collective-permute-start | bytes 393224 | tf_op jit(solution)/shard_map/ppermute | solution.py:337
  59.1 7.2 %collective-permute-start.3 = (f32[64,512]{1,0:T(8,128)S(1)}, f32[64,512]{1,0:T(8,128)S(1)}, u32[]{:S(2)}, u32[]{:S(2)}) collective-permute-start(f32[64,512]{1,0:T(8,128)S(1)} %get-tuple-element.24), channel_id=1, source_target_pairs={{0,4},{8,12},{16,20},{24,28},{32,36},{40,44},{48,52},{56,60},{64,6... | collective-permute-start | bytes 393224 | tf_op jit(solution)/shard_map/ppermute | solution.py:337
  62.0 4.3 %collective-permute-start.4 = (f32[64,512]{1,0:T(8,128)S(1)}, f32[64,512]{1,0:T(8,128)S(1)}, u32[]{:S(2)}, u32[]{:S(2)}) collective-permute-start(f32[64,512]{1,0:T(8,128)S(1)} %get-tuple-element.25), channel_id=1, source_target_pairs={{0,5},{8,13},{16,21},{24,29},{32,37},{40,45},{48,53},{56,61},{64,6... | collective-permute-start | bytes 393224 | tf_op jit(solution)/shard_map/ppermute | solution.py:337
  63.4 4.6 %collective-permute-start.5 = (f32[64,512]{1,0:T(8,128)S(1)}, f32[64,512]{1,0:T(8,128)S(1)}, u32[]{:S(2)}, u32[]{:S(2)}) collective-permute-start(f32[64,512]{1,0:T(8,128)S(1)} %get-tuple-element.26), channel_id=1, source_target_pairs={{0,6},{8,14},{16,22},{24,30},{32,38},{40,46},{48,54},{56,62},{64,7... | collective-permute-start | bytes 393224 | tf_op jit(solution)/shard_map/ppermute | solution.py:337
  64.7 6.1 %collective-permute-start.6 = (f32[64,512]{1,0:T(8,128)S(1)}, f32[64,512]{1,0:T(8,128)S(1)}, u32[]{:S(2)}, u32[]{:S(2)}) collective-permute-start(f32[64,512]{1,0:T(8,128)S(1)} %get-tuple-element.27), channel_id=1, source_target_pairs={{0,7},{8,15},{16,23},{24,31},{32,39},{40,47},{48,55},{56,63},{64,7... | collective-permute-start | bytes 393224 | tf_op jit(solution)/shard_map/ppermute | solution.py:337
  71.5 5.1 %collective-permute-start.8 = (f32[768,128]{1,0:T(8,128)S(1)}, f32[768,128]{1,0:T(8,128)S(1)}, u32[]{:S(2)}, u32[]{:S(2)}) collective-permute-start(f32[768,128]{1,0:T(8,128)S(1)} %get-tuple-element.31), channel_id=1, source_target_pairs={{0,8},{8,0},{1,9},{9,1},{2,10},{10,2},{3,11},{11,3},{4,12},{12,4},... | collective-permute-start | bytes 1179656 | tf_op jit(solution)/shard_map/ppermute | solution.py:294
  95.2 18.6 %copy-start.14 = (f32[512,512]{1,0:T(8,128)S(1)}, f32[512,512]{1,0:T(8,128)}, u32[]{:S(2)}) copy-start(f32[512,512]{1,0:T(8,128)} %copy-done.13) | copy-start | bytes 3145732
  108.3 17.0 %all-to-all-start.4 = ((f32[32,24,128]{2,1,0:T(8,128)}), f32[32,24,128]{2,1,0:T(8,128)S(1)}, u32[]{:S(2)}, u32[]{:S(2)}) async-start(f32[32,24,128]{2,1,0:T(8,128)} %first.1), calls=%async_computation.4 | async-start | bytes 786432 | tf_op jit(solution)/shard_map/all_to_all | solution.py:290
  113.9 1.2 copy-start.4
  117.0 15.5 %collective-permute-start.7 = (f32[256,512]{1,0:T(8,128)S(1)}, f32[256,512]{1,0:T(8,128)S(1)}, u32[]{:S(2)}, u32[]{:S(2)}) collective-permute-start(f32[256,512]{1,0:T(8,128)S(1)} %get-tuple-element.29), channel_id=1, source_target_pairs={{0,8},{8,0},{1,9},{9,1},{2,10},{10,2},{3,11},{11,3},{4,12},{12,4},... | collective-permute-start | bytes 1572872 | tf_op jit(solution)/shard_map/ppermute | solution.py:294
  125.3 12.1 %collective-permute-start.9 = (f32[768,128]{1,0:T(8,128)S(1)}, f32[768,128]{1,0:T(8,128)S(1)}, u32[]{:S(2)}, u32[]{:S(2)}) collective-permute-start(f32[768,128]{1,0:T(8,128)S(1)} %bitcast.14), channel_id=1, source_target_pairs={{0,8},{8,0},{1,9},{9,1},{2,10},{10,2},{3,11},{11,3},{4,12},{12,4},... | collective-permute-start | bytes 1179656 | tf_op jit(solution)/shard_map/ppermute | solution.py:294
  133.3 21.1 %all-to-all-start.1 = ((f32[32,8,512]{2,1,0:T(8,128)}), f32[32,8,512]{2,1,0:T(8,128)S(1)}, u32[]{:S(2)}, u32[]{:S(2)}) async-start(f32[32,8,512]{2,1,0:T(8,128)} %bitcast.6), calls=%async_computation.1 | async-start | bytes 1048576 | tf_op jit(solution)/shard_map/all_to_all | solution.py:290
  146.2 9.1 %copy-start.6 = (f32[256,768]{1,0:T(8,128)}, f32[256,768]{1,0:T(8,128)S(1)}, u32[]{:S(2)}) copy-start(f32[256,768]{1,0:T(8,128)S(1)} %factor0.1.refs_3_.refs_0_.refs_6_) | copy-start | bytes 2359300
  155.3 20.0 %all-to-all-start.5 = ((f32[32,8,512]{2,1,0:T(8,128)}), f32[32,8,512]{2,1,0:T(8,128)S(1)}, u32[]{:S(2)}, u32[]{:S(2)}) async-start(f32[32,8,512]{2,1,0:T(8,128)} %fold.2), calls=%async_computation.5 | async-start | bytes 1048576 | tf_op jit(solution)/shard_map/all_to_all | solution.py:290
  161.4 19.3 %copy-start.5 = (f32[512,512]{1,0:T(8,128)S(1)}, f32[512,512]{1,0:T(8,128)}, u32[]{:S(2)}) copy-start(f32[512,512]{1,0:T(8,128)} %all-gather.2.cloned.1.call-done.panel_ref) | copy-start | bytes 3145732
  175.4 9.8 %collective-permute-start.10 = (f32[256,512]{1,0:T(8,128)S(1)}, f32[256,512]{1,0:T(8,128)S(1)}, u32[]{:S(2)}, u32[]{:S(2)}) collective-permute-start(f32[256,512]{1,0:T(8,128)S(1)} %bitcast.12), channel_id=1, source_target_pairs={{0,8},{8,0},{1,9},{9,1},{2,10},{10,2},{3,11},{11,3},{4,12},{12,4},... | collective-permute-start | bytes 1572872 | tf_op jit(solution)/shard_map/ppermute | solution.py:294
  182.9 2.2 %copy-start.9 = (f32[256,768]{1,0:T(8,128)S(1)}, f32[256,768]{1,0:T(8,128)}, u32[]{:S(2)}) copy-start(f32[256,768]{1,0:T(8,128)} %copy-done.6) | copy-start | bytes 2359300
  182.9 2.3 %copy-start.12 = (f32[256,768]{1,0:T(8,128)S(1)}, f32[256,768]{1,0:T(8,128)}, u32[]{:S(2)}) copy-start(f32[256,768]{1,0:T(8,128)} %copy-done.10) | copy-start | bytes 2359300
  182.9 2.3 %copy-start.15 = (f32[512,512]{1,0:T(8,128)S(1)}, f32[512,512]{1,0:T(8,128)}, u32[]{:S(2)}) copy-start(f32[512,512]{1,0:T(8,128)} %copy-done.13) | copy-start | bytes 3145732
  (9 other events, 8.3 us)
Sparse Core Ops, SparseCore 0:
  71.6 32.5 all-gather.1

commit v5 on v4

--- a/solution.py
+++ b/solution.py
@@ -14,6 +14,7 @@
 ROW = ("z", "x", "core")
 VMEM = pl.BlockSpec(memory_space=pltpu.VMEM)
 SMEM = pl.BlockSpec(memory_space=pltpu.SMEM)
+HBM = pl.BlockSpec(memory_space=pltpu.MemorySpace.HBM)
 
 
 def dot_fast(a, b, ca=1, cb=0):
@@ -44,12 +45,14 @@
     return jax.ShapeDtypeStruct(shape, jnp.float32)
 
 
-def call(kernel, out_shape, name, flops, *args, scalars=(), scratch=(), vmem=14):
+def call(
+    kernel, out_shape, name, flops, *args, scalars=(), scratch=(), vmem=14, ins=None, outs=None
+):
     return pl.pallas_call(
         kernel,
         out_shape=out_shape,
-        in_specs=[SMEM] * len(scalars) + [VMEM] * len(args),
-        out_specs=jax.tree.map(lambda _: VMEM, out_shape),
+        in_specs=[SMEM] * len(scalars) + (ins or [VMEM] * len(args)),
+        out_specs=outs or jax.tree.map(lambda _: VMEM, out_shape),
         scratch_shapes=scratch,
         name=name,
         compiler_params=pltpu.CompilerParams(vmem_limit_bytes=vmem << 20),
@@ -69,11 +72,19 @@
     return (iota((size, size), 0) == iota((size, size), 1)).astype(jnp.float32)
 
 
-def pack_kernel(height, capacity, child_ref, rows_ref, live_ref, out_ref):
-    count, width = child_ref.shape
+def pack_kernel(height, capacity, child_hbm, rows_hbm, live_hbm, out_ref, rows_ref, live_ref, sems):
+    count, width = child_hbm.shape
+    copies = [
+        pltpu.make_async_copy(live_hbm, live_ref, sems.at[0]),
+        pltpu.make_async_copy(rows_hbm, rows_ref, sems.at[1]),
+        pltpu.make_async_copy(child_hbm, out_ref.at[:, pl.ds(0, width)], sems.at[2]),
+    ]
+    for copy in copies:
+        copy.start()
+    copies[0].wait()
+    copies[1].wait()
     owners = live_ref.shape[1]
     lanes = rows_ref.shape[1]
-    out_ref[:, :width] = child_ref[...]
     live = jnp.broadcast_to(live_ref[...].astype(jnp.float32), (count, owners))
     owner = lax.div(iota((count, owners), 0), jnp.int32(capacity))
     live = jnp.sum(jnp.where(owner == iota((count, owners), 1), live, 0.0), axis=1, keepdims=True)
@@ -89,6 +100,7 @@
     )
     targets = jnp.where(slot < live, rows, -1.0)
     out_ref[:, width:] = jnp.broadcast_to(targets, (count, BLOCK))
+    copies[2].wait()
 
 
 def placed(front, rows, targets, cols):
@@ -144,11 +156,13 @@
 def place_kernel(
     core_ref, front_ref, arrived_ref, cols_ref, out_ref, keep_ref, send_ref, *refs
 ):
-    share_refs, whole_ref = refs[:-1], refs[-1]
+    share_refs, (whole_ref, copied_ref, sem) = refs[:-3], refs[-3:]
     child_width = cols_ref.shape[1]
     targets = arrived_ref[:, child_width : child_width + 1].astype(jnp.int32)
     front = placed(front_ref[...], arrived_ref[:, :child_width], targets, cols_ref[...])
-    out_ref[...] = front
+    copied_ref[...] = front
+    copy = pltpu.make_async_copy(copied_ref, out_ref, sem)
+    copy.start()
     height = share_refs[0].shape[0]
     for k, ref in enumerate(share_refs):
         ref[...] = front[k * height : (k + 1) * height, :]
@@ -162,9 +176,15 @@
                 left = (j - 2 * first) * BLOCK
                 whole_ref[at : at + BLOCK, :] = product[i * BLOCK : (i + 1) * BLOCK, left : left + BLOCK]
     halves(core_ref, whole_ref, keep_ref, send_ref)
-
-
-def product_kernel(core_ref, panel_ref, front_ref, keep_ref, send_ref, whole_ref):
+    copy.wait()
+
+
+def product_kernel(core_ref, col_ref, front_ref, *refs):
+    shares, (panel_ref, keep_ref, send_ref, whole_ref) = refs[:-4], refs[-4:]
+    height, parts = shares[0].shape[0], len(shares)
+    for k, ref in enumerate(shares):
+        source = lax.rem(col_ref[0, 0] + (parts - k), jnp.int32(parts))
+        panel_ref[pl.ds(pl.multiple_of(source * height, height), height), :] = ref[...]
     whole_ref[...] = dot(panel_ref[...], front_ref[...], 0, 0)
     halves(core_ref, whole_ref, keep_ref, send_ref)
 
@@ -252,27 +272,33 @@
     return ref[at : at + BLOCK, left : left + (i + 1) * BLOCK]
 
 
-def basis_kernel(panel_ref, *refs):
-    blocks, out_ref = refs[:-1], refs[-1]
+def last_factor_kernel(core_ref, own_ref, other_ref, panel_ref, *refs):
+    blocks, basis_ref = refs[:-1], refs[-1]
+    factor_kernel(PIECES - 1, core_ref, own_ref, other_ref, *blocks)
     for i in range(PANELS // BLOCK):
         upto = (i + 1) * BLOCK
-        out_ref[:, i * BLOCK : upto] = dot(panel_ref[:, :upto], inverse_rows(blocks, i), 1, 1)
-
-
-def final_kernel(root_rows, core_ref, root_ref, front_ref, basis_ref, own_ref, other_ref, *refs):
-    blocks, (out_ref, factor_ref) = refs[:-2], refs[-2:]
+        basis_ref[:, i * BLOCK : upto] = dot(panel_ref[:, :upto], inverse_rows(blocks, i), 1, 1)
+
+
+def final_kernel(root_rows, core_ref, root_ref, *refs):
+    ins, (out_hbm, factor_hbm), refs = refs[:6], refs[6:8], refs[8:]
+    held, (out_ref, factor_ref, sems) = refs[:6], refs[6:]
+    copies = [
+        pltpu.make_async_copy(source, target, sems.at[i])
+        for i, (source, target) in enumerate(zip(ins, held))
+    ]
+    for copy in copies:
+        copy.start()
+    upper_ref, lower_ref, own_ref, other_ref, basis_ref, front_ref = held
+    blocks = (upper_ref, lower_ref)
+    for copy in copies[:4]:
+        copy.wait()
     sums = in_order(core_ref, own_ref[...], other_ref[...])
     coupled = jnp.concatenate(
         [dot(inverse_rows(blocks, i), sums[: (i + 1) * BLOCK, :]) for i in range(PANELS // BLOCK)],
         axis=0,
     )
     is_root = root_ref[0, 0] == 1
-    basis = basis_ref[...]
-    basis_hi, basis_mid, _ = split3(basis)
-    coupled_hi, coupled_mid, _ = split3(coupled)
-    update = dot_fast(basis_mid, coupled_hi) + dot_fast(basis_hi, coupled_mid)
-    update = update + dot_fast(basis_hi, coupled_hi)
-    out_ref[...] = jnp.where(is_root, basis * root_rows, front_ref[...] - update)
     per = PANELS // PIECES
     upper = jnp.concatenate(
         [
@@ -284,6 +310,25 @@
         axis=0,
     )
     factor_ref[...] = jnp.where(is_root, upper, coupled) * (1.0 / root_rows)
+    written = [pltpu.make_async_copy(factor_ref, factor_hbm, sems.at[6])]
+    written[0].start()
+    coupled_hi, coupled_mid, _ = split3(coupled)
+    for copy in copies[4:]:
+        copy.wait()
+    half = out_ref.shape[0] // 2
+    for i in range(2):
+        rows = pl.ds(i * half, half)
+        basis = basis_ref[rows, :]
+        basis_hi, basis_mid, _ = split3(basis)
+        update = dot_fast(basis_mid, coupled_hi) + dot_fast(basis_hi, coupled_mid)
+        update = update + dot_fast(basis_hi, coupled_hi)
+        out_ref[rows, :] = jnp.where(is_root, basis * root_rows, front_ref[rows, :] - update)
+        written.append(
+            pltpu.make_async_copy(out_ref.at[rows, :], out_hbm.at[rows, :], sems.at[7 + i])
+        )
+        written[-1].start()
+    for copy in written:
+        copy.wait()
 
 
 def exchange(blocks, axis):
@@ -317,7 +362,8 @@
     count, child_width = child_block.shape
     capacity = count // owners
     core = lax.axis_index("core").astype(jnp.int32)
-    is_root = (lax.axis_index("col") == 0).astype(jnp.int32)
+    col = lax.axis_index("col").astype(jnp.int32)
+    is_root = (col == 0).astype(jnp.int32)
     halved = (f32(3 * PANELS // 2, BLOCK),) * 2
     local_cols = column_map % cols_dev
 
@@ -325,6 +371,13 @@
         lambda *refs: pack_kernel(rows_dev, capacity, *refs),
         f32(count, child_width + BLOCK), "pack", 1 << 20,
         child_block, child_rows.reshape(count // BLOCK, BLOCK), live_counts,
+        ins=[HBM] * 3,
+        vmem=56,
+        scratch=[
+            pltpu.VMEM((count // BLOCK, BLOCK), jnp.int32),
+            pltpu.VMEM((1, owners), jnp.int32),
+            pltpu.SemaphoreType.DMA((3,)),
+        ],
     )
     arrived = merge_rows(exchange(sent.reshape(owners, capacity, child_width + BLOCK), ROW))
 
@@ -332,49 +385,63 @@
     front, keep, send, *shares = call(
         place_kernel, [f32(rows_dev, cols_dev), *halved] + [share] * parts,
         "place", 4 << 30, front_in, arrived, local_cols.reshape(1, child_width), scalars=(core,),
-        scratch=[pltpu.VMEM((3 * PANELS, BLOCK), jnp.float32)],
-    )
+        scratch=[
+            pltpu.VMEM((3 * PANELS, BLOCK), jnp.float32),
+            pltpu.VMEM((rows_dev, cols_dev), jnp.float32),
+            pltpu.SemaphoreType.DMA,
+        ],
+        outs=[HBM] + [VMEM] * (parts + 2),
+    )
+    half = summed(keep, swapped(send))
+    half, shares = lax.optimization_barrier((half, shares))
     sent_shares = [lax.ppermute(shares[k], "col", [(0, k)]) for k in range(1, parts)]
     panel_share = call(
         choose_kernel, share, "choose", 1 << 20, shares[0], *sent_shares, scalars=(is_root,), vmem=4
     )
-    panel = lax.all_gather(panel_share, "col", tiled=True)
-
-    half = summed(keep, swapped(send))
-    gram_share = folded(exchange(split_rows(half, chips), ("z", "x")), parts)
-    gram_share = exchange(gram_share, "col")
+    grams = exchange(split_rows(half, chips), ("z", "x"))
+    grams, panel_share = lax.optimization_barrier((grams, panel_share))
+    panel_shares = [panel_share] + [
+        lax.ppermute(panel_share, "col", [(i, (i + k) % parts) for i in range(parts)])
+        for k in range(1, parts)
+    ]
+
+    gram_share = exchange(folded(grams, parts), "col")
+    gram_share, panel_shares[5:] = lax.optimization_barrier((gram_share, panel_shares[5:]))
     gram_share = call(
         first_kernel, f32(chips, *gram_share.shape[1:]), "first", 1 << 20, gram_share, vmem=4
     )
     own_gram = merge_rows(exchange(gram_share, ("z", "x")))
     other_gram = swapped(own_gram)
 
-    keep, send = call(
-        product_kernel, (f32(PANELS // 2, cols_dev),) * 2, "products", 2 << 30, panel, front,
-        scalars=(core,), scratch=[pltpu.VMEM((PANELS, cols_dev), jnp.float32)],
+    panel, keep, send = call(
+        product_kernel, (f32(rows_dev, PANELS),) + (f32(PANELS // 2, cols_dev),) * 2,
+        "products", 2 << 30, front, *panel_shares, scalars=(core, col), scratch=[pltpu.VMEM((PANELS, cols_dev), jnp.float32)],
     )
     half = summed(keep, swapped(send))
-    sums_share = folded(exchange(split_rows(half, chips), ("z", "x")), chips)
-
-    blocks = []
-    for piece in range(PIECES):
-        blocks.append(
-            call(
-                lambda *refs, piece=piece: factor_kernel(piece, *refs),
-                f32(PANELS // PIECES, 3 * PANELS // 2), f"factor{piece}", 10 << 30,
-                own_gram, other_gram, *blocks, scalars=(core,),
-            )
-        )
-        if piece == 0:
-            sums_share, blocks[0] = lax.optimization_barrier((sums_share, blocks[0]))
-            own_sums = merge_rows(exchange(sums_share, ("z", "x")))
-    own_sums, blocks[1] = lax.optimization_barrier((own_sums, blocks[1]))
+    summands = exchange(split_rows(half, chips), ("z", "x"))
+
+    block_shape = f32(PANELS // PIECES, 3 * PANELS // 2)
+    upper = call(
+        lambda *refs: factor_kernel(0, *refs), block_shape, "factor0", 10 << 30,
+        own_gram, other_gram, scalars=(core,),
+    )
+    summands, upper = lax.optimization_barrier((summands, upper))
+    own_sums = merge_rows(exchange(folded(summands, chips), ("z", "x")))
+    lower, basis = call(
+        last_factor_kernel, (block_shape, f32(rows_dev, PANELS)), "factor1", 12 << 30,
+        own_gram, other_gram, panel, upper, scalars=(core,),
+    )
+    own_sums, basis = lax.optimization_barrier((own_sums, basis))
     other_sums = swapped(own_sums)
-    basis = call(basis_kernel, f32(rows_dev, PANELS), "basis", 2 << 30, panel, *blocks)
+    whole = (rows_dev, cols_dev)
+    ins = (upper, lower, own_sums, other_sums, basis, front)
     return call(
         lambda *refs: final_kernel(math.sqrt(rows_dev * owners), *refs),
-        (f32(rows_dev, cols_dev), f32(PANELS, cols_dev)), "final", 4 << 30,
-        front, basis, own_sums, other_sums, *blocks, scalars=(core, is_root),
+        (f32(*whole), f32(PANELS, cols_dev)), "final", 4 << 30, *ins, scalars=(core, is_root),
+        ins=[HBM] * len(ins), outs=(HBM, HBM), vmem=56,
+        scratch=[pltpu.VMEM(x.shape, jnp.float32) for x in ins]
+        + [pltpu.VMEM(whole, jnp.float32), pltpu.VMEM((PANELS, cols_dev), jnp.float32)]
+        + [pltpu.SemaphoreType.DMA((9,))],
     )
 
 

time: 196 us -> 209 us (1.066)
  starting transfers between devices: 64.3 us -> 102 us
  blocking collectives: 30.8 us -> 0 us
  waiting for transfers between devices: 43.1 us -> 61.4 us
  between operations: 14.4 us -> 1.21 us
  local copies, waits for them, and re-layouts: 9.52 us -> 5.21 us
  Pallas kernels: 33.4 us -> 37.4 us
    all_to_all x2 -> x0, blocking collectives: 30.8 us -> none  [exchange(): return lax.all_to_all(blocks, axis, split_axis=0, concat_axis=0, tiled=True)]
    ppermute x0 -> x7, starting transfers between devices: none -> 26.9 us  [on_device(): lax.ppermute(panel_share, 'col', [(i, (i + k) % parts) for i in range(par...]
    ppermute x0 -> x7, waiting for transfers between devices: none -> 23.3 us  [on_device(): lax.ppermute(panel_share, 'col', [(i, (i + k) % parts) for i in range(par...]
    all_to_all x4 -> x6, starting transfers between devices: 29.5 us -> 48.6 us  [exchange(): return lax.all_to_all(blocks, axis, split_axis=0, concat_axis=0, tiled=True)]
    ppermute x4, starting transfers between devices: 21.4 us -> 13.5 us  [swapped(): return lax.ppermute(x, 'core', [(0, 1), (1, 0)])]
    all_to_all x4 -> x6, waiting for transfers between devices: 36.9 us -> 30.2 us  [exchange(): return lax.all_to_all(blocks, axis, split_axis=0, concat_axis=0, tiled=True)]
    unnamed x34 -> x24, local copies, waits for them, and re-layouts: 9.52 us -> 5.21 us
    pallas_call x13 -> x12, Pallas kernels: 33.4 us -> 37.4 us  [call(): pl.pallas_call(kernel, out_shape=out_shape, in_specs=[SMEM] * len(scalars...]
  transfers between devices with their start and end apart: 16 -> 24, of which waited for: 8 -> 13; matrix products, arithmetic and copies ran while one was open for 0% -> 0% of each run, Pallas kernels for 12% -> 11%
where the time goes in v5:
time: 209 us; the launch traced here: 208 us
  starting transfers between devices  102 us (49%)
  waiting for transfers between devices  61.4 us (29%)
  Pallas kernels  37.4 us (18%)
  local copies, waits for them, and re-layouts  5.21 us (2%)
    all_to_all x6, starting transfers between devices, exchange(): return lax.all_to_all(blocks, axis, split_axis=0, concat_axis=0, tiled=True)  48.6 us
    pallas_call x12, Pallas kernels, call(): pl.pallas_call(kernel, out_shape=out_shape, in_specs=[SMEM] * len(scalars...  37.4 us
    all_to_all x6, waiting for transfers between devices, exchange(): return lax.all_to_all(blocks, axis, split_axis=0, concat_axis=0, tiled=True)  30.2 us
    ppermute x7, starting transfers between devices, on_device(): lax.ppermute(panel_share, 'col', [(i, (i + k) % parts) for i in range(par...  26.9 us
    ppermute x7, waiting for transfers between devices, on_device(): lax.ppermute(panel_share, 'col', [(i, (i + k) % parts) for i in range(par...  23.3 us
    ppermute x4, starting transfers between devices, swapped(): return lax.ppermute(x, 'core', [(0, 1), (1, 0)])  13.5 us
    ppermute x7, starting transfers between devices, on_device(): lax.ppermute(shares[k], 'col', [(0, k)])  13.4 us
    unnamed x24, local copies, waits for them, and re-layouts  5.21 us
  transfers between devices with their start and end apart: 24, of which 13 were waited for; matrix products, arithmetic and copies ran while one was open for 0% of the time, Pallas kernels for 11%

profile of v5, /device:TPU:1, one launch (start us, length us, event | category | flops | bytes accessed | tf_op | source)
XLA Modules:
  0.0 207.6 jit_solution(13292212501423610503)
XLA Ops:
  2.6 15.0 %all-to-all-start = ((f32[64,8,384]{2,1,0:T(8,128)}), f32[64,8,384]{2,1,0:T(8,128)S(1)}, u32[]{:S(2)}, u32[]{:S(2)}) async-start(f32[64,8,384]{2,1,0:T(8,128)} %bitcast.16), calls=%async_computation | async-start | bytes 1572864 | tf_op jit(solution)/shard_map/all_to_all | solution.py:335
  18.3 22.1 %all-to-all-done = f32[64,8,384]{2,1,0:T(8,128)S(1)} async-done(((f32[64,8,384]{2,1,0:T(8,128)}), f32[64,8,384]{2,1,0:T(8,128)S(1)}, u32[]{:S(2)}, u32[]{:S(2)}) %all-to-all-start) | async-done | bytes 786464 | tf_op jit(solution)/shard_map/all_to_all | solution.py:335
  40.4 4.1 %place.1 = (f32[512,512]{1,0:T(8,128)S(1)}, f32[768,128]{1,0:T(8,128)S(1)}, f32[768,128]{1,0:T(8,128)S(1)}, f32[64,512]{1,0:T(8,128)S(1)}, f32[64,512]{1,0:T(8,1...) custom-call(s32[1,1]{1,0:T(1,128)} %bitcast.core_ref.refs_0_, ...), custom_call_target="tpu_custom_call" | custom-call | flops 4294967296 | bytes 4194304 | tf_op jit(solution)/shard_map/place/pallas_call | solution.py:51
  49.5 4.8 %all-to-all-start.1 = ((f32[32,24,128]{2,1,0:T(8,128)}), f32[32,24,128]{2,1,0:T(8,128)S(1)}, u32[]{:S(2)}, u32[]{:S(2)}) async-start(f32[32,24,128]{2,1,0:T(8,128)} %bitcast.7), calls=%async_computation.1 | async-start | bytes 786432 | tf_op jit(solution)/shard_map/all_to_all | solution.py:335
  54.3 3.2 %collective-permute-start.1 = (f32[64,512]{1,0:T(8,128)S(1)}, f32[64,512]{1,0:T(8,128)S(1)}, u32[]{:S(2)}, u32[]{:S(2)}) collective-permute-start(f32[64,512]{1,0:T(8,128)S(1)} %get-tuple-element.50), channel_id=1, source_target_pairs={{0,1},{8,9},{16,17},{24,25},{32,33},{40,41},{48,49},{56,57},{64,65... | collective-permute-start | bytes 393224 | tf_op jit(solution)/shard_map/ppermute | solution.py:397
  60.9 2.9 %collective-permute-start.4 = (f32[64,512]{1,0:T(8,128)S(1)}, f32[64,512]{1,0:T(8,128)S(1)}, u32[]{:S(2)}, u32[]{:S(2)}) collective-permute-start(f32[64,512]{1,0:T(8,128)S(1)} %get-tuple-element.53), channel_id=1, source_target_pairs={{0,4},{8,12},{16,20},{24,28},{32,36},{40,44},{48,52},{56,60},{64,6... | collective-permute-start | bytes 393224 | tf_op jit(solution)/shard_map/ppermute | solution.py:397
  73.6 4.7 %all-to-all-start.2 = ((f32[8,24,128]{2,1,0:T(8,128)}), f32[8,24,128]{2,1,0:T(8,128)S(1)}, u32[]{:S(2)}, u32[]{:S(2)}) async-start(f32[8,24,128]{2,1,0:T(8,128)} %fold.2), calls=%async_computation.2 | async-start | bytes 196608 | tf_op jit(solution)/shard_map/all_to_all | solution.py:335
  78.3 4.6 %collective-permute-start.14 = (f32[64,512]{1,0:T(8,128)S(1)}, f32[64,512]{1,0:T(8,128)S(1)}, u32[]{:S(2)}, u32[]{:S(2)}) collective-permute-start(f32[64,512]{1,0:T(8,128)S(1)} %choose.1.refs_0_), channel_id=1, source_target_pairs={{0,7},{1,0},{2,1},{3,2},{4,3},{5,4},{6,5},{7,6},{8,15},{9,8},{10,9... | collective-permute-start | bytes 393224 | tf_op jit(solution)/shard_map/ppermute | solution.py:404
  82.9 4.0 %collective-permute-start.13 = (f32[64,512]{1,0:T(8,128)S(1)}, f32[64,512]{1,0:T(8,128)S(1)}, u32[]{:S(2)}, u32[]{:S(2)}) collective-permute-start(f32[64,512]{1,0:T(8,128)S(1)} %choose.1.refs_0_), channel_id=1, source_target_pairs={{0,6},{1,7},{2,0},{3,1},{4,2},{5,3},{6,4},{7,5},{8,14},{9,15},{10,... | collective-permute-start | bytes 393224 | tf_op jit(solution)/shard_map/ppermute | solution.py:404
  86.9 3.1 %collective-permute-start.12 = (f32[64,512]{1,0:T(8,128)S(1)}, f32[64,512]{1,0:T(8,128)S(1)}, u32[]{:S(2)}, u32[]{:S(2)}) collective-permute-start(f32[64,512]{1,0:T(8,128)S(1)} %choose.1.refs_0_), channel_id=1, source_target_pairs={{0,5},{1,6},{2,7},{3,0},{4,1},{5,2},{6,3},{7,4},{8,13},{9,14},{10,... | collective-permute-start | bytes 393224 | tf_op jit(solution)/shard_map/ppermute | solution.py:404
  90.9 7.7 %collective-permute-done.12.refs_5_ = f32[64,512]{1,0:T(8,128)S(1)} collective-permute-done((f32[64,512]{1,0:T(8,128)S(1)}, f32[64,512]{1,0:T(8,128)S(1)}, u32[]{:S(2)}, u32[]{:S(2)}) %collective-permute-start.12) | collective-permute-done | bytes 131104 | tf_op jit(solution)/shard_map/ppermute | solution.py:404
  99.3 9.2 %all-to-all-start.4 = ((f32[32,24,128]{2,1,0:T(8,128)}), f32[32,24,128]{2,1,0:T(8,128)S(1)}, u32[]{:S(2)}, u32[]{:S(2)}) async-start(f32[32,24,128]{2,1,0:T(8,128)} %first.1), calls=%async_computation.4 | async-start | bytes 786432 | tf_op jit(solution)/shard_map/all_to_all | solution.py:335
  110.5 8.4 %collective-permute-start.10 = (f32[64,512]{1,0:T(8,128)S(1)}, f32[64,512]{1,0:T(8,128)S(1)}, u32[]{:S(2)}, u32[]{:S(2)}) collective-permute-start(f32[64,512]{1,0:T(8,128)S(1)} %choose.1.refs_0_), channel_id=1, source_target_pairs={{0,3},{1,4},{2,5},{3,6},{4,7},{5,0},{6,1},{7,2},{8,11},{9,12},{10,... | collective-permute-start | bytes 393224 | tf_op jit(solution)/shard_map/ppermute | solution.py:404
  123.9 3.4 %collective-permute-done.10.refs_3_ = f32[64,512]{1,0:T(8,128)S(1)} collective-permute-done((f32[64,512]{1,0:T(8,128)S(1)}, f32[64,512]{1,0:T(8,128)S(1)}, u32[]{:S(2)}, u32[]{:S(2)}) %collective-permute-start.10) | collective-permute-done | bytes 131104 | tf_op jit(solution)/shard_map/ppermute | solution.py:404
  127.3 7.9 %collective-permute-done.9.refs_2_ = f32[64,512]{1,0:T(8,128)S(1)} collective-permute-done((f32[64,512]{1,0:T(8,128)S(1)}, f32[64,512]{1,0:T(8,128)S(1)}, u32[]{:S(2)}, u32[]{:S(2)}) %collective-permute-start.9) | collective-permute-done | bytes 131104 | tf_op jit(solution)/shard_map/ppermute | solution.py:404
  135.2 3.4 %collective-permute-done.8.refs_1_ = f32[64,512]{1,0:T(8,128)S(1)} collective-permute-done((f32[64,512]{1,0:T(8,128)S(1)}, f32[64,512]{1,0:T(8,128)S(1)}, u32[]{:S(2)}, u32[]{:S(2)}) %collective-permute-start.8) | collective-permute-done | bytes 131104 | tf_op jit(solution)/shard_map/ppermute | solution.py:404
  141.6 3.1 %collective-permute-start.15 = (f32[256,512]{1,0:T(8,128)S(1)}, f32[256,512]{1,0:T(8,128)S(1)}, u32[]{:S(2)}, u32[]{:S(2)}) collective-permute-start(f32[256,512]{1,0:T(8,128)S(1)} %get-tuple-element.63), channel_id=1, source_target_pairs={{0,8},{8,0},{1,9},{9,1},{2,10},{10,2},{3,11},{11,3},{4,12},{12,4},... | collective-permute-start | bytes 1572872 | tf_op jit(solution)/shard_map/ppermute | solution.py:339
  147.6 9.4 %all-to-all-start.3 = ((f32[32,8,512]{2,1,0:T(8,128)}), f32[32,8,512]{2,1,0:T(8,128)S(1)}, u32[]{:S(2)}, u32[]{:S(2)}) async-start(f32[32,8,512]{2,1,0:T(8,128)} %bitcast.8), calls=%async_computation.3 | async-start | bytes 1048576 | tf_op jit(solution)/shard_map/all_to_all | solution.py:335
  157.0 8.8 %factor0.1.refs_0_.refs_2_ = f32[256,768]{1,0:T(8,128)S(1)} custom-call(s32[1,1]{1,0:T(1,128)} %bitcast.core_ref.refs_0_, f32[768,128]{1,0:T(8,128)S(1)} %bitcast.13, f32[768,128]{1,0:T(8,128)S(1)} %collective-permute-done.16.refs_2_.other_ref), custom_call_target="tpu_custom_call" | custom-call | flops 10737418240 | bytes 4194304 | tf_op jit(solution)/shard_map/factor0/pallas_call | solution.py:51
  166.7 6.6 %all-to-all-done.3.x_ref = f32[32,8,512]{2,1,0:T(8,128)S(1)} async-done(((f32[32,8,512]{2,1,0:T(8,128)}), f32[32,8,512]{2,1,0:T(8,128)S(1)}, u32[]{:S(2)}, u32[]{:S(2)}) %all-to-all-start.3) | async-done | bytes 524320 | tf_op jit(solution)/shard_map/all_to_all | solution.py:335
  174.1 5.5 %all-to-all-start.5 = ((f32[32,8,512]{2,1,0:T(8,128)}), f32[32,8,512]{2,1,0:T(8,128)S(1)}, u32[]{:S(2)}, u32[]{:S(2)}) async-start(f32[32,8,512]{2,1,0:T(8,128)} %fold.3), calls=%async_computation.5 | async-start | bytes 1048576 | tf_op jit(solution)/shard_map/all_to_all | solution.py:335
  179.6 11.6 %factor1.1 = (f32[256,768]{1,0:T(8,128)S(1)}, f32[512,512]{1,0:T(8,128)S(1)}) custom-call(s32[1,1]{1,0:T(1,128)} %bitcast.core_ref.refs_0_, f32[768,128]{1,0:T(8,128)S(1)} %bitcast.14, f32[768,128]{1,0:T(8,128)S(1)} %collective-permute-done.16.refs_2_.other_ref, f32[512,512]{1,0:T(8,128)S(1)} %copy-done.4, f32[256,768]{1,0:T(8,128)S(1)} %copy-done.7), custom_call_target="tpu_custom_call" | custom-call | flops 12884901888 | bytes 4194304 | tf_op jit(solution)/shard_map/factor1/pallas_call | solution.py:51
  194.6 5.5 %collective-permute-start.17 = (f32[256,512]{1,0:T(8,128)S(1)}, f32[256,512]{1,0:T(8,128)S(1)}, u32[]{:S(2)}, u32[]{:S(2)}) collective-permute-start(f32[256,512]{1,0:T(8,128)S(1)} %bitcast.17), channel_id=1, source_target_pairs={{0,8},{8,0},{1,9},{9,1},{2,10},{10,2},{3,11},{11,3},{4,12},{12,4},... | collective-permute-start | bytes 1572872 | tf_op jit(solution)/shard_map/ppermute | solution.py:339
  202.4 5.0 %final.1 = (f32[512,512]{1,0:T(8,128)}, f32[512,512]{1,0:T(8,128)}) custom-call(s32[1,1]{1,0:T(1,128)} %bitcast.core_ref.refs_0_, s32[1,1]{1,0:T(1,128)} %bitcast.1.root_ref.refs_1_, f32[256,768]{1,0:T(8,128)} %copy-done.6, f32[256,768]{1,0:T(8,128)} %copy-done.8, f32[256,512]{1,0:T(8,128)} %bitcast.18, f32[256,512]{1,0:T(8,128)} %copy-done.11, ...), custom_call_target="tpu_custom_call" | custom-call | flops 4294967296 | bytes 4194304 | tf_op jit(solution)/shard_map/final/pallas_call | solution.py:51
  (61 shorter events, 42.5 us)
Async XLA Ops:
  2.6 37.7 %all-to-all-start = ((f32[64,8,384]{2,1,0:T(8,128)}), f32[64,8,384]{2,1,0:T(8,128)S(1)}, u32[]{:S(2)}, u32[]{:S(2)}) async-start(f32[64,8,384]{2,1,0:T(8,128)} %bitcast.16), calls=%async_computation | async-start | bytes 1572864 | tf_op jit(solution)/shard_map/all_to_all | solution.py:335
  44.5 4.2 %collective-permute-start = (f32[768,128]{1,0:T(8,128)S(1)}, f32[768,128]{1,0:T(8,128)S(1)}, u32[]{:S(2)}, u32[]{:S(2)}) collective-permute-start(f32[768,128]{1,0:T(8,128)S(1)} %get-tuple-element.39), channel_id=1, source_target_pairs={{0,8},{8,0},{1,9},{9,1},{2,10},{10,2},{3,11},{11,3},{4,12},{12,4},... | collective-permute-start | bytes 1179656 | tf_op jit(solution)/shard_map/ppermute | solution.py:339
  49.5 23.5 %all-to-all-start.1 = ((f32[32,24,128]{2,1,0:T(8,128)}), f32[32,24,128]{2,1,0:T(8,128)S(1)}, u32[]{:S(2)}, u32[]{:S(2)}) async-start(f32[32,24,128]{2,1,0:T(8,128)} %bitcast.7), calls=%async_computation.1 | async-start | bytes 786432 | tf_op jit(solution)/shard_map/all_to_all | solution.py:335
  54.3 10.8 %collective-permute-start.1 = (f32[64,512]{1,0:T(8,128)S(1)}, f32[64,512]{1,0:T(8,128)S(1)}, u32[]{:S(2)}, u32[]{:S(2)}) collective-permute-start(f32[64,512]{1,0:T(8,128)S(1)} %get-tuple-element.50), channel_id=1, source_target_pairs={{0,1},{8,9},{16,17},{24,25},{32,33},{40,41},{48,49},{56,57},{64,65... | collective-permute-start | bytes 393224 | tf_op jit(solution)/shard_map/ppermute | solution.py:397
  57.5 8.9 %collective-permute-start.2 = (f32[64,512]{1,0:T(8,128)S(1)}, f32[64,512]{1,0:T(8,128)S(1)}, u32[]{:S(2)}, u32[]{:S(2)}) collective-permute-start(f32[64,512]{1,0:T(8,128)S(1)} %get-tuple-element.51), channel_id=1, source_target_pairs={{0,2},{8,10},{16,18},{24,26},{32,34},{40,42},{48,50},{56,58},{64,6... | collective-permute-start | bytes 393224 | tf_op jit(solution)/shard_map/ppermute | solution.py:397
  59.2 8.5 %collective-permute-start.3 = (f32[64,512]{1,0:T(8,128)S(1)}, f32[64,512]{1,0:T(8,128)S(1)}, u32[]{:S(2)}, u32[]{:S(2)}) collective-permute-start(f32[64,512]{1,0:T(8,128)S(1)} %get-tuple-element.52), channel_id=1, source_target_pairs={{0,3},{8,11},{16,19},{24,27},{32,35},{40,43},{48,51},{56,59},{64,6... | collective-permute-start | bytes 393224 | tf_op jit(solution)/shard_map/ppermute | solution.py:397
  60.9 7.2 %collective-permute-start.4 = (f32[64,512]{1,0:T(8,128)S(1)}, f32[64,512]{1,0:T(8,128)S(1)}, u32[]{:S(2)}, u32[]{:S(2)}) collective-permute-start(f32[64,512]{1,0:T(8,128)S(1)} %get-tuple-element.53), channel_id=1, source_target_pairs={{0,4},{8,12},{16,20},{24,28},{32,36},{40,44},{48,52},{56,60},{64,6... | collective-permute-start | bytes 393224 | tf_op jit(solution)/shard_map/ppermute | solution.py:397
  63.8 4.3 %collective-permute-start.5 = (f32[64,512]{1,0:T(8,128)S(1)}, f32[64,512]{1,0:T(8,128)S(1)}, u32[]{:S(2)}, u32[]{:S(2)}) collective-permute-start(f32[64,512]{1,0:T(8,128)S(1)} %get-tuple-element.54), channel_id=1, source_target_pairs={{0,5},{8,13},{16,21},{24,29},{32,37},{40,45},{48,53},{56,61},{64,6... | collective-permute-start | bytes 393224 | tf_op jit(solution)/shard_map/ppermute | solution.py:397
  65.1 5.0 %collective-permute-start.6 = (f32[64,512]{1,0:T(8,128)S(1)}, f32[64,512]{1,0:T(8,128)S(1)}, u32[]{:S(2)}, u32[]{:S(2)}) collective-permute-start(f32[64,512]{1,0:T(8,128)S(1)} %get-tuple-element.55), channel_id=1, source_target_pairs={{0,6},{8,14},{16,22},{24,30},{32,38},{40,46},{48,54},{56,62},{64,7... | collective-permute-start | bytes 393224 | tf_op jit(solution)/shard_map/ppermute | solution.py:397
  66.4 6.5 %collective-permute-start.7 = (f32[64,512]{1,0:T(8,128)S(1)}, f32[64,512]{1,0:T(8,128)S(1)}, u32[]{:S(2)}, u32[]{:S(2)}) collective-permute-start(f32[64,512]{1,0:T(8,128)S(1)} %get-tuple-element.56), channel_id=1, source_target_pairs={{0,7},{8,15},{16,23},{24,31},{32,39},{40,47},{48,55},{56,63},{64,7... | collective-permute-start | bytes 393224 | tf_op jit(solution)/shard_map/ppermute | solution.py:397
  73.6 25.0 %all-to-all-start.2 = ((f32[8,24,128]{2,1,0:T(8,128)}), f32[8,24,128]{2,1,0:T(8,128)S(1)}, u32[]{:S(2)}, u32[]{:S(2)}) async-start(f32[8,24,128]{2,1,0:T(8,128)} %fold.2), calls=%async_computation.2 | async-start | bytes 196608 | tf_op jit(solution)/shard_map/all_to_all | solution.py:335
  78.3 11.7 %collective-permute-start.14 = (f32[64,512]{1,0:T(8,128)S(1)}, f32[64,512]{1,0:T(8,128)S(1)}, u32[]{:S(2)}, u32[]{:S(2)}) collective-permute-start(f32[64,512]{1,0:T(8,128)S(1)} %choose.1.refs_0_), channel_id=1, source_target_pairs={{0,7},{1,0},{2,1},{3,2},{4,3},{5,4},{6,5},{7,6},{8,15},{9,8},{10,9... | collective-permute-start | bytes 393224 | tf_op jit(solution)/shard_map/ppermute | solution.py:404
  82.9 8.0 %collective-permute-start.13 = (f32[64,512]{1,0:T(8,128)S(1)}, f32[64,512]{1,0:T(8,128)S(1)}, u32[]{:S(2)}, u32[]{:S(2)}) collective-permute-start(f32[64,512]{1,0:T(8,128)S(1)} %choose.1.refs_0_), channel_id=1, source_target_pairs={{0,6},{1,7},{2,0},{3,1},{4,2},{5,3},{6,4},{7,5},{8,14},{9,15},{10,... | collective-permute-start | bytes 393224 | tf_op jit(solution)/shard_map/ppermute | solution.py:404
  86.9 11.7 %collective-permute-start.12 = (f32[64,512]{1,0:T(8,128)S(1)}, f32[64,512]{1,0:T(8,128)S(1)}, u32[]{:S(2)}, u32[]{:S(2)}) collective-permute-start(f32[64,512]{1,0:T(8,128)S(1)} %choose.1.refs_0_), channel_id=1, source_target_pairs={{0,5},{1,6},{2,7},{3,0},{4,1},{5,2},{6,3},{7,4},{8,13},{9,14},{10,... | collective-permute-start | bytes 393224 | tf_op jit(solution)/shard_map/ppermute | solution.py:404
  99.3 45.4 %all-to-all-start.4 = ((f32[32,24,128]{2,1,0:T(8,128)}), f32[32,24,128]{2,1,0:T(8,128)S(1)}, u32[]{:S(2)}, u32[]{:S(2)}) async-start(f32[32,24,128]{2,1,0:T(8,128)} %first.1), calls=%async_computation.4 | async-start | bytes 786432 | tf_op jit(solution)/shard_map/all_to_all | solution.py:335
  108.6 15.3 %collective-permute-start.11 = (f32[64,512]{1,0:T(8,128)S(1)}, f32[64,512]{1,0:T(8,128)S(1)}, u32[]{:S(2)}, u32[]{:S(2)}) collective-permute-start(f32[64,512]{1,0:T(8,128)S(1)} %choose.1.refs_0_), channel_id=1, source_target_pairs={{0,4},{1,5},{2,6},{3,7},{4,0},{5,1},{6,2},{7,3},{8,12},{9,13},{10,... | collective-permute-start | bytes 393224 | tf_op jit(solution)/shard_map/ppermute | solution.py:404
  110.5 16.8 %collective-permute-start.10 = (f32[64,512]{1,0:T(8,128)S(1)}, f32[64,512]{1,0:T(8,128)S(1)}, u32[]{:S(2)}, u32[]{:S(2)}) collective-permute-start(f32[64,512]{1,0:T(8,128)S(1)} %choose.1.refs_0_), channel_id=1, source_target_pairs={{0,3},{1,4},{2,5},{3,6},{4,7},{5,0},{6,1},{7,2},{8,11},{9,12},{10,... | collective-permute-start | bytes 393224 | tf_op jit(solution)/shard_map/ppermute | solution.py:404
  119.0 16.2 %collective-permute-start.9 = (f32[64,512]{1,0:T(8,128)S(1)}, f32[64,512]{1,0:T(8,128)S(1)}, u32[]{:S(2)}, u32[]{:S(2)}) collective-permute-start(f32[64,512]{1,0:T(8,128)S(1)} %choose.1.refs_0_), channel_id=1, source_target_pairs={{0,2},{1,3},{2,4},{3,5},{4,6},{5,7},{6,0},{7,1},{8,10},{9,11},{10,... | collective-permute-start | bytes 393224 | tf_op jit(solution)/shard_map/ppermute | solution.py:404
  121.1 17.6 %collective-permute-start.8 = (f32[64,512]{1,0:T(8,128)S(1)}, f32[64,512]{1,0:T(8,128)S(1)}, u32[]{:S(2)}, u32[]{:S(2)}) collective-permute-start(f32[64,512]{1,0:T(8,128)S(1)} %choose.1.refs_0_), channel_id=1, source_target_pairs={{0,1},{1,2},{2,3},{3,4},{4,5},{5,6},{6,7},{7,0},{8,9},{9,10},{10,1... | collective-permute-start | bytes 393224 | tf_op jit(solution)/shard_map/ppermute | solution.py:404
  141.6 5.1 %collective-permute-start.15 = (f32[256,512]{1,0:T(8,128)S(1)}, f32[256,512]{1,0:T(8,128)S(1)}, u32[]{:S(2)}, u32[]{:S(2)}) collective-permute-start(f32[256,512]{1,0:T(8,128)S(1)} %get-tuple-element.63), channel_id=1, source_target_pairs={{0,8},{8,0},{1,9},{9,1},{2,10},{10,2},{3,11},{11,3},{4,12},{12,4},... | collective-permute-start | bytes 1572872 | tf_op jit(solution)/shard_map/ppermute | solution.py:339
  144.8 12.2 %collective-permute-start.16 = (f32[768,128]{1,0:T(8,128)S(1)}, f32[768,128]{1,0:T(8,128)S(1)}, u32[]{:S(2)}, u32[]{:S(2)}) collective-permute-start(f32[768,128]{1,0:T(8,128)S(1)} %bitcast.12), channel_id=1, source_target_pairs={{0,8},{8,0},{1,9},{9,1},{2,10},{10,2},{3,11},{11,3},{4,12},{12,4},... | collective-permute-start | bytes 1179656 | tf_op jit(solution)/shard_map/ppermute | solution.py:339
  147.6 25.7 %all-to-all-start.3 = ((f32[32,8,512]{2,1,0:T(8,128)}), f32[32,8,512]{2,1,0:T(8,128)S(1)}, u32[]{:S(2)}, u32[]{:S(2)}) async-start(f32[32,8,512]{2,1,0:T(8,128)} %bitcast.8), calls=%async_computation.3 | async-start | bytes 1048576 | tf_op jit(solution)/shard_map/all_to_all | solution.py:335
  174.1 20.5 %all-to-all-start.5 = ((f32[32,8,512]{2,1,0:T(8,128)}), f32[32,8,512]{2,1,0:T(8,128)S(1)}, u32[]{:S(2)}, u32[]{:S(2)}) async-start(f32[32,8,512]{2,1,0:T(8,128)} %fold.3), calls=%async_computation.5 | async-start | bytes 1048576 | tf_op jit(solution)/shard_map/all_to_all | solution.py:335
  194.6 7.0 %collective-permute-start.17 = (f32[256,512]{1,0:T(8,128)S(1)}, f32[256,512]{1,0:T(8,128)S(1)}, u32[]{:S(2)}, u32[]{:S(2)}) collective-permute-start(f32[256,512]{1,0:T(8,128)S(1)} %bitcast.17), channel_id=1, source_target_pairs={{0,8},{8,0},{1,9},{9,1},{2,10},{10,2},{3,11},{11,3},{4,12},{12,4},... | collective-permute-start | bytes 1572872 | tf_op jit(solution)/shard_map/ppermute | solution.py:339
  (12 other events, 139.2 us)

commit v6 on v5

--- a/solution.py
+++ b/solution.py
@@ -115,12 +115,25 @@
     return total
 
 
-def choose_kernel(root_ref, own_ref, *refs):
+def bundle_kernel(root_ref, grams_ref, own_ref, *refs):
     arrived, out_ref = refs[:-1], refs[-1]
-    total = arrived[0][...]
-    for ref in arrived[1:]:
-        total = total + ref[...]
-    out_ref[...] = jnp.where(root_ref[0, 0] == 1, own_ref[...], total)
+    share = total([ref[...] for ref in arrived])
+    share = jnp.where(root_ref[0, 0] == 1, own_ref[...], share)
+    gram = total([grams_ref[i] for i in range(grams_ref.shape[0])])
+    height = share.shape[0]
+    for i in range(out_ref.shape[0]):
+        for lanes in range(share.shape[1] // BLOCK):
+            out_ref[i, lanes * height : (lanes + 1) * height, :] = share[
+                :, lanes * BLOCK : (lanes + 1) * BLOCK
+            ]
+        out_ref[i, share.shape[1] // BLOCK * height :, :] = gram
+
+
+def total(terms):
+    while len(terms) > 1:
+        pairs = [a + b for a, b in zip(terms[::2], terms[1::2])]
+        terms = pairs + terms[len(pairs) * 2 :]
+    return terms[0]
 
 
 def add_kernel(a_ref, b_ref, out_ref):
@@ -128,16 +141,15 @@
 
 
 def fold_kernel(x_ref, out_ref):
-    terms = [x_ref[i] for i in range(x_ref.shape[0])]
-    while len(terms) > 1:
-        terms = [a + b for a, b in zip(terms[::2], terms[1::2])]
+    x = total([x_ref[i] for i in range(x_ref.shape[0])])
     for i in range(out_ref.shape[0]):
-        out_ref[i] = terms[0]
-
-
-def first_kernel(x_ref, out_ref):
+        out_ref[i] = x
+
+
+def gram_kernel(bundle_ref, out_ref):
+    height = out_ref.shape[1]
     for i in range(out_ref.shape[0]):
-        out_ref[i] = x_ref[0]
+        out_ref[i] = bundle_ref[0, bundle_ref.shape[1] - height :, :]
 
 
 def halves(core_ref, whole_ref, keep_ref, send_ref):
@@ -156,13 +168,11 @@
 def place_kernel(
     core_ref, front_ref, arrived_ref, cols_ref, out_ref, keep_ref, send_ref, *refs
 ):
-    share_refs, (whole_ref, copied_ref, sem) = refs[:-3], refs[-3:]
+    share_refs, whole_ref = refs[:-1], refs[-1]
     child_width = cols_ref.shape[1]
     targets = arrived_ref[:, child_width : child_width + 1].astype(jnp.int32)
     front = placed(front_ref[...], arrived_ref[:, :child_width], targets, cols_ref[...])
-    copied_ref[...] = front
-    copy = pltpu.make_async_copy(copied_ref, out_ref, sem)
-    copy.start()
+    out_ref[...] = front
     height = share_refs[0].shape[0]
     for k, ref in enumerate(share_refs):
         ref[...] = front[k * height : (k + 1) * height, :]
@@ -176,15 +186,16 @@
                 left = (j - 2 * first) * BLOCK
                 whole_ref[at : at + BLOCK, :] = product[i * BLOCK : (i + 1) * BLOCK, left : left + BLOCK]
     halves(core_ref, whole_ref, keep_ref, send_ref)
-    copy.wait()
-
-
-def product_kernel(core_ref, col_ref, front_ref, *refs):
-    shares, (panel_ref, keep_ref, send_ref, whole_ref) = refs[:-4], refs[-4:]
-    height, parts = shares[0].shape[0], len(shares)
-    for k, ref in enumerate(shares):
-        source = lax.rem(col_ref[0, 0] + (parts - k), jnp.int32(parts))
-        panel_ref[pl.ds(pl.multiple_of(source * height, height), height), :] = ref[...]
+
+
+def product_kernel(core_ref, front_ref, bundle_ref, panel_ref, keep_ref, send_ref, whole_ref):
+    parts = bundle_ref.shape[0]
+    height = panel_ref.shape[0] // parts
+    for k in range(parts):
+        for lanes in range(panel_ref.shape[1] // BLOCK):
+            panel_ref[k * height : (k + 1) * height, lanes * BLOCK : (lanes + 1) * BLOCK] = bundle_ref[
+                k, lanes * height : (lanes + 1) * height, :
+            ]
     whole_ref[...] = dot(panel_ref[...], front_ref[...], 0, 0)
     halves(core_ref, whole_ref, keep_ref, send_ref)
 
@@ -385,37 +396,29 @@
     front, keep, send, *shares = call(
         place_kernel, [f32(rows_dev, cols_dev), *halved] + [share] * parts,
         "place", 4 << 30, front_in, arrived, local_cols.reshape(1, child_width), scalars=(core,),
-        scratch=[
-            pltpu.VMEM((3 * PANELS, BLOCK), jnp.float32),
-            pltpu.VMEM((rows_dev, cols_dev), jnp.float32),
-            pltpu.SemaphoreType.DMA,
-        ],
-        outs=[HBM] + [VMEM] * (parts + 2),
+        scratch=[pltpu.VMEM((3 * PANELS, BLOCK), jnp.float32)],
     )
     half = summed(keep, swapped(send))
     half, shares = lax.optimization_barrier((half, shares))
     sent_shares = [lax.ppermute(shares[k], "col", [(0, k)]) for k in range(1, parts)]
-    panel_share = call(
-        choose_kernel, share, "choose", 1 << 20, shares[0], *sent_shares, scalars=(is_root,), vmem=4
-    )
     grams = exchange(split_rows(half, chips), ("z", "x"))
-    grams, panel_share = lax.optimization_barrier((grams, panel_share))
-    panel_shares = [panel_share] + [
-        lax.ppermute(panel_share, "col", [(i, (i + k) % parts) for i in range(parts)])
-        for k in range(1, parts)
-    ]
-
-    gram_share = exchange(folded(grams, parts), "col")
-    gram_share, panel_shares[5:] = lax.optimization_barrier((gram_share, panel_shares[5:]))
+    share_rows = rows_dev // parts * PANELS // BLOCK
+    gram_rows = grams.shape[1]
+    bundle = call(
+        bundle_kernel, f32(parts, share_rows + gram_rows, BLOCK), "bundle", 1 << 20,
+        grams, shares[0], *sent_shares, scalars=(is_root,), vmem=8,
+    )
+    bundle = exchange(bundle, "col")
     gram_share = call(
-        first_kernel, f32(chips, *gram_share.shape[1:]), "first", 1 << 20, gram_share, vmem=4
+        gram_kernel, f32(chips, gram_rows, BLOCK), "gram_share", 1 << 20, bundle, vmem=6
     )
     own_gram = merge_rows(exchange(gram_share, ("z", "x")))
     other_gram = swapped(own_gram)
 
     panel, keep, send = call(
         product_kernel, (f32(rows_dev, PANELS),) + (f32(PANELS // 2, cols_dev),) * 2,
-        "products", 2 << 30, front, *panel_shares, scalars=(core, col), scratch=[pltpu.VMEM((PANELS, cols_dev), jnp.float32)],
+        "products", 2 << 30, front, bundle, scalars=(core,),
+        scratch=[pltpu.VMEM((PANELS, cols_dev), jnp.float32)],
     )
     half = summed(keep, swapped(send))
     summands = exchange(split_rows(half, chips), ("z", "x"))

time: 209 us -> 189 us (0.904)
  blocking collectives: 0 us -> 32.7 us
  starting transfers between devices: 102 us -> 72.3 us
  waiting for transfers between devices: 61.4 us -> 39.4 us
    all_to_all x0 -> x1, blocking collectives: none -> 32.7 us  [exchange(): return lax.all_to_all(blocks, axis, split_axis=0, concat_axis=0, tiled=True)]
    ppermute x7 -> x0, starting transfers between devices: 26.9 us -> none  [on_device(): lax.ppermute(panel_share, 'col', [(i, (i + k) % parts) for i in range(par...]
    ppermute x7 -> x0, waiting for transfers between devices: 23.3 us -> none  [on_device(): lax.ppermute(panel_share, 'col', [(i, (i + k) % parts) for i in range(par...]
    all_to_all x6 -> x5, starting transfers between devices: 48.6 us -> 37.2 us  [exchange(): return lax.all_to_all(blocks, axis, split_axis=0, concat_axis=0, tiled=True)]
    ppermute x4, starting transfers between devices: 13.5 us -> 21.7 us  [swapped(): return lax.ppermute(x, 'core', [(0, 1), (1, 0)])]
    pallas_call x12 -> x11, Pallas kernels: 37.4 us -> 35.8 us  [call(): pl.pallas_call(kernel, out_shape=out_shape, in_specs=[SMEM] * len(scalars...]
    all_to_all x6 -> x5, waiting for transfers between devices: 30.2 us -> 31.5 us  [exchange(): return lax.all_to_all(blocks, axis, split_axis=0, concat_axis=0, tiled=True)]
  transfers between devices with their start and end apart: 24 -> 16, of which waited for: 13 -> 9; matrix products, arithmetic and copies ran while one was open for 0% -> 0% of each run, Pallas kernels for 11% -> 12%
where the time goes in v6:
time: 189 us; the launch traced here: 188 us
  starting transfers between devices  72.3 us (38%)
  waiting for transfers between devices  39.4 us (21%)
  Pallas kernels  35.8 us (19%)
  blocking collectives  32.7 us (17%)
  local copies, waits for them, and re-layouts  6.88 us (4%)
    all_to_all x5, starting transfers between devices, exchange(): return lax.all_to_all(blocks, axis, split_axis=0, concat_axis=0, tiled=True)  37.2 us
    pallas_call x11, Pallas kernels, call(): pl.pallas_call(kernel, out_shape=out_shape, in_specs=[SMEM] * len(scalars...  35.8 us
    all_to_all x1, blocking collectives, exchange(): return lax.all_to_all(blocks, axis, split_axis=0, concat_axis=0, tiled=True)  32.7 us
    all_to_all x5, waiting for transfers between devices, exchange(): return lax.all_to_all(blocks, axis, split_axis=0, concat_axis=0, tiled=True)  31.5 us
    ppermute x4, starting transfers between devices, swapped(): return lax.ppermute(x, 'core', [(0, 1), (1, 0)])  21.7 us
    ppermute x7, starting transfers between devices, on_device(): lax.ppermute(shares[k], 'col', [(0, k)])  13.3 us
    unnamed x24, local copies, waits for them, and re-layouts  6.88 us
    ppermute x7, waiting for transfers between devices, on_device(): lax.ppermute(shares[k], 'col', [(0, k)])  5.14 us
  transfers between devices with their start and end apart: 16, of which 9 were waited for; matrix products, arithmetic and copies ran while one was open for 0% of the time, Pallas kernels for 12%

profile of v6, /device:TPU:1, one launch (start us, length us, event | category | flops | bytes accessed | tf_op | source)
XLA Modules:
  0.0 188.3 jit_solution(12667326263970330908)
XLA Ops:
  0.7 2.1 %pack.1 = f32[512,384]{1,0:T(8,128)} custom-call(f32[512,256]{1,0:T(8,128)} %refs_0_.1, s32[4,128]{1,0:T(4,128)} %bitcast.18, s32[1,64]{1,0:T(1,128)} %refs_2_.1), custom_call_target="tpu_custom_call" | custom-call | flops 1048576 | bytes 4194304 | tf_op jit(solution)/shard_map/pack/pallas_call | solution.py:51
  2.7 14.8 %all-to-all-start = ((f32[64,8,384]{2,1,0:T(8,128)}), f32[64,8,384]{2,1,0:T(8,128)S(1)}, u32[]{:S(2)}, u32[]{:S(2)}) async-start(f32[64,8,384]{2,1,0:T(8,128)} %bitcast.15), calls=%async_computation | async-start | bytes 1572864 | tf_op jit(solution)/shard_map/all_to_all | solution.py:346
  17.6 22.7 %all-to-all-done = f32[64,8,384]{2,1,0:T(8,128)S(1)} async-done(((f32[64,8,384]{2,1,0:T(8,128)}), f32[64,8,384]{2,1,0:T(8,128)S(1)}, u32[]{:S(2)}, u32[]{:S(2)}) %all-to-all-start) | async-done | bytes 786464 | tf_op jit(solution)/shard_map/all_to_all | solution.py:346
  40.3 3.0 %place.1 = (f32[512,512]{1,0:T(8,128)S(1)}, f32[768,128]{1,0:T(8,128)S(1)}, f32[768,128]{1,0:T(8,128)S(1)}, f32[64,512]{1,0:T(8,128)S(1)}, f32[64,512]{1,0:T(8,1...) custom-call(s32[1,1]{1,0:T(1,128)} %bitcast.core_ref.refs_0_, ...), custom_call_target="tpu_custom_call" | custom-call | flops 4294967296 | bytes 4194304 | tf_op jit(solution)/shard_map/place/pallas_call | solution.py:51
  43.4 2.9 %collective-permute-start = (f32[768,128]{1,0:T(8,128)S(1)}, f32[768,128]{1,0:T(8,128)S(1)}, u32[]{:S(2)}, u32[]{:S(2)}) collective-permute-start(f32[768,128]{1,0:T(8,128)S(1)} %get-tuple-element.33), channel_id=1, source_target_pairs={{0,8},{8,0},{1,9},{9,1},{2,10},{10,2},{3,11},{11,3},{4,12},{12,4},... | collective-permute-start | bytes 1179656 | tf_op jit(solution)/shard_map/ppermute | solution.py:350
  48.4 4.8 %all-to-all-start.1 = ((f32[32,24,128]{2,1,0:T(8,128)}), f32[32,24,128]{2,1,0:T(8,128)S(1)}, u32[]{:S(2)}, u32[]{:S(2)}) async-start(f32[32,24,128]{2,1,0:T(8,128)} %bitcast.6), calls=%async_computation.1 | async-start | bytes 786432 | tf_op jit(solution)/shard_map/all_to_all | solution.py:346
  53.2 3.2 %collective-permute-start.1 = (f32[64,512]{1,0:T(8,128)S(1)}, f32[64,512]{1,0:T(8,128)S(1)}, u32[]{:S(2)}, u32[]{:S(2)}) collective-permute-start(f32[64,512]{1,0:T(8,128)S(1)} %get-tuple-element.44), channel_id=1, source_target_pairs={{0,1},{8,9},{16,17},{24,25},{32,33},{40,41},{48,49},{56,57},{64,65... | collective-permute-start | bytes 393224 | tf_op jit(solution)/shard_map/ppermute | solution.py:403
  56.4 1.7 collective-permute-start.2
  58.1 1.7 collective-permute-start.3
  59.8 2.9 %collective-permute-start.4 = (f32[64,512]{1,0:T(8,128)S(1)}, f32[64,512]{1,0:T(8,128)S(1)}, u32[]{:S(2)}, u32[]{:S(2)}) collective-permute-start(f32[64,512]{1,0:T(8,128)S(1)} %get-tuple-element.47), channel_id=1, source_target_pairs={{0,4},{8,12},{16,20},{24,28},{32,36},{40,44},{48,52},{56,60},{64,6... | collective-permute-start | bytes 393224 | tf_op jit(solution)/shard_map/ppermute | solution.py:403
  67.0 2.0 %collective-permute-done.6.refs_5_ = f32[64,512]{1,0:T(8,128)S(1)} collective-permute-done((f32[64,512]{1,0:T(8,128)S(1)}, f32[64,512]{1,0:T(8,128)S(1)}, u32[]{:S(2)}, u32[]{:S(2)}) %collective-permute-start.6) | collective-permute-done | bytes 131104 | tf_op jit(solution)/shard_map/ppermute | solution.py:403
  69.0 2.8 %collective-permute-done.7.refs_6_ = f32[64,512]{1,0:T(8,128)S(1)} collective-permute-done((f32[64,512]{1,0:T(8,128)S(1)}, f32[64,512]{1,0:T(8,128)S(1)}, u32[]{:S(2)}, u32[]{:S(2)}) %collective-permute-start.7) | collective-permute-done | bytes 131104 | tf_op jit(solution)/shard_map/ppermute | solution.py:403
  71.9 32.7 %all_to_all.30.bundle_ref = f32[8,280,128]{2,1,0:T(8,128)S(1)} all-to-all(f32[8,280,128]{2,1,0:T(8,128)S(1)} %bundle.1), channel_id=1, replica_groups=mesh['z'=8,'x'=4,'core'=2,'col'=8] {'col'}, dimensions={0} | all-to-all | bytes 2293760 | tf_op jit(solution)/shard_map/all_to_all | solution.py:346
  105.4 8.2 %all-to-all-start.4 = ((f32[32,24,128]{2,1,0:T(8,128)}), f32[32,24,128]{2,1,0:T(8,128)S(1)}, u32[]{:S(2)}, u32[]{:S(2)}) async-start(f32[32,24,128]{2,1,0:T(8,128)} %gram_share.1), calls=%async_computation.4 | async-start | bytes 786432 | tf_op jit(solution)/shard_map/all_to_all | solution.py:346
  114.8 2.0 %products.1 = (f32[512,512]{1,0:T(8,128)S(1)}, f32[256,512]{1,0:T(8,128)S(1)}, f32[256,512]{1,0:T(8,128)S(1)}) custom-call(s32[1,1]{1,0:T(1,128)} %bitcast.core_ref.refs_0_, f32[512,512]{1,0:T(8,128)S(1)} %copy-done.2, f32[8,280,128]{2,1,0:T(8,128)S(1)} %all_to_all.30.bundle_ref), custom_call_target="tpu_custom_call" | custom-call | flops 2147483648 | bytes 4194304 | tf_op jit(solution)/shard_map/products/pallas_call | solution.py:51
  117.8 6.2 %collective-permute-start.8 = (f32[256,512]{1,0:T(8,128)S(1)}, f32[256,512]{1,0:T(8,128)S(1)}, u32[]{:S(2)}, u32[]{:S(2)}) collective-permute-start(f32[256,512]{1,0:T(8,128)S(1)} %get-tuple-element.52), channel_id=1, source_target_pairs={{0,8},{8,0},{1,9},{9,1},{2,10},{10,2},{3,11},{11,3},{4,12},{12,4},... | collective-permute-start | bytes 1572872 | tf_op jit(solution)/shard_map/ppermute | solution.py:350
  125.1 7.4 %collective-permute-start.9 = (f32[768,128]{1,0:T(8,128)S(1)}, f32[768,128]{1,0:T(8,128)S(1)}, u32[]{:S(2)}, u32[]{:S(2)}) collective-permute-start(f32[768,128]{1,0:T(8,128)S(1)} %bitcast.11), channel_id=1, source_target_pairs={{0,8},{8,0},{1,9},{9,1},{2,10},{10,2},{3,11},{11,3},{4,12},{12,4},... | collective-permute-start | bytes 1179656 | tf_op jit(solution)/shard_map/ppermute | solution.py:350
  133.4 4.1 %all-to-all-start.3 = ((f32[32,8,512]{2,1,0:T(8,128)}), f32[32,8,512]{2,1,0:T(8,128)S(1)}, u32[]{:S(2)}, u32[]{:S(2)}) async-start(f32[32,8,512]{2,1,0:T(8,128)} %bitcast.7), calls=%async_computation.3 | async-start | bytes 1048576 | tf_op jit(solution)/shard_map/all_to_all | solution.py:346
  137.5 8.8 %factor0.1.refs_0_.refs_2_ = f32[256,768]{1,0:T(8,128)S(1)} custom-call(s32[1,1]{1,0:T(1,128)} %bitcast.core_ref.refs_0_, f32[768,128]{1,0:T(8,128)S(1)} %bitcast.12, f32[768,128]{1,0:T(8,128)S(1)} %collective-permute-done.9.refs_2_.other_ref), custom_call_target="tpu_custom_call" | custom-call | flops 10737418240 | bytes 4194304 | tf_op jit(solution)/shard_map/factor0/pallas_call | solution.py:51
  147.2 6.9 %all-to-all-done.3.x_ref = f32[32,8,512]{2,1,0:T(8,128)S(1)} async-done(((f32[32,8,512]{2,1,0:T(8,128)}), f32[32,8,512]{2,1,0:T(8,128)S(1)}, u32[]{:S(2)}, u32[]{:S(2)}) %all-to-all-start.3) | async-done | bytes 524320 | tf_op jit(solution)/shard_map/all_to_all | solution.py:346
  155.0 5.3 %all-to-all-start.5 = ((f32[32,8,512]{2,1,0:T(8,128)}), f32[32,8,512]{2,1,0:T(8,128)S(1)}, u32[]{:S(2)}, u32[]{:S(2)}) async-start(f32[32,8,512]{2,1,0:T(8,128)} %fold.1), calls=%async_computation.5 | async-start | bytes 1048576 | tf_op jit(solution)/shard_map/all_to_all | solution.py:346
  161.4 11.6 %factor1.1 = (f32[256,768]{1,0:T(8,128)S(1)}, f32[512,512]{1,0:T(8,128)S(1)}) custom-call(s32[1,1]{1,0:T(1,128)} %bitcast.core_ref.refs_0_, f32[768,128]{1,0:T(8,128)S(1)} %bitcast.13, f32[768,128]{1,0:T(8,128)S(1)} %collective-permute-done.9.refs_2_.other_ref, f32[512,512]{1,0:T(8,128)S(1)} %copy-done.4, f32[256,768]{1,0:T(8,128)S(1)} %copy-done.7), custom_call_target="tpu_custom_call" | custom-call | flops 12884901888 | bytes 4194304 | tf_op jit(solution)/shard_map/factor1/pallas_call | solution.py:51
  175.4 5.3 %collective-permute-start.10 = (f32[256,512]{1,0:T(8,128)S(1)}, f32[256,512]{1,0:T(8,128)S(1)}, u32[]{:S(2)}, u32[]{:S(2)}) collective-permute-start(f32[256,512]{1,0:T(8,128)S(1)} %bitcast.16), channel_id=1, source_target_pairs={{0,8},{8,0},{1,9},{9,1},{2,10},{10,2},{3,11},{11,3},{4,12},{12,4},... | collective-permute-start | bytes 1572872 | tf_op jit(solution)/shard_map/ppermute | solution.py:350
  183.0 5.0 %final.1 = (f32[512,512]{1,0:T(8,128)}, f32[512,512]{1,0:T(8,128)}) custom-call(s32[1,1]{1,0:T(1,128)} %bitcast.core_ref.refs_0_, s32[1,1]{1,0:T(1,128)} %bitcast.1.root_ref.refs_1_, f32[256,768]{1,0:T(8,128)} %copy-done.6, f32[256,768]{1,0:T(8,128)} %copy-done.8, f32[256,512]{1,0:T(8,128)} %bitcast.17, f32[256,512]{1,0:T(8,128)} %copy-done.11, ...), custom_call_target="tpu_custom_call" | custom-call | flops 4294967296 | bytes 4194304 | tf_op jit(solution)/shard_map/final/pallas_call | solution.py:51
  (45 shorter events, 19.2 us)
Async XLA Ops:
  0.6 17.0 %copy-start.10 = (s32[256]{0:T(256)S(1)}, s32[256]{0:T(256)}, u32[]{:S(2)}) copy-start(s32[256]{0:T(256)} %param.9) | copy-start | bytes 3076
  0.6 39.7 %copy-start = (f32[512,512]{1,0:T(8,128)S(1)}, f32[512,512]{1,0:T(8,128)}, u32[]{:S(2)}) copy-start(f32[512,512]{1,0:T(8,128)} %front_ref.1) | copy-start | bytes 3145732
  2.7 37.6 %all-to-all-start = ((f32[64,8,384]{2,1,0:T(8,128)}), f32[64,8,384]{2,1,0:T(8,128)S(1)}, u32[]{:S(2)}, u32[]{:S(2)}) async-start(f32[64,8,384]{2,1,0:T(8,128)} %bitcast.15), calls=%async_computation | async-start | bytes 1572864 | tf_op jit(solution)/shard_map/all_to_all | solution.py:346
  43.4 5.0 %copy-start.1 = (f32[512,512]{1,0:T(8,128)}, f32[512,512]{1,0:T(8,128)S(1)}, u32[]{:S(2)}) copy-start(f32[512,512]{1,0:T(8,128)S(1)} %get-tuple-element.31.front_ref.refs_7_) | copy-start | bytes 3145732
  43.4 4.2 %collective-permute-start = (f32[768,128]{1,0:T(8,128)S(1)}, f32[768,128]{1,0:T(8,128)S(1)}, u32[]{:S(2)}, u32[]{:S(2)}) collective-permute-start(f32[768,128]{1,0:T(8,128)S(1)} %get-tuple-element.33), channel_id=1, source_target_pairs={{0,8},{8,0},{1,9},{9,1},{2,10},{10,2},{3,11},{11,3},{4,12},{12,4},... | collective-permute-start | bytes 1179656 | tf_op jit(solution)/shard_map/ppermute | solution.py:350
  48.4 23.4 %all-to-all-start.1 = ((f32[32,24,128]{2,1,0:T(8,128)}), f32[32,24,128]{2,1,0:T(8,128)S(1)}, u32[]{:S(2)}, u32[]{:S(2)}) async-start(f32[32,24,128]{2,1,0:T(8,128)} %bitcast.6), calls=%async_computation.1 | async-start | bytes 786432 | tf_op jit(solution)/shard_map/all_to_all | solution.py:346
  53.2 10.8 %collective-permute-start.1 = (f32[64,512]{1,0:T(8,128)S(1)}, f32[64,512]{1,0:T(8,128)S(1)}, u32[]{:S(2)}, u32[]{:S(2)}) collective-permute-start(f32[64,512]{1,0:T(8,128)S(1)} %get-tuple-element.44), channel_id=1, source_target_pairs={{0,1},{8,9},{16,17},{24,25},{32,33},{40,41},{48,49},{56,57},{64,65... | collective-permute-start | bytes 393224 | tf_op jit(solution)/shard_map/ppermute | solution.py:403
  56.4 8.9 %collective-permute-start.2 = (f32[64,512]{1,0:T(8,128)S(1)}, f32[64,512]{1,0:T(8,128)S(1)}, u32[]{:S(2)}, u32[]{:S(2)}) collective-permute-start(f32[64,512]{1,0:T(8,128)S(1)} %get-tuple-element.45), channel_id=1, source_target_pairs={{0,2},{8,10},{16,18},{24,26},{32,34},{40,42},{48,50},{56,58},{64,6... | collective-permute-start | bytes 393224 | tf_op jit(solution)/shard_map/ppermute | solution.py:403
  58.1 8.5 %collective-permute-start.3 = (f32[64,512]{1,0:T(8,128)S(1)}, f32[64,512]{1,0:T(8,128)S(1)}, u32[]{:S(2)}, u32[]{:S(2)}) collective-permute-start(f32[64,512]{1,0:T(8,128)S(1)} %get-tuple-element.46), channel_id=1, source_target_pairs={{0,3},{8,11},{16,19},{24,27},{32,35},{40,43},{48,51},{56,59},{64,6... | collective-permute-start | bytes 393224 | tf_op jit(solution)/shard_map/ppermute | solution.py:403
  59.8 7.2 %collective-permute-start.4 = (f32[64,512]{1,0:T(8,128)S(1)}, f32[64,512]{1,0:T(8,128)S(1)}, u32[]{:S(2)}, u32[]{:S(2)}) collective-permute-start(f32[64,512]{1,0:T(8,128)S(1)} %get-tuple-element.47), channel_id=1, source_target_pairs={{0,4},{8,12},{16,20},{24,28},{32,36},{40,44},{48,52},{56,60},{64,6... | collective-permute-start | bytes 393224 | tf_op jit(solution)/shard_map/ppermute | solution.py:403
  62.7 4.3 %collective-permute-start.5 = (f32[64,512]{1,0:T(8,128)S(1)}, f32[64,512]{1,0:T(8,128)S(1)}, u32[]{:S(2)}, u32[]{:S(2)}) collective-permute-start(f32[64,512]{1,0:T(8,128)S(1)} %get-tuple-element.48), channel_id=1, source_target_pairs={{0,5},{8,13},{16,21},{24,29},{32,37},{40,45},{48,53},{56,61},{64,6... | collective-permute-start | bytes 393224 | tf_op jit(solution)/shard_map/ppermute | solution.py:403
  64.0 5.0 %collective-permute-start.6 = (f32[64,512]{1,0:T(8,128)S(1)}, f32[64,512]{1,0:T(8,128)S(1)}, u32[]{:S(2)}, u32[]{:S(2)}) collective-permute-start(f32[64,512]{1,0:T(8,128)S(1)} %get-tuple-element.49), channel_id=1, source_target_pairs={{0,6},{8,14},{16,22},{24,30},{32,38},{40,46},{48,54},{56,62},{64,7... | collective-permute-start | bytes 393224 | tf_op jit(solution)/shard_map/ppermute | solution.py:403
  65.3 6.5 %collective-permute-start.7 = (f32[64,512]{1,0:T(8,128)S(1)}, f32[64,512]{1,0:T(8,128)S(1)}, u32[]{:S(2)}, u32[]{:S(2)}) collective-permute-start(f32[64,512]{1,0:T(8,128)S(1)} %get-tuple-element.50), channel_id=1, source_target_pairs={{0,7},{8,15},{16,23},{24,31},{32,39},{40,47},{48,55},{56,63},{64,7... | collective-permute-start | bytes 393224 | tf_op jit(solution)/shard_map/ppermute | solution.py:403
  105.4 19.7 %all-to-all-start.4 = ((f32[32,24,128]{2,1,0:T(8,128)}), f32[32,24,128]{2,1,0:T(8,128)S(1)}, u32[]{:S(2)}, u32[]{:S(2)}) async-start(f32[32,24,128]{2,1,0:T(8,128)} %gram_share.1), calls=%async_computation.4 | async-start | bytes 786432 | tf_op jit(solution)/shard_map/all_to_all | solution.py:346
  113.6 1.2 copy-start.2
  116.8 1.0 copy-start.3
  117.8 14.8 %collective-permute-start.8 = (f32[256,512]{1,0:T(8,128)S(1)}, f32[256,512]{1,0:T(8,128)S(1)}, u32[]{:S(2)}, u32[]{:S(2)}) collective-permute-start(f32[256,512]{1,0:T(8,128)S(1)} %get-tuple-element.52), channel_id=1, source_target_pairs={{0,8},{8,0},{1,9},{9,1},{2,10},{10,2},{3,11},{11,3},{4,12},{12,4},... | collective-permute-start | bytes 1572872 | tf_op jit(solution)/shard_map/ppermute | solution.py:350
  125.1 12.3 %collective-permute-start.9 = (f32[768,128]{1,0:T(8,128)S(1)}, f32[768,128]{1,0:T(8,128)S(1)}, u32[]{:S(2)}, u32[]{:S(2)}) collective-permute-start(f32[768,128]{1,0:T(8,128)S(1)} %bitcast.11), channel_id=1, source_target_pairs={{0,8},{8,0},{1,9},{9,1},{2,10},{10,2},{3,11},{11,3},{4,12},{12,4},... | collective-permute-start | bytes 1179656 | tf_op jit(solution)/shard_map/ppermute | solution.py:350
  133.4 20.7 %all-to-all-start.3 = ((f32[32,8,512]{2,1,0:T(8,128)}), f32[32,8,512]{2,1,0:T(8,128)S(1)}, u32[]{:S(2)}, u32[]{:S(2)}) async-start(f32[32,8,512]{2,1,0:T(8,128)} %bitcast.7), calls=%async_computation.3 | async-start | bytes 1048576 | tf_op jit(solution)/shard_map/all_to_all | solution.py:346
  147.2 13.1 %copy-start.4 = (f32[512,512]{1,0:T(8,128)S(1)}, f32[512,512]{1,0:T(8,128)}, u32[]{:S(2)}) copy-start(f32[512,512]{1,0:T(8,128)} %copy-done.3) | copy-start | bytes 3145732
  155.0 20.4 %all-to-all-start.5 = ((f32[32,8,512]{2,1,0:T(8,128)}), f32[32,8,512]{2,1,0:T(8,128)S(1)}, u32[]{:S(2)}, u32[]{:S(2)}) async-start(f32[32,8,512]{2,1,0:T(8,128)} %fold.1), calls=%async_computation.5 | async-start | bytes 1048576 | tf_op jit(solution)/shard_map/all_to_all | solution.py:346
  160.3 1.1 copy-start.7
  175.4 6.8 %copy-start.9 = (f32[32,8,512]{2,1,0:T(8,128)}, f32[32,8,512]{2,1,0:T(8,128)S(1)}, u32[]{:S(2)}) copy-start(f32[32,8,512]{2,1,0:T(8,128)S(1)} %all-to-all-done.5) | copy-start | bytes 1572868
  175.4 6.8 %collective-permute-start.10 = (f32[256,512]{1,0:T(8,128)S(1)}, f32[256,512]{1,0:T(8,128)S(1)}, u32[]{:S(2)}, u32[]{:S(2)}) collective-permute-start(f32[256,512]{1,0:T(8,128)S(1)} %bitcast.16), channel_id=1, source_target_pairs={{0,8},{8,0},{1,9},{9,1},{2,10},{10,2},{3,11},{11,3},{4,12},{12,4},... | collective-permute-start | bytes 1572872 | tf_op jit(solution)/shard_map/ppermute | solution.py:350
  (4 other events, 3.6 us)

commit v7 on v6

--- a/solution.py
+++ b/solution.py
@@ -72,23 +72,23 @@
     return (iota((size, size), 0) == iota((size, size), 1)).astype(jnp.float32)
 
 
-def pack_kernel(height, capacity, child_hbm, rows_hbm, live_hbm, out_ref, rows_ref, live_ref, sems):
-    count, width = child_hbm.shape
+def pack_kernel(height, child_hbm, rows_hbm, live_hbm, out_ref, child_ref, rows_ref, live_ref, sems):
     copies = [
         pltpu.make_async_copy(live_hbm, live_ref, sems.at[0]),
         pltpu.make_async_copy(rows_hbm, rows_ref, sems.at[1]),
-        pltpu.make_async_copy(child_hbm, out_ref.at[:, pl.ds(0, width)], sems.at[2]),
+        pltpu.make_async_copy(child_hbm, child_ref, sems.at[2]),
     ]
     for copy in copies:
         copy.start()
     copies[0].wait()
     copies[1].wait()
+    count, width = child_ref.shape
     owners = live_ref.shape[1]
-    lanes = rows_ref.shape[1]
+    capacity, lanes = count // owners, rows_ref.shape[1]
     live = jnp.broadcast_to(live_ref[...].astype(jnp.float32), (count, owners))
     owner = lax.div(iota((count, owners), 0), jnp.int32(capacity))
     live = jnp.sum(jnp.where(owner == iota((count, owners), 1), live, 0.0), axis=1, keepdims=True)
-    slot = lax.rem(iota((count, 1), 0), jnp.int32(capacity)).astype(jnp.float32)
+    slot = lax.rem(iota((count, 1), 0), jnp.int32(capacity))
     local = lax.rem(rows_ref[...], jnp.int32(height)).astype(jnp.float32)
     identity = eye(lanes)
     rows = jnp.concatenate(
@@ -98,9 +98,46 @@
         ],
         axis=0,
     )
-    targets = jnp.where(slot < live, rows, -1.0)
-    out_ref[:, width:] = jnp.broadcast_to(targets, (count, BLOCK))
+    places = jnp.where(slot.astype(jnp.float32) < live, rows, -1.0)
+    spread = jnp.where(iota((count, lanes), 1) == slot, jnp.broadcast_to(places, (count, lanes)), 0.0)
+    places = jnp.sum(spread.reshape(owners, capacity, lanes), axis=1)
     copies[2].wait()
+    step = out_ref.shape[0] // owners
+    for s in range(owners):
+        for h in range(width // BLOCK):
+            at = s * step + h * capacity
+            out_ref[at : at + capacity, :] = child_ref[
+                s * capacity : (s + 1) * capacity, h * BLOCK : (h + 1) * BLOCK
+            ]
+        out_ref[s * step + step - 1 : s * step + step, :] = places[s : s + 1, :]
+
+
+def unpacked(ref, owners, capacity, width):
+    step = ref.shape[0] // owners
+    rows = jnp.concatenate(
+        [
+            jnp.concatenate(
+                [
+                    ref[s * step + h * capacity : s * step + (h + 1) * capacity, :]
+                    for s in range(owners)
+                ],
+                axis=0,
+            )
+            for h in range(width // BLOCK)
+        ],
+        axis=1,
+    )
+    shape = (owners * capacity, BLOCK)
+    places = jnp.concatenate(
+        [
+            jnp.broadcast_to(ref[s * step + step - 1 : s * step + step, :], (capacity, BLOCK))
+            for s in range(owners)
+        ],
+        axis=0,
+    )
+    own = iota(shape, 1) == lax.rem(iota(shape, 0), jnp.int32(capacity))
+    places = jnp.sum(jnp.where(own, places, 0.0), axis=1, keepdims=True)
+    return rows, places.astype(jnp.int32)
 
 
 def placed(front, rows, targets, cols):
@@ -166,12 +203,13 @@
 
 
 def place_kernel(
-    core_ref, front_ref, arrived_ref, cols_ref, out_ref, keep_ref, send_ref, *refs
+    owners, core_ref, front_ref, arrived_ref, cols_ref, out_ref, keep_ref, send_ref, *refs
 ):
     share_refs, whole_ref = refs[:-1], refs[-1]
-    child_width = cols_ref.shape[1]
-    targets = arrived_ref[:, child_width : child_width + 1].astype(jnp.int32)
-    front = placed(front_ref[...], arrived_ref[:, :child_width], targets, cols_ref[...])
+    width = cols_ref.shape[1]
+    capacity = (arrived_ref.shape[0] // owners - 1) // (width // BLOCK)
+    rows, places = unpacked(arrived_ref, owners, capacity, width)
+    front = placed(front_ref[...], rows, places, cols_ref[...])
     out_ref[...] = front
     height = share_refs[0].shape[0]
     for k, ref in enumerate(share_refs):
@@ -378,29 +416,31 @@
     halved = (f32(3 * PANELS // 2, BLOCK),) * 2
     local_cols = column_map % cols_dev
 
+    step = capacity * (child_width // BLOCK) + 1
     sent = call(
-        lambda *refs: pack_kernel(rows_dev, capacity, *refs),
-        f32(count, child_width + BLOCK), "pack", 1 << 20,
+        lambda *refs: pack_kernel(rows_dev, *refs), f32(owners * step, BLOCK), "pack", 1 << 20,
         child_block, child_rows.reshape(count // BLOCK, BLOCK), live_counts,
         ins=[HBM] * 3,
         vmem=56,
         scratch=[
+            pltpu.VMEM((count, child_width), jnp.float32),
             pltpu.VMEM((count // BLOCK, BLOCK), jnp.int32),
             pltpu.VMEM((1, owners), jnp.int32),
             pltpu.SemaphoreType.DMA((3,)),
         ],
     )
-    arrived = merge_rows(exchange(sent.reshape(owners, capacity, child_width + BLOCK), ROW))
+    arrived = exchange(sent.reshape(owners, step, 1, BLOCK), ROW).reshape(owners * step, BLOCK)
 
     share = f32(rows_dev // parts, cols_dev)
     front, keep, send, *shares = call(
-        place_kernel, [f32(rows_dev, cols_dev), *halved] + [share] * parts,
+        lambda *refs: place_kernel(owners, *refs), [f32(rows_dev, cols_dev), *halved] + [share] * parts,
         "place", 4 << 30, front_in, arrived, local_cols.reshape(1, child_width), scalars=(core,),
         scratch=[pltpu.VMEM((3 * PANELS, BLOCK), jnp.float32)],
     )
     half = summed(keep, swapped(send))
     half, shares = lax.optimization_barrier((half, shares))
-    sent_shares = [lax.ppermute(shares[k], "col", [(0, k)]) for k in range(1, parts)]
+    far_first = sorted(range(1, parts), key=lambda k: -min(k, parts - k))
+    sent_shares = [lax.ppermute(shares[k], "col", [(0, k)]) for k in far_first]
     grams = exchange(split_rows(half, chips), ("z", "x"))
     share_rows = rows_dev // parts * PANELS // BLOCK
     gram_rows = grams.shape[1]

time: 189 us -> 184 us (0.974)
  waiting for transfers between devices: 39.4 us -> 33 us
    all_to_all x5, waiting for transfers between devices: 31.5 us -> 27.4 us  [exchange(): return lax.all_to_all(blocks, axis, split_axis=0, concat_axis=0, tiled=True)]
    ppermute x7, waiting for transfers between devices: 5.14 us -> 2.74 us  [on_device(): sent_shares = [lax.ppermute(shares[k], 'col', [(0, k)]) for k in far_first]]
    ppermute x7, starting transfers between devices: 13.3 us -> 15.2 us  [on_device(): sent_shares = [lax.ppermute(shares[k], 'col', [(0, k)]) for k in far_first]]
  transfers between devices with their start and end apart: 16 -> 16, of which waited for: 9 -> 7; matrix products, arithmetic and copies ran while one was open for 0% -> 0% of each run, Pallas kernels for 12% -> 13%
where the time goes in v7:
time: 184 us; the launch traced here: 183 us
  starting transfers between devices  72.9 us (40%)
  Pallas kernels  35.8 us (19%)
  blocking collectives  33.4 us (18%)
  waiting for transfers between devices  33 us (18%)
  local copies, waits for them, and re-layouts  6.88 us (4%)
    all_to_all x5, starting transfers between devices, exchange(): return lax.all_to_all(blocks, axis, split_axis=0, concat_axis=0, tiled=True)  37.2 us
    pallas_call x11, Pallas kernels, call(): pl.pallas_call(kernel, out_shape=out_shape, in_specs=[SMEM] * len(scalars...  35.8 us
    all_to_all x1, blocking collectives, exchange(): return lax.all_to_all(blocks, axis, split_axis=0, concat_axis=0, tiled=True)  33.4 us
    all_to_all x5, waiting for transfers between devices, exchange(): return lax.all_to_all(blocks, axis, split_axis=0, concat_axis=0, tiled=True)  27.4 us
    ppermute x4, starting transfers between devices, swapped(): return lax.ppermute(x, 'core', [(0, 1), (1, 0)])  20.4 us
    ppermute x7, starting transfers between devices, on_device(): sent_shares = [lax.ppermute(shares[k], 'col', [(0, k)]) for k in far_first]  15.2 us
    unnamed x24, local copies, waits for them, and re-layouts  6.88 us
  transfers between devices with their start and end apart: 16, of which 7 were waited for; matrix products, arithmetic and copies ran while one was open for 0% of the time, Pallas kernels for 13%

profile of v7, /device:TPU:1, one launch (start us, length us, event | category | flops | bytes accessed | tf_op | source)
XLA Modules:
  0.0 183.1 jit_solution(15935759958279474070)
XLA Ops:
  0.7 2.0 %pack.1 = f32[1088,128]{1,0:T(8,128)} custom-call(f32[512,256]{1,0:T(8,128)} %refs_0_.1, s32[4,128]{1,0:T(4,128)} %bitcast.18, s32[1,64]{1,0:T(1,128)} %refs_2_.1), custom_call_target="tpu_custom_call" | custom-call | flops 1048576 | bytes 4194304 | tf_op jit(solution)/shard_map/pack/pallas_call | solution.py:51
  2.7 14.8 %all-to-all-start = ((f32[64,17,1,128]{3,2,1,0:T(1,128)}), f32[64,17,1,128]{3,2,1,0:T(1,128)S(1)}, u32[]{:S(2)}, u32[]{:S(2)}) async-start(f32[64,17,1,128]{3,2,1,0:T(1,128)} %bitcast.15), calls=%async_computation | async-start | bytes 1114112 | tf_op jit(solution)/shard_map/all_to_all | solution.py:384
  17.6 18.4 %all-to-all-done = f32[64,17,1,128]{3,2,1,0:T(1,128)S(1)} async-done(((f32[64,17,1,128]{3,2,1,0:T(1,128)}), f32[64,17,1,128]{3,2,1,0:T(1,128)S(1)}, u32[]{:S(2)}, u32[]{:S(2)}) %all-to-all-start) | async-done | bytes 557088 | tf_op jit(solution)/shard_map/all_to_all | solution.py:384
  35.9 3.0 %place.1 = (f32[512,512]{1,0:T(8,128)S(1)}, f32[768,128]{1,0:T(8,128)S(1)}, f32[768,128]{1,0:T(8,128)S(1)}, f32[64,512]{1,0:T(8,128)S(1)}, f32[64,512]{1,0:T(8,1...) custom-call(s32[1,1]{1,0:T(1,128)} %bitcast.refs_0_.core_ref, ...), custom_call_target="tpu_custom_call" | custom-call | flops 4294967296 | bytes 4194304 | tf_op jit(solution)/shard_map/place/pallas_call | solution.py:51
  39.0 2.3 %collective-permute-start = (f32[768,128]{1,0:T(8,128)S(1)}, f32[768,128]{1,0:T(8,128)S(1)}, u32[]{:S(2)}, u32[]{:S(2)}) collective-permute-start(f32[768,128]{1,0:T(8,128)S(1)} %get-tuple-element.33), channel_id=1, source_target_pairs={{0,8},{8,0},{1,9},{9,1},{2,10},{10,2},{3,11},{11,3},{4,12},{12,4},... | collective-permute-start | bytes 1179656 | tf_op jit(solution)/shard_map/ppermute | solution.py:388
  41.3 1.3 collective-permute-done.b_ref
  43.5 4.9 %all-to-all-start.1 = ((f32[32,24,128]{2,1,0:T(8,128)}), f32[32,24,128]{2,1,0:T(8,128)S(1)}, u32[]{:S(2)}, u32[]{:S(2)}) async-start(f32[32,24,128]{2,1,0:T(8,128)} %bitcast.6), calls=%async_computation.1 | async-start | bytes 786432 | tf_op jit(solution)/shard_map/all_to_all | solution.py:384
  48.3 7.5 %collective-permute-start.1 = (f32[64,512]{1,0:T(8,128)S(1)}, f32[64,512]{1,0:T(8,128)S(1)}, u32[]{:S(2)}, u32[]{:S(2)}) collective-permute-start(f32[64,512]{1,0:T(8,128)S(1)} %get-tuple-element.44), channel_id=1, source_target_pairs={{0,4},{8,12},{16,20},{24,28},{32,36},{40,44},{48,52},{56,60},{64,6... | collective-permute-start | bytes 393224 | tf_op jit(solution)/shard_map/ppermute | solution.py:443
  57.1 1.3 collective-permute-start.3
  63.7 2.7 %collective-permute-done.6.refs_5_ = f32[64,512]{1,0:T(8,128)S(1)} collective-permute-done((f32[64,512]{1,0:T(8,128)S(1)}, f32[64,512]{1,0:T(8,128)S(1)}, u32[]{:S(2)}, u32[]{:S(2)}) %collective-permute-start.6) | collective-permute-done | bytes 131104 | tf_op jit(solution)/shard_map/ppermute | solution.py:443
  66.5 33.4 %all_to_all.30.bundle_ref = f32[8,280,128]{2,1,0:T(8,128)S(1)} all-to-all(f32[8,280,128]{2,1,0:T(8,128)S(1)} %bundle.1), channel_id=1, replica_groups=mesh['z'=8,'x'=4,'core'=2,'col'=8] {'col'}, dimensions={0} | all-to-all | bytes 2293760 | tf_op jit(solution)/shard_map/all_to_all | solution.py:384
  100.7 8.1 %all-to-all-start.4 = ((f32[32,24,128]{2,1,0:T(8,128)}), f32[32,24,128]{2,1,0:T(8,128)S(1)}, u32[]{:S(2)}, u32[]{:S(2)}) async-start(f32[32,24,128]{2,1,0:T(8,128)} %gram_share.1), calls=%async_computation.4 | async-start | bytes 786432 | tf_op jit(solution)/shard_map/all_to_all | solution.py:384
  110.0 2.0 %products.1 = (f32[512,512]{1,0:T(8,128)S(1)}, f32[256,512]{1,0:T(8,128)S(1)}, f32[256,512]{1,0:T(8,128)S(1)}) custom-call(s32[1,1]{1,0:T(1,128)} %bitcast.refs_0_.core_ref, f32[512,512]{1,0:T(8,128)S(1)} %copy-done.2, f32[8,280,128]{2,1,0:T(8,128)S(1)} %all_to_all.30.bundle_ref), custom_call_target="tpu_custom_call" | custom-call | flops 2147483648 | bytes 4194304 | tf_op jit(solution)/shard_map/products/pallas_call | solution.py:51
  113.0 5.8 %collective-permute-start.8 = (f32[256,512]{1,0:T(8,128)S(1)}, f32[256,512]{1,0:T(8,128)S(1)}, u32[]{:S(2)}, u32[]{:S(2)}) collective-permute-start(f32[256,512]{1,0:T(8,128)S(1)} %get-tuple-element.52), channel_id=1, source_target_pairs={{0,8},{8,0},{1,9},{9,1},{2,10},{10,2},{3,11},{11,3},{4,12},{12,4},... | collective-permute-start | bytes 1572872 | tf_op jit(solution)/shard_map/ppermute | solution.py:388
  118.8 1.6 all-to-all-done.4
  120.4 7.0 %collective-permute-start.9 = (f32[768,128]{1,0:T(8,128)S(1)}, f32[768,128]{1,0:T(8,128)S(1)}, u32[]{:S(2)}, u32[]{:S(2)}) collective-permute-start(f32[768,128]{1,0:T(8,128)S(1)} %bitcast.11), channel_id=1, source_target_pairs={{0,8},{8,0},{1,9},{9,1},{2,10},{10,2},{3,11},{11,3},{4,12},{12,4},... | collective-permute-start | bytes 1179656 | tf_op jit(solution)/shard_map/ppermute | solution.py:388
  128.2 4.1 %all-to-all-start.3 = ((f32[32,8,512]{2,1,0:T(8,128)}), f32[32,8,512]{2,1,0:T(8,128)S(1)}, u32[]{:S(2)}, u32[]{:S(2)}) async-start(f32[32,8,512]{2,1,0:T(8,128)} %bitcast.7), calls=%async_computation.3 | async-start | bytes 1048576 | tf_op jit(solution)/shard_map/all_to_all | solution.py:384
  132.3 8.8 %factor0.1.refs_0_.refs_2_ = f32[256,768]{1,0:T(8,128)S(1)} custom-call(s32[1,1]{1,0:T(1,128)} %bitcast.refs_0_.core_ref, f32[768,128]{1,0:T(8,128)S(1)} %bitcast.12, f32[768,128]{1,0:T(8,128)S(1)} %collective-permute-done.9.refs_2_.other_ref), custom_call_target="tpu_custom_call" | custom-call | flops 10737418240 | bytes 4194304 | tf_op jit(solution)/shard_map/factor0/pallas_call | solution.py:51
  142.0 6.9 %all-to-all-done.3.x_ref = f32[32,8,512]{2,1,0:T(8,128)S(1)} async-done(((f32[32,8,512]{2,1,0:T(8,128)}), f32[32,8,512]{2,1,0:T(8,128)S(1)}, u32[]{:S(2)}, u32[]{:S(2)}) %all-to-all-start.3) | async-done | bytes 524320 | tf_op jit(solution)/shard_map/all_to_all | solution.py:384
  149.8 5.3 %all-to-all-start.5 = ((f32[32,8,512]{2,1,0:T(8,128)}), f32[32,8,512]{2,1,0:T(8,128)S(1)}, u32[]{:S(2)}, u32[]{:S(2)}) async-start(f32[32,8,512]{2,1,0:T(8,128)} %fold.1), calls=%async_computation.5 | async-start | bytes 1048576 | tf_op jit(solution)/shard_map/all_to_all | solution.py:384
  156.2 11.6 %factor1.1 = (f32[256,768]{1,0:T(8,128)S(1)}, f32[512,512]{1,0:T(8,128)S(1)}) custom-call(s32[1,1]{1,0:T(1,128)} %bitcast.refs_0_.core_ref, f32[768,128]{1,0:T(8,128)S(1)} %bitcast.13, f32[768,128]{1,0:T(8,128)S(1)} %collective-permute-done.9.refs_2_.other_ref, f32[512,512]{1,0:T(8,128)S(1)} %copy-done.4, f32[256,768]{1,0:T(8,128)S(1)} %copy-done.7), custom_call_target="tpu_custom_call" | custom-call | flops 12884901888 | bytes 4194304 | tf_op jit(solution)/shard_map/factor1/pallas_call | solution.py:51
  170.3 5.3 %collective-permute-start.10 = (f32[256,512]{1,0:T(8,128)S(1)}, f32[256,512]{1,0:T(8,128)S(1)}, u32[]{:S(2)}, u32[]{:S(2)}) collective-permute-start(f32[256,512]{1,0:T(8,128)S(1)} %bitcast.16), channel_id=1, source_target_pairs={{0,8},{8,0},{1,9},{9,1},{2,10},{10,2},{3,11},{11,3},{4,12},{12,4},... | collective-permute-start | bytes 1572872 | tf_op jit(solution)/shard_map/ppermute | solution.py:388
  175.5 1.5 collective-permute-done.10.refs_5_
  177.9 5.0 %final.1 = (f32[512,512]{1,0:T(8,128)}, f32[512,512]{1,0:T(8,128)}) custom-call(s32[1,1]{1,0:T(1,128)} %bitcast.refs_0_.core_ref, s32[1,1]{1,0:T(1,128)} %bitcast.1.root_ref.refs_1_, f32[256,768]{1,0:T(8,128)} %copy-done.6, f32[256,768]{1,0:T(8,128)} %copy-done.8, f32[256,512]{1,0:T(8,128)} %bitcast.17, f32[256,512]{1,0:T(8,128)} %copy-done.11, ...), custom_call_target="tpu_custom_call" | custom-call | flops 4294967296 | bytes 4194304 | tf_op jit(solution)/shard_map/final/pallas_call | solution.py:51
  (45 shorter events, 17.4 us)
Async XLA Ops:
  0.6 16.9 %copy-start.10 = (s32[256]{0:T(256)S(1)}, s32[256]{0:T(256)}, u32[]{:S(2)}) copy-start(s32[256]{0:T(256)} %param.9) | copy-start | bytes 3076
  0.6 35.3 %copy-start = (f32[512,512]{1,0:T(8,128)S(1)}, f32[512,512]{1,0:T(8,128)}, u32[]{:S(2)}) copy-start(f32[512,512]{1,0:T(8,128)} %refs_1_.1) | copy-start | bytes 3145732
  2.7 33.2 %all-to-all-start = ((f32[64,17,1,128]{3,2,1,0:T(1,128)}), f32[64,17,1,128]{3,2,1,0:T(1,128)S(1)}, u32[]{:S(2)}, u32[]{:S(2)}) async-start(f32[64,17,1,128]{3,2,1,0:T(1,128)} %bitcast.15), calls=%async_computation | async-start | bytes 1114112 | tf_op jit(solution)/shard_map/all_to_all | solution.py:384
  39.0 4.5 %copy-start.1 = (f32[512,512]{1,0:T(8,128)}, f32[512,512]{1,0:T(8,128)S(1)}, u32[]{:S(2)}) copy-start(f32[512,512]{1,0:T(8,128)S(1)} %get-tuple-element.31.front_ref.refs_7_) | copy-start | bytes 3145732
  39.0 3.7 %collective-permute-start = (f32[768,128]{1,0:T(8,128)S(1)}, f32[768,128]{1,0:T(8,128)S(1)}, u32[]{:S(2)}, u32[]{:S(2)}) collective-permute-start(f32[768,128]{1,0:T(8,128)S(1)} %get-tuple-element.33), channel_id=1, source_target_pairs={{0,8},{8,0},{1,9},{9,1},{2,10},{10,2},{3,11},{11,3},{4,12},{12,4},... | collective-permute-start | bytes 1179656 | tf_op jit(solution)/shard_map/ppermute | solution.py:388
  43.5 23.0 %all-to-all-start.1 = ((f32[32,24,128]{2,1,0:T(8,128)}), f32[32,24,128]{2,1,0:T(8,128)S(1)}, u32[]{:S(2)}, u32[]{:S(2)}) async-start(f32[32,24,128]{2,1,0:T(8,128)} %bitcast.6), calls=%async_computation.1 | async-start | bytes 786432 | tf_op jit(solution)/shard_map/all_to_all | solution.py:384
  48.3 12.7 %collective-permute-start.1 = (f32[64,512]{1,0:T(8,128)S(1)}, f32[64,512]{1,0:T(8,128)S(1)}, u32[]{:S(2)}, u32[]{:S(2)}) collective-permute-start(f32[64,512]{1,0:T(8,128)S(1)} %get-tuple-element.44), channel_id=1, source_target_pairs={{0,4},{8,12},{16,20},{24,28},{32,36},{40,44},{48,52},{56,60},{64,6... | collective-permute-start | bytes 393224 | tf_op jit(solution)/shard_map/ppermute | solution.py:443
  55.8 6.5 %collective-permute-start.2 = (f32[64,512]{1,0:T(8,128)S(1)}, f32[64,512]{1,0:T(8,128)S(1)}, u32[]{:S(2)}, u32[]{:S(2)}) collective-permute-start(f32[64,512]{1,0:T(8,128)S(1)} %get-tuple-element.45), channel_id=1, source_target_pairs={{0,3},{8,11},{16,19},{24,27},{32,35},{40,43},{48,51},{56,59},{64,6... | collective-permute-start | bytes 393224 | tf_op jit(solution)/shard_map/ppermute | solution.py:443
  57.1 6.6 %collective-permute-start.3 = (f32[64,512]{1,0:T(8,128)S(1)}, f32[64,512]{1,0:T(8,128)S(1)}, u32[]{:S(2)}, u32[]{:S(2)}) collective-permute-start(f32[64,512]{1,0:T(8,128)S(1)} %get-tuple-element.46), channel_id=1, source_target_pairs={{0,5},{8,13},{16,21},{24,29},{32,37},{40,45},{48,53},{56,61},{64,6... | collective-permute-start | bytes 393224 | tf_op jit(solution)/shard_map/ppermute | solution.py:443
  58.4 5.3 %collective-permute-start.4 = (f32[64,512]{1,0:T(8,128)S(1)}, f32[64,512]{1,0:T(8,128)S(1)}, u32[]{:S(2)}, u32[]{:S(2)}) collective-permute-start(f32[64,512]{1,0:T(8,128)S(1)} %get-tuple-element.47), channel_id=1, source_target_pairs={{0,2},{8,10},{16,18},{24,26},{32,34},{40,42},{48,50},{56,58},{64,6... | collective-permute-start | bytes 393224 | tf_op jit(solution)/shard_map/ppermute | solution.py:443
  59.7 4.0 %collective-permute-start.5 = (f32[64,512]{1,0:T(8,128)S(1)}, f32[64,512]{1,0:T(8,128)S(1)}, u32[]{:S(2)}, u32[]{:S(2)}) collective-permute-start(f32[64,512]{1,0:T(8,128)S(1)} %get-tuple-element.48), channel_id=1, source_target_pairs={{0,6},{8,14},{16,22},{24,30},{32,38},{40,46},{48,54},{56,62},{64,7... | collective-permute-start | bytes 393224 | tf_op jit(solution)/shard_map/ppermute | solution.py:443
  61.0 5.4 %collective-permute-start.6 = (f32[64,512]{1,0:T(8,128)S(1)}, f32[64,512]{1,0:T(8,128)S(1)}, u32[]{:S(2)}, u32[]{:S(2)}) collective-permute-start(f32[64,512]{1,0:T(8,128)S(1)} %get-tuple-element.49), channel_id=1, source_target_pairs={{0,1},{8,9},{16,17},{24,25},{32,33},{40,41},{48,49},{56,57},{64,65... | collective-permute-start | bytes 393224 | tf_op jit(solution)/shard_map/ppermute | solution.py:443
  62.3 4.1 %collective-permute-start.7 = (f32[64,512]{1,0:T(8,128)S(1)}, f32[64,512]{1,0:T(8,128)S(1)}, u32[]{:S(2)}, u32[]{:S(2)}) collective-permute-start(f32[64,512]{1,0:T(8,128)S(1)} %get-tuple-element.50), channel_id=1, source_target_pairs={{0,7},{8,15},{16,23},{24,31},{32,39},{40,47},{48,55},{56,63},{64,7... | collective-permute-start | bytes 393224 | tf_op jit(solution)/shard_map/ppermute | solution.py:443
  100.7 19.7 %all-to-all-start.4 = ((f32[32,24,128]{2,1,0:T(8,128)}), f32[32,24,128]{2,1,0:T(8,128)S(1)}, u32[]{:S(2)}, u32[]{:S(2)}) async-start(f32[32,24,128]{2,1,0:T(8,128)} %gram_share.1), calls=%async_computation.4 | async-start | bytes 786432 | tf_op jit(solution)/shard_map/all_to_all | solution.py:384
  108.8 1.2 copy-start.2
  112.0 1.0 copy-start.3
  113.0 14.4 %collective-permute-start.8 = (f32[256,512]{1,0:T(8,128)S(1)}, f32[256,512]{1,0:T(8,128)S(1)}, u32[]{:S(2)}, u32[]{:S(2)}) collective-permute-start(f32[256,512]{1,0:T(8,128)S(1)} %get-tuple-element.52), channel_id=1, source_target_pairs={{0,8},{8,0},{1,9},{9,1},{2,10},{10,2},{3,11},{11,3},{4,12},{12,4},... | collective-permute-start | bytes 1572872 | tf_op jit(solution)/shard_map/ppermute | solution.py:388
  120.4 11.9 %collective-permute-start.9 = (f32[768,128]{1,0:T(8,128)S(1)}, f32[768,128]{1,0:T(8,128)S(1)}, u32[]{:S(2)}, u32[]{:S(2)}) collective-permute-start(f32[768,128]{1,0:T(8,128)S(1)} %bitcast.11), channel_id=1, source_target_pairs={{0,8},{8,0},{1,9},{9,1},{2,10},{10,2},{3,11},{11,3},{4,12},{12,4},... | collective-permute-start | bytes 1179656 | tf_op jit(solution)/shard_map/ppermute | solution.py:388
  128.2 20.6 %all-to-all-start.3 = ((f32[32,8,512]{2,1,0:T(8,128)}), f32[32,8,512]{2,1,0:T(8,128)S(1)}, u32[]{:S(2)}, u32[]{:S(2)}) async-start(f32[32,8,512]{2,1,0:T(8,128)} %bitcast.7), calls=%async_computation.3 | async-start | bytes 1048576 | tf_op jit(solution)/shard_map/all_to_all | solution.py:384
  142.0 13.1 %copy-start.4 = (f32[512,512]{1,0:T(8,128)S(1)}, f32[512,512]{1,0:T(8,128)}, u32[]{:S(2)}) copy-start(f32[512,512]{1,0:T(8,128)} %copy-done.3) | copy-start | bytes 3145732
  149.8 20.5 %all-to-all-start.5 = ((f32[32,8,512]{2,1,0:T(8,128)}), f32[32,8,512]{2,1,0:T(8,128)S(1)}, u32[]{:S(2)}, u32[]{:S(2)}) async-start(f32[32,8,512]{2,1,0:T(8,128)} %fold.1), calls=%async_computation.5 | async-start | bytes 1048576 | tf_op jit(solution)/shard_map/all_to_all | solution.py:384
  155.1 1.1 copy-start.7
  170.3 6.8 %copy-start.9 = (f32[32,8,512]{2,1,0:T(8,128)}, f32[32,8,512]{2,1,0:T(8,128)S(1)}, u32[]{:S(2)}) copy-start(f32[32,8,512]{2,1,0:T(8,128)S(1)} %all-to-all-done.5) | copy-start | bytes 1572868
  170.3 6.8 %collective-permute-start.10 = (f32[256,512]{1,0:T(8,128)S(1)}, f32[256,512]{1,0:T(8,128)S(1)}, u32[]{:S(2)}, u32[]{:S(2)}) collective-permute-start(f32[256,512]{1,0:T(8,128)S(1)} %bitcast.16), channel_id=1, source_target_pairs={{0,8},{8,0},{1,9},{9,1},{2,10},{10,2},{3,11},{11,3},{4,12},{12,4},... | collective-permute-start | bytes 1572872 | tf_op jit(solution)/shard_map/ppermute | solution.py:388
  (4 other events, 3.6 us)

commit v8 on v7

--- a/solution.py
+++ b/solution.py
@@ -152,18 +152,29 @@
     return total
 
 
-def bundle_kernel(root_ref, grams_ref, own_ref, *refs):
+def bundle_kernel(root_ref, own_ref, *refs):
     arrived, out_ref = refs[:-1], refs[-1]
-    share = total([ref[...] for ref in arrived])
-    share = jnp.where(root_ref[0, 0] == 1, own_ref[...], share)
-    gram = total([grams_ref[i] for i in range(grams_ref.shape[0])])
-    height = share.shape[0]
+    share = jnp.where(root_ref[0, 0] == 1, own_ref[...], total([ref[...] for ref in arrived]))
     for i in range(out_ref.shape[0]):
-        for lanes in range(share.shape[1] // BLOCK):
-            out_ref[i, lanes * height : (lanes + 1) * height, :] = share[
-                :, lanes * BLOCK : (lanes + 1) * BLOCK
-            ]
-        out_ref[i, share.shape[1] // BLOCK * height :, :] = gram
+        out_ref[i] = share
+
+
+def gram_share_kernel(grams_ref, out_ref):
+    out_ref[...] = total([grams_ref[i] for i in range(grams_ref.shape[0])])
+
+
+def chosen_kernel(root_ref, own_ref, *refs):
+    arrived, out_ref = refs[:-1], refs[-1]
+    out_ref[...] = jnp.where(root_ref[0, 0] == 1, own_ref[...], total([ref[...] for ref in arrived]))
+
+
+def line_kernel(x_ref, *refs):
+    shares, out_ref = refs[:-1], refs[-1]
+    height, n = shares[0].shape[0], len(shares)
+    for k, ref in enumerate(shares):
+        source = lax.rem(x_ref[0, 0] + (n - k), jnp.int32(n))
+        for i in range(out_ref.shape[0]):
+            out_ref[i, pl.ds(pl.multiple_of(source * height, 8), height), :] = ref[...]
 
 
 def total(terms):
@@ -181,12 +192,6 @@
     x = total([x_ref[i] for i in range(x_ref.shape[0])])
     for i in range(out_ref.shape[0]):
         out_ref[i] = x
-
-
-def gram_kernel(bundle_ref, out_ref):
-    height = out_ref.shape[1]
-    for i in range(out_ref.shape[0]):
-        out_ref[i] = bundle_ref[0, bundle_ref.shape[1] - height :, :]
 
 
 def halves(core_ref, whole_ref, keep_ref, send_ref):
@@ -230,10 +235,7 @@
     parts = bundle_ref.shape[0]
     height = panel_ref.shape[0] // parts
     for k in range(parts):
-        for lanes in range(panel_ref.shape[1] // BLOCK):
-            panel_ref[k * height : (k + 1) * height, lanes * BLOCK : (lanes + 1) * BLOCK] = bundle_ref[
-                k, lanes * height : (lanes + 1) * height, :
-            ]
+        panel_ref[k * height : (k + 1) * height, :] = bundle_ref[k]
     whole_ref[...] = dot(panel_ref[...], front_ref[...], 0, 0)
     halves(core_ref, whole_ref, keep_ref, send_ref)
 
@@ -442,18 +444,28 @@
     far_first = sorted(range(1, parts), key=lambda k: -min(k, parts - k))
     sent_shares = [lax.ppermute(shares[k], "col", [(0, k)]) for k in far_first]
     grams = exchange(split_rows(half, chips), ("z", "x"))
-    share_rows = rows_dev // parts * PANELS // BLOCK
-    gram_rows = grams.shape[1]
     bundle = call(
-        bundle_kernel, f32(parts, share_rows + gram_rows, BLOCK), "bundle", 1 << 20,
-        grams, shares[0], *sent_shares, scalars=(is_root,), vmem=8,
-    )
+        bundle_kernel, f32(parts, rows_dev // parts, PANELS), "bundle", 1 << 20,
+        shares[0], *sent_shares, scalars=(is_root,), vmem=8,
+    )
+    grams, bundle = lax.optimization_barrier((grams, bundle))
     bundle = exchange(bundle, "col")
-    gram_share = call(
-        gram_kernel, f32(chips, gram_rows, BLOCK), "gram_share", 1 << 20, bundle, vmem=6
-    )
-    own_gram = merge_rows(exchange(gram_share, ("z", "x")))
-    other_gram = swapped(own_gram)
+    gram_share = f32(*grams.shape[1:])
+    reduced = call(gram_share_kernel, gram_share, "gram_share", 1 << 20, grams, vmem=6)
+    sent_grams = [lax.ppermute(reduced, "col", [(0, k)]) for k in far_first]
+    reduced = call(
+        chosen_kernel, gram_share, "chosen", 1 << 20, reduced, *sent_grams, scalars=(is_root,), vmem=4
+    )
+    line, column = lax.axis_size("x"), lax.axis_size("z")
+    along_x = [reduced] + [
+        lax.ppermute(reduced, "x", [(i, (i + k) % line) for i in range(line)]) for k in range(1, line)
+    ]
+    gram_line = call(
+        line_kernel, f32(column, line * grams.shape[1], BLOCK), "line", 1 << 20, *along_x,
+        scalars=(lax.axis_index("x").astype(jnp.int32),), vmem=6,
+    )
+    bundle, gram_line = lax.optimization_barrier((bundle, gram_line))
+    own_gram = merge_rows(exchange(gram_line, "z"))
 
     panel, keep, send = call(
         product_kernel, (f32(rows_dev, PANELS),) + (f32(PANELS // 2, cols_dev),) * 2,
@@ -461,6 +473,8 @@
         scratch=[pltpu.VMEM((PANELS, cols_dev), jnp.float32)],
     )
     half = summed(keep, swapped(send))
+    half, own_gram = lax.optimization_barrier((half, own_gram))
+    other_gram = swapped(own_gram)
     summands = exchange(split_rows(half, chips), ("z", "x"))
 
     block_shape = f32(PANELS // PIECES, 3 * PANELS // 2)

time: 184 us -> 189 us (1.027)
  blocking collectives: 33.4 us -> 0 us
  starting transfers between devices: 72.9 us -> 99.4 us
  waiting for transfers between devices: 33 us -> 43.8 us
    all_to_all x1 -> x0, blocking collectives: 33.4 us -> none  [exchange(): return lax.all_to_all(blocks, axis, split_axis=0, concat_axis=0, tiled=True)]
    ppermute x0 -> x10, starting transfers between devices: none -> 21.1 us  [the longest x7 12.4 us: on_device(): sent_grams = [lax.ppermute(reduced, 'col', [(0, k)]) for k in far_first]]
    ppermute x0 -> x10, waiting for transfers between devices: none -> 11.6 us  [the longest x7 8.42 us: on_device(): sent_grams = [lax.ppermute(reduced, 'col', [(0, k)]) for k in far_first]]
    all_to_all x5 -> x6, starting transfers between devices: 37.2 us -> 40.1 us  [exchange(): return lax.all_to_all(blocks, axis, split_axis=0, concat_axis=0, tiled=True)]
    ppermute x4, starting transfers between devices: 20.4 us -> 23 us  [swapped(): return lax.ppermute(x, 'core', [(0, 1), (1, 0)])]
    all_to_all x5 -> x6, waiting for transfers between devices: 27.4 us -> 25.1 us  [exchange(): return lax.all_to_all(blocks, axis, split_axis=0, concat_axis=0, tiled=True)]
    pallas_call x11 -> x13, Pallas kernels: 35.8 us -> 36.8 us  [call(): pl.pallas_call(kernel, out_shape=out_shape, in_specs=[SMEM] * len(scalars...]
  transfers between devices with their start and end apart: 16 -> 27, of which waited for: 7 -> 12; matrix products, arithmetic and copies ran while one was open for 0% -> 0% of each run, Pallas kernels for 13% -> 13%
where the time goes in v8:
time: 189 us; the launch traced here: 188 us
  starting transfers between devices  99.4 us (53%)
  waiting for transfers between devices  43.8 us (23%)
  Pallas kernels  36.8 us (19%)
  local copies, waits for them, and re-layouts  6.32 us (3%)
    all_to_all x6, starting transfers between devices, exchange(): return lax.all_to_all(blocks, axis, split_axis=0, concat_axis=0, tiled=True)  40.1 us
    pallas_call x13, Pallas kernels, call(): pl.pallas_call(kernel, out_shape=out_shape, in_specs=[SMEM] * len(scalars...  36.8 us
    all_to_all x6, waiting for transfers between devices, exchange(): return lax.all_to_all(blocks, axis, split_axis=0, concat_axis=0, tiled=True)  25.1 us
    ppermute x4, starting transfers between devices, swapped(): return lax.ppermute(x, 'core', [(0, 1), (1, 0)])  23 us
    ppermute x7, starting transfers between devices, on_device(): sent_shares = [lax.ppermute(shares[k], 'col', [(0, k)]) for k in far_first]  15.2 us
    ppermute x7, starting transfers between devices, on_device(): sent_grams = [lax.ppermute(reduced, 'col', [(0, k)]) for k in far_first]  12.4 us
    ppermute x3, starting transfers between devices, on_device(): lax.ppermute(reduced, 'x', [(i, (i + k) % line) for i in range(line)])  8.64 us
    ppermute x7, waiting for transfers between devices, on_device(): sent_grams = [lax.ppermute(reduced, 'col', [(0, k)]) for k in far_first]  8.42 us
  transfers between devices with their start and end apart: 27, of which 12 were waited for; matrix products, arithmetic and copies ran while one was open for 0% of the time, Pallas kernels for 13%

profile of v8, /device:TPU:1, one launch (start us, length us, event | category | flops | bytes accessed | tf_op | source)
XLA Modules:
  0.0 187.6 jit_solution(2467430149650874958)
XLA Ops:
  2.7 14.8 %all-to-all-start = ((f32[64,17,1,128]{3,2,1,0:T(1,128)}), f32[64,17,1,128]{3,2,1,0:T(1,128)S(1)}, u32[]{:S(2)}, u32[]{:S(2)}) async-start(f32[64,17,1,128]{3,2,1,0:T(1,128)} %bitcast.16), calls=%async_computation | async-start | bytes 1114112 | tf_op jit(solution)/shard_map/all_to_all | solution.py:386
  18.2 17.7 %all-to-all-done = f32[64,17,1,128]{3,2,1,0:T(1,128)S(1)} async-done(((f32[64,17,1,128]{3,2,1,0:T(1,128)}), f32[64,17,1,128]{3,2,1,0:T(1,128)S(1)}, u32[]{:S(2)}, u32[]{:S(2)}) %all-to-all-start) | async-done | bytes 557088 | tf_op jit(solution)/shard_map/all_to_all | solution.py:386
  35.9 3.0 %place.1 = (f32[512,512]{1,0:T(8,128)S(1)}, f32[768,128]{1,0:T(8,128)S(1)}, f32[768,128]{1,0:T(8,128)S(1)}, f32[64,512]{1,0:T(8,128)S(1)}, f32[64,512]{1,0:T(8,1...) custom-call(s32[1,1]{1,0:T(1,128)} %bitcast.refs_0_.core_ref, ...), custom_call_target="tpu_custom_call" | custom-call | flops 4294967296 | bytes 4194304 | tf_op jit(solution)/shard_map/place/pallas_call | solution.py:51
  39.0 2.3 %collective-permute-start = (f32[768,128]{1,0:T(8,128)S(1)}, f32[768,128]{1,0:T(8,128)S(1)}, u32[]{:S(2)}, u32[]{:S(2)}) collective-permute-start(f32[768,128]{1,0:T(8,128)S(1)} %get-tuple-element.39), channel_id=1, source_target_pairs={{0,8},{8,0},{1,9},{9,1},{2,10},{10,2},{3,11},{11,3},{4,12},{12,4},... | collective-permute-start | bytes 1179656 | tf_op jit(solution)/shard_map/ppermute | solution.py:390
  43.4 4.9 %all-to-all-start.1 = ((f32[32,24,128]{2,1,0:T(8,128)}), f32[32,24,128]{2,1,0:T(8,128)S(1)}, u32[]{:S(2)}, u32[]{:S(2)}) async-start(f32[32,24,128]{2,1,0:T(8,128)} %bitcast.6), calls=%async_computation.1 | async-start | bytes 786432 | tf_op jit(solution)/shard_map/all_to_all | solution.py:386
  48.3 7.5 %collective-permute-start.1 = (f32[64,512]{1,0:T(8,128)S(1)}, f32[64,512]{1,0:T(8,128)S(1)}, u32[]{:S(2)}, u32[]{:S(2)}) collective-permute-start(f32[64,512]{1,0:T(8,128)S(1)} %get-tuple-element.50), channel_id=1, source_target_pairs={{0,4},{8,12},{16,20},{24,28},{32,36},{40,44},{48,52},{56,60},{64,6... | collective-permute-start | bytes 393224 | tf_op jit(solution)/shard_map/ppermute | solution.py:445
  63.7 2.7 %collective-permute-done.6.refs_5_ = f32[64,512]{1,0:T(8,128)S(1)} collective-permute-done((f32[64,512]{1,0:T(8,128)S(1)}, f32[64,512]{1,0:T(8,128)S(1)}, u32[]{:S(2)}, u32[]{:S(2)}) %collective-permute-start.6) | collective-permute-done | bytes 131104 | tf_op jit(solution)/shard_map/ppermute | solution.py:445
  67.5 4.7 %all-to-all-start.2 = ((f32[8,64,512]{2,1,0:T(8,128)}), f32[8,64,512]{2,1,0:T(8,128)S(1)}, u32[]{:S(2)}, u32[]{:S(2)}) async-start(f32[8,64,512]{2,1,0:T(8,128)} %bundle.1), calls=%async_computation.2 | async-start | bytes 2097152 | tf_op jit(solution)/shard_map/all_to_all | solution.py:386
  72.2 4.7 %collective-permute-start.14 = (f32[24,128]{1,0:T(8,128)S(1)}, f32[24,128]{1,0:T(8,128)S(1)}, u32[]{:S(2)}, u32[]{:S(2)}) collective-permute-start(f32[24,128]{1,0:T(8,128)S(1)} %gram_share.1.own_ref), channel_id=1, source_target_pairs={{0,7},{8,15},{16,23},{24,31},{32,39},{40,47},{48,55},{56,63},{64,7... | collective-permute-start | bytes 36872 | tf_op jit(solution)/shard_map/ppermute | solution.py:455
  84.3 6.7 %collective-permute-done.13.refs_5_ = f32[24,128]{1,0:T(8,128)S(1)} collective-permute-done((f32[24,128]{1,0:T(8,128)S(1)}, f32[24,128]{1,0:T(8,128)S(1)}, u32[]{:S(2)}, u32[]{:S(2)}) %collective-permute-start.13) | collective-permute-done | bytes 12320 | tf_op jit(solution)/shard_map/ppermute | solution.py:455
  93.1 3.7 %collective-permute-start.17 = (f32[24,128]{1,0:T(8,128)S(1)}, f32[24,128]{1,0:T(8,128)S(1)}, u32[]{:S(2)}, u32[]{:S(2)}) collective-permute-start(f32[24,128]{1,0:T(8,128)S(1)} %chosen.1.refs_0_), channel_id=1, source_target_pairs={{0,48},{16,0},{32,16},{48,32},{1,49},{17,1},{33,17},{49,33},{2,50}... | collective-permute-start | bytes 36872 | tf_op jit(solution)/shard_map/ppermute | solution.py:461
  96.8 2.5 %collective-permute-start.16 = (f32[24,128]{1,0:T(8,128)S(1)}, f32[24,128]{1,0:T(8,128)S(1)}, u32[]{:S(2)}, u32[]{:S(2)}) collective-permute-start(f32[24,128]{1,0:T(8,128)S(1)} %chosen.1.refs_0_), channel_id=1, source_target_pairs={{0,32},{16,48},{32,0},{48,16},{1,33},{17,49},{33,1},{49,17},{2,34}... | collective-permute-start | bytes 36872 | tf_op jit(solution)/shard_map/ppermute | solution.py:461
  99.3 2.5 %collective-permute-start.15 = (f32[24,128]{1,0:T(8,128)S(1)}, f32[24,128]{1,0:T(8,128)S(1)}, u32[]{:S(2)}, u32[]{:S(2)}) collective-permute-start(f32[24,128]{1,0:T(8,128)S(1)} %chosen.1.refs_0_), channel_id=1, source_target_pairs={{0,16},{16,32},{32,48},{48,0},{1,17},{17,33},{33,49},{49,1},{2,18}... | collective-permute-start | bytes 36872 | tf_op jit(solution)/shard_map/ppermute | solution.py:461
  102.7 2.2 %collective-permute-done.15.refs_1_ = f32[24,128]{1,0:T(8,128)S(1)} collective-permute-done((f32[24,128]{1,0:T(8,128)S(1)}, f32[24,128]{1,0:T(8,128)S(1)}, u32[]{:S(2)}, u32[]{:S(2)}) %collective-permute-start.15) | collective-permute-done | bytes 12320 | tf_op jit(solution)/shard_map/ppermute | solution.py:461
  105.7 6.4 %all-to-all-start.3 = ((f32[8,96,128]{2,1,0:T(8,128)}), f32[8,96,128]{2,1,0:T(8,128)S(1)}, u32[]{:S(2)}, u32[]{:S(2)}) async-start(f32[8,96,128]{2,1,0:T(8,128)} %line.1), calls=%async_computation.3 | async-start | bytes 786432 | tf_op jit(solution)/shard_map/all_to_all | solution.py:386
  115.1 8.8 %collective-permute-start.18 = (f32[256,512]{1,0:T(8,128)S(1)}, f32[256,512]{1,0:T(8,128)S(1)}, u32[]{:S(2)}, u32[]{:S(2)}) collective-permute-start(f32[256,512]{1,0:T(8,128)S(1)} %get-tuple-element.61), channel_id=1, source_target_pairs={{0,8},{8,0},{1,9},{9,1},{2,10},{10,2},{3,11},{11,3},{4,12},{12,4},... | collective-permute-start | bytes 1572872 | tf_op jit(solution)/shard_map/ppermute | solution.py:390
  126.2 6.6 %collective-permute-start.19 = (f32[768,128]{1,0:T(8,128)S(1)}, f32[768,128]{1,0:T(8,128)S(1)}, u32[]{:S(2)}, u32[]{:S(2)}) collective-permute-start(f32[768,128]{1,0:T(8,128)S(1)} %bitcast.12), channel_id=1, source_target_pairs={{0,8},{8,0},{1,9},{9,1},{2,10},{10,2},{3,11},{11,3},{4,12},{12,4},... | collective-permute-start | bytes 1179656 | tf_op jit(solution)/shard_map/ppermute | solution.py:390
  132.8 4.1 %all-to-all-start.4 = ((f32[32,8,512]{2,1,0:T(8,128)}), f32[32,8,512]{2,1,0:T(8,128)S(1)}, u32[]{:S(2)}, u32[]{:S(2)}) async-start(f32[32,8,512]{2,1,0:T(8,128)} %bitcast.9), calls=%async_computation.4 | async-start | bytes 1048576 | tf_op jit(solution)/shard_map/all_to_all | solution.py:386
  136.9 8.8 %factor0.1.refs_0_.refs_2_ = f32[256,768]{1,0:T(8,128)S(1)} custom-call(s32[1,1]{1,0:T(1,128)} %bitcast.refs_0_.core_ref, f32[768,128]{1,0:T(8,128)S(1)} %bitcast.13, f32[768,128]{1,0:T(8,128)S(1)} %collective-permute-done.19.refs_2_.other_ref), custom_call_target="tpu_custom_call" | custom-call | flops 10737418240 | bytes 4194304 | tf_op jit(solution)/shard_map/factor0/pallas_call | solution.py:51
  146.6 6.9 %all-to-all-done.4.x_ref = f32[32,8,512]{2,1,0:T(8,128)S(1)} async-done(((f32[32,8,512]{2,1,0:T(8,128)}), f32[32,8,512]{2,1,0:T(8,128)S(1)}, u32[]{:S(2)}, u32[]{:S(2)}) %all-to-all-start.4) | async-done | bytes 524320 | tf_op jit(solution)/shard_map/all_to_all | solution.py:386
  154.3 5.2 %all-to-all-start.5 = ((f32[32,8,512]{2,1,0:T(8,128)}), f32[32,8,512]{2,1,0:T(8,128)S(1)}, u32[]{:S(2)}, u32[]{:S(2)}) async-start(f32[32,8,512]{2,1,0:T(8,128)} %fold.1), calls=%async_computation.5 | async-start | bytes 1048576 | tf_op jit(solution)/shard_map/all_to_all | solution.py:386
  160.7 11.6 %factor1.1 = (f32[256,768]{1,0:T(8,128)S(1)}, f32[512,512]{1,0:T(8,128)S(1)}) custom-call(s32[1,1]{1,0:T(1,128)} %bitcast.refs_0_.core_ref, f32[768,128]{1,0:T(8,128)S(1)} %bitcast.14, f32[768,128]{1,0:T(8,128)S(1)} %collective-permute-done.19.refs_2_.other_ref, f32[512,512]{1,0:T(8,128)S(1)} %copy-done.4, f32[256,768]{1,0:T(8,128)S(1)} %copy-done.7), custom_call_target="tpu_custom_call" | custom-call | flops 12884901888 | bytes 4194304 | tf_op jit(solution)/shard_map/factor1/pallas_call | solution.py:51
  174.7 5.3 %collective-permute-start.20 = (f32[256,512]{1,0:T(8,128)S(1)}, f32[256,512]{1,0:T(8,128)S(1)}, u32[]{:S(2)}, u32[]{:S(2)}) collective-permute-start(f32[256,512]{1,0:T(8,128)S(1)} %bitcast.17), channel_id=1, source_target_pairs={{0,8},{8,0},{1,9},{9,1},{2,10},{10,2},{3,11},{11,3},{4,12},{12,4},... | collective-permute-start | bytes 1572872 | tf_op jit(solution)/shard_map/ppermute | solution.py:390
  182.3 5.0 %final.1 = (f32[512,512]{1,0:T(8,128)}, f32[512,512]{1,0:T(8,128)}) custom-call(s32[1,1]{1,0:T(1,128)} %bitcast.refs_0_.core_ref, s32[1,1]{1,0:T(1,128)} %bitcast.1.root_ref.refs_1_, f32[256,768]{1,0:T(8,128)} %copy-done.6, f32[256,768]{1,0:T(8,128)} %copy-done.8, f32[256,512]{1,0:T(8,128)} %bitcast.18, f32[256,512]{1,0:T(8,128)} %copy-done.11, ...), custom_call_target="tpu_custom_call" | custom-call | flops 4294967296 | bytes 4194304 | tf_op jit(solution)/shard_map/final/pallas_call | solution.py:51
  (68 shorter events, 37.9 us)
Async XLA Ops:
  2.7 33.2 %all-to-all-start = ((f32[64,17,1,128]{3,2,1,0:T(1,128)}), f32[64,17,1,128]{3,2,1,0:T(1,128)S(1)}, u32[]{:S(2)}, u32[]{:S(2)}) async-start(f32[64,17,1,128]{3,2,1,0:T(1,128)} %bitcast.16), calls=%async_computation | async-start | bytes 1114112 | tf_op jit(solution)/shard_map/all_to_all | solution.py:386
  43.4 24.0 %all-to-all-start.1 = ((f32[32,24,128]{2,1,0:T(8,128)}), f32[32,24,128]{2,1,0:T(8,128)S(1)}, u32[]{:S(2)}, u32[]{:S(2)}) async-start(f32[32,24,128]{2,1,0:T(8,128)} %bitcast.6), calls=%async_computation.1 | async-start | bytes 786432 | tf_op jit(solution)/shard_map/all_to_all | solution.py:386
  48.3 12.7 %collective-permute-start.1 = (f32[64,512]{1,0:T(8,128)S(1)}, f32[64,512]{1,0:T(8,128)S(1)}, u32[]{:S(2)}, u32[]{:S(2)}) collective-permute-start(f32[64,512]{1,0:T(8,128)S(1)} %get-tuple-element.50), channel_id=1, source_target_pairs={{0,4},{8,12},{16,20},{24,28},{32,36},{40,44},{48,52},{56,60},{64,6... | collective-permute-start | bytes 393224 | tf_op jit(solution)/shard_map/ppermute | solution.py:445
  55.8 6.5 %collective-permute-start.2 = (f32[64,512]{1,0:T(8,128)S(1)}, f32[64,512]{1,0:T(8,128)S(1)}, u32[]{:S(2)}, u32[]{:S(2)}) collective-permute-start(f32[64,512]{1,0:T(8,128)S(1)} %get-tuple-element.51), channel_id=1, source_target_pairs={{0,3},{8,11},{16,19},{24,27},{32,35},{40,43},{48,51},{56,59},{64,6... | collective-permute-start | bytes 393224 | tf_op jit(solution)/shard_map/ppermute | solution.py:445
  57.1 6.6 %collective-permute-start.3 = (f32[64,512]{1,0:T(8,128)S(1)}, f32[64,512]{1,0:T(8,128)S(1)}, u32[]{:S(2)}, u32[]{:S(2)}) collective-permute-start(f32[64,512]{1,0:T(8,128)S(1)} %get-tuple-element.52), channel_id=1, source_target_pairs={{0,5},{8,13},{16,21},{24,29},{32,37},{40,45},{48,53},{56,61},{64,6... | collective-permute-start | bytes 393224 | tf_op jit(solution)/shard_map/ppermute | solution.py:445
  58.4 5.3 %collective-permute-start.4 = (f32[64,512]{1,0:T(8,128)S(1)}, f32[64,512]{1,0:T(8,128)S(1)}, u32[]{:S(2)}, u32[]{:S(2)}) collective-permute-start(f32[64,512]{1,0:T(8,128)S(1)} %get-tuple-element.53), channel_id=1, source_target_pairs={{0,2},{8,10},{16,18},{24,26},{32,34},{40,42},{48,50},{56,58},{64,6... | collective-permute-start | bytes 393224 | tf_op jit(solution)/shard_map/ppermute | solution.py:445
  61.0 5.4 %collective-permute-start.6 = (f32[64,512]{1,0:T(8,128)S(1)}, f32[64,512]{1,0:T(8,128)S(1)}, u32[]{:S(2)}, u32[]{:S(2)}) collective-permute-start(f32[64,512]{1,0:T(8,128)S(1)} %get-tuple-element.55), channel_id=1, source_target_pairs={{0,1},{8,9},{16,17},{24,25},{32,33},{40,41},{48,49},{56,57},{64,65... | collective-permute-start | bytes 393224 | tf_op jit(solution)/shard_map/ppermute | solution.py:445
  62.3 4.1 %collective-permute-start.7 = (f32[64,512]{1,0:T(8,128)S(1)}, f32[64,512]{1,0:T(8,128)S(1)}, u32[]{:S(2)}, u32[]{:S(2)}) collective-permute-start(f32[64,512]{1,0:T(8,128)S(1)} %get-tuple-element.56), channel_id=1, source_target_pairs={{0,7},{8,15},{16,23},{24,31},{32,39},{40,47},{48,55},{56,63},{64,7... | collective-permute-start | bytes 393224 | tf_op jit(solution)/shard_map/ppermute | solution.py:445
  67.5 38.3 %all-to-all-start.2 = ((f32[8,64,512]{2,1,0:T(8,128)}), f32[8,64,512]{2,1,0:T(8,128)S(1)}, u32[]{:S(2)}, u32[]{:S(2)}) async-start(f32[8,64,512]{2,1,0:T(8,128)} %bundle.1), calls=%async_computation.2 | async-start | bytes 2097152 | tf_op jit(solution)/shard_map/all_to_all | solution.py:386
  72.2 10.9 %collective-permute-start.14 = (f32[24,128]{1,0:T(8,128)S(1)}, f32[24,128]{1,0:T(8,128)S(1)}, u32[]{:S(2)}, u32[]{:S(2)}) collective-permute-start(f32[24,128]{1,0:T(8,128)S(1)} %gram_share.1.own_ref), channel_id=1, source_target_pairs={{0,7},{8,15},{16,23},{24,31},{32,39},{40,47},{48,55},{56,63},{64,7... | collective-permute-start | bytes 36872 | tf_op jit(solution)/shard_map/ppermute | solution.py:455
  76.9 14.1 %collective-permute-start.13 = (f32[24,128]{1,0:T(8,128)S(1)}, f32[24,128]{1,0:T(8,128)S(1)}, u32[]{:S(2)}, u32[]{:S(2)}) collective-permute-start(f32[24,128]{1,0:T(8,128)S(1)} %gram_share.1.own_ref), channel_id=1, source_target_pairs={{0,1},{8,9},{16,17},{24,25},{32,33},{40,41},{48,49},{56,57},{64,65... | collective-permute-start | bytes 36872 | tf_op jit(solution)/shard_map/ppermute | solution.py:455
  78.2 14.1 %collective-permute-start.12 = (f32[24,128]{1,0:T(8,128)S(1)}, f32[24,128]{1,0:T(8,128)S(1)}, u32[]{:S(2)}, u32[]{:S(2)}) collective-permute-start(f32[24,128]{1,0:T(8,128)S(1)} %gram_share.1.own_ref), channel_id=1, source_target_pairs={{0,6},{8,14},{16,22},{24,30},{32,38},{40,46},{48,54},{56,62},{64,7... | collective-permute-start | bytes 36872 | tf_op jit(solution)/shard_map/ppermute | solution.py:455
  79.5 12.8 %collective-permute-start.11 = (f32[24,128]{1,0:T(8,128)S(1)}, f32[24,128]{1,0:T(8,128)S(1)}, u32[]{:S(2)}, u32[]{:S(2)}) collective-permute-start(f32[24,128]{1,0:T(8,128)S(1)} %gram_share.1.own_ref), channel_id=1, source_target_pairs={{0,2},{8,10},{16,18},{24,26},{32,34},{40,42},{48,50},{56,58},{64,6... | collective-permute-start | bytes 36872 | tf_op jit(solution)/shard_map/ppermute | solution.py:455
  80.8 11.5 %collective-permute-start.10 = (f32[24,128]{1,0:T(8,128)S(1)}, f32[24,128]{1,0:T(8,128)S(1)}, u32[]{:S(2)}, u32[]{:S(2)}) collective-permute-start(f32[24,128]{1,0:T(8,128)S(1)} %gram_share.1.own_ref), channel_id=1, source_target_pairs={{0,5},{8,13},{16,21},{24,29},{32,37},{40,45},{48,53},{56,61},{64,6... | collective-permute-start | bytes 36872 | tf_op jit(solution)/shard_map/ppermute | solution.py:455
  83.1 9.3 %collective-permute-start.9 = (f32[24,128]{1,0:T(8,128)S(1)}, f32[24,128]{1,0:T(8,128)S(1)}, u32[]{:S(2)}, u32[]{:S(2)}) collective-permute-start(f32[24,128]{1,0:T(8,128)S(1)} %gram_share.1.own_ref), channel_id=1, source_target_pairs={{0,3},{8,11},{16,19},{24,27},{32,35},{40,43},{48,51},{56,59},{64,6... | collective-permute-start | bytes 36872 | tf_op jit(solution)/shard_map/ppermute | solution.py:455
  93.1 8.7 %collective-permute-start.17 = (f32[24,128]{1,0:T(8,128)S(1)}, f32[24,128]{1,0:T(8,128)S(1)}, u32[]{:S(2)}, u32[]{:S(2)}) collective-permute-start(f32[24,128]{1,0:T(8,128)S(1)} %chosen.1.refs_0_), channel_id=1, source_target_pairs={{0,48},{16,0},{32,16},{48,32},{1,49},{17,1},{33,17},{49,33},{2,50}... | collective-permute-start | bytes 36872 | tf_op jit(solution)/shard_map/ppermute | solution.py:461
  96.8 5.9 %collective-permute-start.16 = (f32[24,128]{1,0:T(8,128)S(1)}, f32[24,128]{1,0:T(8,128)S(1)}, u32[]{:S(2)}, u32[]{:S(2)}) collective-permute-start(f32[24,128]{1,0:T(8,128)S(1)} %chosen.1.refs_0_), channel_id=1, source_target_pairs={{0,32},{16,48},{32,0},{48,16},{1,33},{17,49},{33,1},{49,17},{2,34}... | collective-permute-start | bytes 36872 | tf_op jit(solution)/shard_map/ppermute | solution.py:461
  99.3 5.7 %collective-permute-start.15 = (f32[24,128]{1,0:T(8,128)S(1)}, f32[24,128]{1,0:T(8,128)S(1)}, u32[]{:S(2)}, u32[]{:S(2)}) collective-permute-start(f32[24,128]{1,0:T(8,128)S(1)} %chosen.1.refs_0_), channel_id=1, source_target_pairs={{0,16},{16,32},{32,48},{48,0},{1,17},{17,33},{33,49},{49,1},{2,18}... | collective-permute-start | bytes 36872 | tf_op jit(solution)/shard_map/ppermute | solution.py:461
  105.7 20.5 %all-to-all-start.3 = ((f32[8,96,128]{2,1,0:T(8,128)}), f32[8,96,128]{2,1,0:T(8,128)S(1)}, u32[]{:S(2)}, u32[]{:S(2)}) async-start(f32[8,96,128]{2,1,0:T(8,128)} %line.1), calls=%async_computation.3 | async-start | bytes 786432 | tf_op jit(solution)/shard_map/all_to_all | solution.py:386
  115.1 10.3 %collective-permute-start.18 = (f32[256,512]{1,0:T(8,128)S(1)}, f32[256,512]{1,0:T(8,128)S(1)}, u32[]{:S(2)}, u32[]{:S(2)}) collective-permute-start(f32[256,512]{1,0:T(8,128)S(1)} %get-tuple-element.61), channel_id=1, source_target_pairs={{0,8},{8,0},{1,9},{9,1},{2,10},{10,2},{3,11},{11,3},{4,12},{12,4},... | collective-permute-start | bytes 1572872 | tf_op jit(solution)/shard_map/ppermute | solution.py:390
  126.2 10.7 %collective-permute-start.19 = (f32[768,128]{1,0:T(8,128)S(1)}, f32[768,128]{1,0:T(8,128)S(1)}, u32[]{:S(2)}, u32[]{:S(2)}) collective-permute-start(f32[768,128]{1,0:T(8,128)S(1)} %bitcast.12), channel_id=1, source_target_pairs={{0,8},{8,0},{1,9},{9,1},{2,10},{10,2},{3,11},{11,3},{4,12},{12,4},... | collective-permute-start | bytes 1179656 | tf_op jit(solution)/shard_map/ppermute | solution.py:390
  132.8 20.7 %all-to-all-start.4 = ((f32[32,8,512]{2,1,0:T(8,128)}), f32[32,8,512]{2,1,0:T(8,128)S(1)}, u32[]{:S(2)}, u32[]{:S(2)}) async-start(f32[32,8,512]{2,1,0:T(8,128)} %bitcast.9), calls=%async_computation.4 | async-start | bytes 1048576 | tf_op jit(solution)/shard_map/all_to_all | solution.py:386
  154.3 20.3 %all-to-all-start.5 = ((f32[32,8,512]{2,1,0:T(8,128)}), f32[32,8,512]{2,1,0:T(8,128)S(1)}, u32[]{:S(2)}, u32[]{:S(2)}) async-start(f32[32,8,512]{2,1,0:T(8,128)} %fold.1), calls=%async_computation.5 | async-start | bytes 1048576 | tf_op jit(solution)/shard_map/all_to_all | solution.py:386
  174.7 6.9 %collective-permute-start.20 = (f32[256,512]{1,0:T(8,128)S(1)}, f32[256,512]{1,0:T(8,128)S(1)}, u32[]{:S(2)}, u32[]{:S(2)}) collective-permute-start(f32[256,512]{1,0:T(8,128)S(1)} %bitcast.17), channel_id=1, source_target_pairs={{0,8},{8,0},{1,9},{9,1},{2,10},{10,2},{3,11},{11,3},{4,12},{12,4},... | collective-permute-start | bytes 1572872 | tf_op jit(solution)/shard_map/ppermute | solution.py:390
  (15 other events, 115.6 us)

commit v9 on v7

--- a/solution.py
+++ b/solution.py
@@ -465,7 +465,7 @@
 
     block_shape = f32(PANELS // PIECES, 3 * PANELS // 2)
     upper = call(
-        lambda *refs: factor_kernel(0, *refs), block_shape, "factor0", 10 << 30,
+        lambda *refs: factor_kernel(0, *refs), block_shape, "factor0", 1 << 30,
         own_gram, other_gram, scalars=(core,),
     )
     summands, upper = lax.optimization_barrier((summands, upper))

time: 184 us -> 182 us (0.989)
  local copies, waits for them, and re-layouts: 6.88 us -> 3.66 us
    all_to_all x5, starting transfers between devices: 37.2 us -> 42.7 us  [exchange(): return lax.all_to_all(blocks, axis, split_axis=0, concat_axis=0, tiled=True)]
    ppermute x4, starting transfers between devices: 20.4 us -> 15.9 us  [swapped(): return lax.ppermute(x, 'core', [(0, 1), (1, 0)])]
    unnamed x24 -> x22, local copies, waits for them, and re-layouts: 6.88 us -> 3.66 us
    all_to_all x5, waiting for transfers between devices: 27.4 us -> 24.6 us  [exchange(): return lax.all_to_all(blocks, axis, split_axis=0, concat_axis=0, tiled=True)]
    ppermute x4, waiting for transfers between devices: 2.85 us -> 5.5 us  [swapped(): return lax.ppermute(x, 'core', [(0, 1), (1, 0)])]
  transfers between devices with their start and end apart: 16 -> 16, of which waited for: 7 -> 9; matrix products, arithmetic and copies ran while one was open for 0% -> 0% of each run, Pallas kernels for 13% -> 13%
where the time goes in v9:
time: 182 us; the launch traced here: 181 us
  starting transfers between devices  73.9 us (41%)
  Pallas kernels  35.8 us (20%)
  blocking collectives  33.4 us (18%)
  waiting for transfers between devices  32.8 us (18%)
  local copies, waits for them, and re-layouts  3.66 us (2%)
    all_to_all x5, starting transfers between devices, exchange(): return lax.all_to_all(blocks, axis, split_axis=0, concat_axis=0, tiled=True)  42.7 us
    pallas_call x11, Pallas kernels, call(): pl.pallas_call(kernel, out_shape=out_shape, in_specs=[SMEM] * len(scalars...  35.8 us
    all_to_all x1, blocking collectives, exchange(): return lax.all_to_all(blocks, axis, split_axis=0, concat_axis=0, tiled=True)  33.4 us
    all_to_all x5, waiting for transfers between devices, exchange(): return lax.all_to_all(blocks, axis, split_axis=0, concat_axis=0, tiled=True)  24.6 us
    ppermute x4, starting transfers between devices, swapped(): return lax.ppermute(x, 'core', [(0, 1), (1, 0)])  15.9 us
    ppermute x7, starting transfers between devices, on_device(): sent_shares = [lax.ppermute(shares[k], 'col', [(0, k)]) for k in far_first]  15.2 us
    ppermute x4, waiting for transfers between devices, swapped(): return lax.ppermute(x, 'core', [(0, 1), (1, 0)])  5.5 us
    unnamed x22, local copies, waits for them, and re-layouts  3.66 us
  transfers between devices with their start and end apart: 16, of which 9 were waited for; matrix products, arithmetic and copies ran while one was open for 0% of the time, Pallas kernels for 13%

profile of v9, /device:TPU:1, one launch (start us, length us, event | category | flops | bytes accessed | tf_op | source)
XLA Modules:
  0.0 180.8 jit_solution(89059938760512715)
XLA Ops:
  0.7 2.0 %pack.1 = f32[1088,128]{1,0:T(8,128)} custom-call(f32[512,256]{1,0:T(8,128)} %refs_0_.1, s32[4,128]{1,0:T(4,128)} %bitcast.18, s32[1,64]{1,0:T(1,128)} %refs_2_.1), custom_call_target="tpu_custom_call" | custom-call | flops 1048576 | bytes 4194304 | tf_op jit(solution)/shard_map/pack/pallas_call | solution.py:51
  2.7 14.8 %all-to-all-start = ((f32[64,17,1,128]{3,2,1,0:T(1,128)}), f32[64,17,1,128]{3,2,1,0:T(1,128)S(1)}, u32[]{:S(2)}, u32[]{:S(2)}) async-start(f32[64,17,1,128]{3,2,1,0:T(1,128)} %bitcast.15), calls=%async_computation | async-start | bytes 1114112 | tf_op jit(solution)/shard_map/all_to_all | solution.py:384
  17.6 18.4 %all-to-all-done = f32[64,17,1,128]{3,2,1,0:T(1,128)S(1)} async-done(((f32[64,17,1,128]{3,2,1,0:T(1,128)}), f32[64,17,1,128]{3,2,1,0:T(1,128)S(1)}, u32[]{:S(2)}, u32[]{:S(2)}) %all-to-all-start) | async-done | bytes 557088 | tf_op jit(solution)/shard_map/all_to_all | solution.py:384
  35.9 3.0 %place.1 = (f32[512,512]{1,0:T(8,128)S(1)}, f32[768,128]{1,0:T(8,128)S(1)}, f32[768,128]{1,0:T(8,128)S(1)}, f32[64,512]{1,0:T(8,128)S(1)}, f32[64,512]{1,0:T(8,1...) custom-call(s32[1,1]{1,0:T(1,128)} %bitcast.refs_0_.core_ref, ...), custom_call_target="tpu_custom_call" | custom-call | flops 4294967296 | bytes 4194304 | tf_op jit(solution)/shard_map/place/pallas_call | solution.py:51
  39.0 2.3 %collective-permute-start = (f32[768,128]{1,0:T(8,128)S(1)}, f32[768,128]{1,0:T(8,128)S(1)}, u32[]{:S(2)}, u32[]{:S(2)}) collective-permute-start(f32[768,128]{1,0:T(8,128)S(1)} %get-tuple-element.33), channel_id=1, source_target_pairs={{0,8},{8,0},{1,9},{9,1},{2,10},{10,2},{3,11},{11,3},{4,12},{12,4},... | collective-permute-start | bytes 1179656 | tf_op jit(solution)/shard_map/ppermute | solution.py:388
  41.3 1.3 collective-permute-done.b_ref
  43.5 4.9 %all-to-all-start.1 = ((f32[32,24,128]{2,1,0:T(8,128)}), f32[32,24,128]{2,1,0:T(8,128)S(1)}, u32[]{:S(2)}, u32[]{:S(2)}) async-start(f32[32,24,128]{2,1,0:T(8,128)} %bitcast.6), calls=%async_computation.1 | async-start | bytes 786432 | tf_op jit(solution)/shard_map/all_to_all | solution.py:384
  48.3 7.5 %collective-permute-start.1 = (f32[64,512]{1,0:T(8,128)S(1)}, f32[64,512]{1,0:T(8,128)S(1)}, u32[]{:S(2)}, u32[]{:S(2)}) collective-permute-start(f32[64,512]{1,0:T(8,128)S(1)} %get-tuple-element.44), channel_id=1, source_target_pairs={{0,4},{8,12},{16,20},{24,28},{32,36},{40,44},{48,52},{56,60},{64,6... | collective-permute-start | bytes 393224 | tf_op jit(solution)/shard_map/ppermute | solution.py:443
  63.7 2.7 %collective-permute-done.6.refs_5_ = f32[64,512]{1,0:T(8,128)S(1)} collective-permute-done((f32[64,512]{1,0:T(8,128)S(1)}, f32[64,512]{1,0:T(8,128)S(1)}, u32[]{:S(2)}, u32[]{:S(2)}) %collective-permute-start.6) | collective-permute-done | bytes 131104 | tf_op jit(solution)/shard_map/ppermute | solution.py:443
  66.5 33.4 %all_to_all.30.bundle_ref = f32[8,280,128]{2,1,0:T(8,128)S(1)} all-to-all(f32[8,280,128]{2,1,0:T(8,128)S(1)} %bundle.1), channel_id=1, replica_groups=mesh['z'=8,'x'=4,'core'=2,'col'=8] {'col'}, dimensions={0} | all-to-all | bytes 2293760 | tf_op jit(solution)/shard_map/all_to_all | solution.py:384
  100.7 8.1 %all-to-all-start.4 = ((f32[32,24,128]{2,1,0:T(8,128)}), f32[32,24,128]{2,1,0:T(8,128)S(1)}, u32[]{:S(2)}, u32[]{:S(2)}) async-start(f32[32,24,128]{2,1,0:T(8,128)} %gram_share.1), calls=%async_computation.4 | async-start | bytes 786432 | tf_op jit(solution)/shard_map/all_to_all | solution.py:384
  108.8 2.0 %products.1 = (f32[512,512]{1,0:T(8,128)S(1)}, f32[256,512]{1,0:T(8,128)S(1)}, f32[256,512]{1,0:T(8,128)S(1)}) custom-call(s32[1,1]{1,0:T(1,128)} %bitcast.refs_0_.core_ref, f32[512,512]{1,0:T(8,128)S(1)} %copy-done.3, f32[8,280,128]{2,1,0:T(8,128)S(1)} %all_to_all.30.bundle_ref), custom_call_target="tpu_custom_call" | custom-call | flops 2147483648 | bytes 4194304 | tf_op jit(solution)/shard_map/products/pallas_call | solution.py:51
  111.8 5.8 %collective-permute-start.8 = (f32[256,512]{1,0:T(8,128)S(1)}, f32[256,512]{1,0:T(8,128)S(1)}, u32[]{:S(2)}, u32[]{:S(2)}) collective-permute-start(f32[256,512]{1,0:T(8,128)S(1)} %get-tuple-element.52), channel_id=1, source_target_pairs={{0,8},{8,0},{1,9},{9,1},{2,10},{10,2},{3,11},{11,3},{4,12},{12,4},... | collective-permute-start | bytes 1572872 | tf_op jit(solution)/shard_map/ppermute | solution.py:388
  117.6 1.5 collective-permute-done.8.b_ref
  120.4 9.1 %all-to-all-start.3 = ((f32[32,8,512]{2,1,0:T(8,128)}), f32[32,8,512]{2,1,0:T(8,128)S(1)}, u32[]{:S(2)}, u32[]{:S(2)}) async-start(f32[32,8,512]{2,1,0:T(8,128)} %bitcast.7), calls=%async_computation.3 | async-start | bytes 1048576 | tf_op jit(solution)/shard_map/all_to_all | solution.py:384
  129.5 2.7 %collective-permute-start.9 = (f32[768,128]{1,0:T(8,128)S(1)}, f32[768,128]{1,0:T(8,128)S(1)}, u32[]{:S(2)}, u32[]{:S(2)}) collective-permute-start(f32[768,128]{1,0:T(8,128)S(1)} %bitcast.11), channel_id=1, source_target_pairs={{0,8},{8,0},{1,9},{9,1},{2,10},{10,2},{3,11},{11,3},{4,12},{12,4},... | collective-permute-start | bytes 1179656 | tf_op jit(solution)/shard_map/ppermute | solution.py:388
  133.4 8.8 %factor0.1.refs_0_.refs_2_ = f32[256,768]{1,0:T(8,128)S(1)} custom-call(s32[1,1]{1,0:T(1,128)} %bitcast.refs_0_.core_ref, f32[768,128]{1,0:T(8,128)S(1)} %bitcast.12, f32[768,128]{1,0:T(8,128)S(1)} %collective-permute-done.9.refs_2_.other_ref), custom_call_target="tpu_custom_call" | custom-call | flops 1073741824 | bytes 4194304 | tf_op jit(solution)/shard_map/factor0/pallas_call | solution.py:51
  142.2 3.9 %all-to-all-done.3.x_ref = f32[32,8,512]{2,1,0:T(8,128)S(1)} async-done(((f32[32,8,512]{2,1,0:T(8,128)}), f32[32,8,512]{2,1,0:T(8,128)S(1)}, u32[]{:S(2)}, u32[]{:S(2)}) %all-to-all-start.3) | async-done | bytes 524320 | tf_op jit(solution)/shard_map/all_to_all | solution.py:384
  146.9 5.8 %all-to-all-start.5 = ((f32[32,8,512]{2,1,0:T(8,128)}), f32[32,8,512]{2,1,0:T(8,128)S(1)}, u32[]{:S(2)}, u32[]{:S(2)}) async-start(f32[32,8,512]{2,1,0:T(8,128)} %fold.1), calls=%async_computation.5 | async-start | bytes 1048576 | tf_op jit(solution)/shard_map/all_to_all | solution.py:384
  152.8 11.6 %factor1.1 = (f32[256,768]{1,0:T(8,128)S(1)}, f32[512,512]{1,0:T(8,128)S(1)}) custom-call(s32[1,1]{1,0:T(1,128)} %bitcast.refs_0_.core_ref, f32[768,128]{1,0:T(8,128)S(1)} %bitcast.13, f32[768,128]{1,0:T(8,128)S(1)} %collective-permute-done.9.refs_2_.other_ref, f32[512,512]{1,0:T(8,128)S(1)} %copy-done.5, f32[256,768]{1,0:T(8,128)S(1)} %factor0.1.refs_0_.refs_2_), custom_call_target="tpu_custom_call" | custom-call | flops 12884901888 | bytes 4194304 | tf_op jit(solution)/shard_map/factor1/pallas_call | solution.py:51
  166.2 1.9 %all-to-all-done.5 = f32[32,8,512]{2,1,0:T(8,128)S(1)} async-done(((f32[32,8,512]{2,1,0:T(8,128)}), f32[32,8,512]{2,1,0:T(8,128)S(1)}, u32[]{:S(2)}, u32[]{:S(2)}) %all-to-all-start.5) | async-done | bytes 524320 | tf_op jit(solution)/shard_map/all_to_all | solution.py:384
  168.2 5.0 %collective-permute-start.10 = (f32[256,512]{1,0:T(8,128)S(1)}, f32[256,512]{1,0:T(8,128)S(1)}, u32[]{:S(2)}, u32[]{:S(2)}) collective-permute-start(f32[256,512]{1,0:T(8,128)S(1)} %bitcast.16), channel_id=1, source_target_pairs={{0,8},{8,0},{1,9},{9,1},{2,10},{10,2},{3,11},{11,3},{4,12},{12,4},... | collective-permute-start | bytes 1572872 | tf_op jit(solution)/shard_map/ppermute | solution.py:388
  173.2 1.5 collective-permute-done.10.refs_5_
  175.6 5.0 %final.1 = (f32[512,512]{1,0:T(8,128)}, f32[512,512]{1,0:T(8,128)}) custom-call(s32[1,1]{1,0:T(1,128)} %bitcast.refs_0_.core_ref, s32[1,1]{1,0:T(1,128)} %bitcast.1.root_ref.refs_1_, f32[256,768]{1,0:T(8,128)} %copy-done.1, f32[256,768]{1,0:T(8,128)} %copy-done.7, f32[256,512]{1,0:T(8,128)} %bitcast.17, f32[256,512]{1,0:T(8,128)} %copy-done.10, ...), custom_call_target="tpu_custom_call" | custom-call | flops 4294967296 | bytes 4194304 | tf_op jit(solution)/shard_map/final/pallas_call | solution.py:51
  (43 shorter events, 16.5 us)
Async XLA Ops:
  0.6 16.9 %copy-start.9 = (s32[256]{0:T(256)S(1)}, s32[256]{0:T(256)}, u32[]{:S(2)}) copy-start(s32[256]{0:T(256)} %param.9) | copy-start | bytes 3076
  0.6 35.3 %copy-start = (f32[512,512]{1,0:T(8,128)S(1)}, f32[512,512]{1,0:T(8,128)}, u32[]{:S(2)}) copy-start(f32[512,512]{1,0:T(8,128)} %refs_1_.1) | copy-start | bytes 3145732
  2.7 33.2 %all-to-all-start = ((f32[64,17,1,128]{3,2,1,0:T(1,128)}), f32[64,17,1,128]{3,2,1,0:T(1,128)S(1)}, u32[]{:S(2)}, u32[]{:S(2)}) async-start(f32[64,17,1,128]{3,2,1,0:T(1,128)} %bitcast.15), calls=%async_computation | async-start | bytes 1114112 | tf_op jit(solution)/shard_map/all_to_all | solution.py:384
  39.0 4.5 %copy-start.2 = (f32[512,512]{1,0:T(8,128)}, f32[512,512]{1,0:T(8,128)S(1)}, u32[]{:S(2)}) copy-start(f32[512,512]{1,0:T(8,128)S(1)} %get-tuple-element.31.front_ref.refs_7_) | copy-start | bytes 3145732
  39.0 3.7 %collective-permute-start = (f32[768,128]{1,0:T(8,128)S(1)}, f32[768,128]{1,0:T(8,128)S(1)}, u32[]{:S(2)}, u32[]{:S(2)}) collective-permute-start(f32[768,128]{1,0:T(8,128)S(1)} %get-tuple-element.33), channel_id=1, source_target_pairs={{0,8},{8,0},{1,9},{9,1},{2,10},{10,2},{3,11},{11,3},{4,12},{12,4},... | collective-permute-start | bytes 1179656 | tf_op jit(solution)/shard_map/ppermute | solution.py:388
  43.5 23.0 %all-to-all-start.1 = ((f32[32,24,128]{2,1,0:T(8,128)}), f32[32,24,128]{2,1,0:T(8,128)S(1)}, u32[]{:S(2)}, u32[]{:S(2)}) async-start(f32[32,24,128]{2,1,0:T(8,128)} %bitcast.6), calls=%async_computation.1 | async-start | bytes 786432 | tf_op jit(solution)/shard_map/all_to_all | solution.py:384
  48.3 12.7 %collective-permute-start.1 = (f32[64,512]{1,0:T(8,128)S(1)}, f32[64,512]{1,0:T(8,128)S(1)}, u32[]{:S(2)}, u32[]{:S(2)}) collective-permute-start(f32[64,512]{1,0:T(8,128)S(1)} %get-tuple-element.44), channel_id=1, source_target_pairs={{0,4},{8,12},{16,20},{24,28},{32,36},{40,44},{48,52},{56,60},{64,6... | collective-permute-start | bytes 393224 | tf_op jit(solution)/shard_map/ppermute | solution.py:443
  55.8 6.5 %collective-permute-start.2 = (f32[64,512]{1,0:T(8,128)S(1)}, f32[64,512]{1,0:T(8,128)S(1)}, u32[]{:S(2)}, u32[]{:S(2)}) collective-permute-start(f32[64,512]{1,0:T(8,128)S(1)} %get-tuple-element.45), channel_id=1, source_target_pairs={{0,3},{8,11},{16,19},{24,27},{32,35},{40,43},{48,51},{56,59},{64,6... | collective-permute-start | bytes 393224 | tf_op jit(solution)/shard_map/ppermute | solution.py:443
  57.1 6.6 %collective-permute-start.3 = (f32[64,512]{1,0:T(8,128)S(1)}, f32[64,512]{1,0:T(8,128)S(1)}, u32[]{:S(2)}, u32[]{:S(2)}) collective-permute-start(f32[64,512]{1,0:T(8,128)S(1)} %get-tuple-element.46), channel_id=1, source_target_pairs={{0,5},{8,13},{16,21},{24,29},{32,37},{40,45},{48,53},{56,61},{64,6... | collective-permute-start | bytes 393224 | tf_op jit(solution)/shard_map/ppermute | solution.py:443
  58.4 5.3 %collective-permute-start.4 = (f32[64,512]{1,0:T(8,128)S(1)}, f32[64,512]{1,0:T(8,128)S(1)}, u32[]{:S(2)}, u32[]{:S(2)}) collective-permute-start(f32[64,512]{1,0:T(8,128)S(1)} %get-tuple-element.47), channel_id=1, source_target_pairs={{0,2},{8,10},{16,18},{24,26},{32,34},{40,42},{48,50},{56,58},{64,6... | collective-permute-start | bytes 393224 | tf_op jit(solution)/shard_map/ppermute | solution.py:443
  59.7 4.0 %collective-permute-start.5 = (f32[64,512]{1,0:T(8,128)S(1)}, f32[64,512]{1,0:T(8,128)S(1)}, u32[]{:S(2)}, u32[]{:S(2)}) collective-permute-start(f32[64,512]{1,0:T(8,128)S(1)} %get-tuple-element.48), channel_id=1, source_target_pairs={{0,6},{8,14},{16,22},{24,30},{32,38},{40,46},{48,54},{56,62},{64,7... | collective-permute-start | bytes 393224 | tf_op jit(solution)/shard_map/ppermute | solution.py:443
  61.0 5.4 %collective-permute-start.6 = (f32[64,512]{1,0:T(8,128)S(1)}, f32[64,512]{1,0:T(8,128)S(1)}, u32[]{:S(2)}, u32[]{:S(2)}) collective-permute-start(f32[64,512]{1,0:T(8,128)S(1)} %get-tuple-element.49), channel_id=1, source_target_pairs={{0,1},{8,9},{16,17},{24,25},{32,33},{40,41},{48,49},{56,57},{64,65... | collective-permute-start | bytes 393224 | tf_op jit(solution)/shard_map/ppermute | solution.py:443
  62.3 4.1 %collective-permute-start.7 = (f32[64,512]{1,0:T(8,128)S(1)}, f32[64,512]{1,0:T(8,128)S(1)}, u32[]{:S(2)}, u32[]{:S(2)}) collective-permute-start(f32[64,512]{1,0:T(8,128)S(1)} %get-tuple-element.50), channel_id=1, source_target_pairs={{0,7},{8,15},{16,23},{24,31},{32,39},{40,47},{48,55},{56,63},{64,7... | collective-permute-start | bytes 393224 | tf_op jit(solution)/shard_map/ppermute | solution.py:443
  100.0 8.9 %copy-start.3 = (f32[512,512]{1,0:T(8,128)S(1)}, f32[512,512]{1,0:T(8,128)}, u32[]{:S(2)}) copy-start(f32[512,512]{1,0:T(8,128)} %copy-done.2) | copy-start | bytes 3145732
  100.7 19.7 %all-to-all-start.4 = ((f32[32,24,128]{2,1,0:T(8,128)}), f32[32,24,128]{2,1,0:T(8,128)S(1)}, u32[]{:S(2)}, u32[]{:S(2)}) async-start(f32[32,24,128]{2,1,0:T(8,128)} %gram_share.1), calls=%async_computation.4 | async-start | bytes 786432 | tf_op jit(solution)/shard_map/all_to_all | solution.py:384
  110.8 1.0 copy-start.4
  111.8 7.3 %collective-permute-start.8 = (f32[256,512]{1,0:T(8,128)S(1)}, f32[256,512]{1,0:T(8,128)S(1)}, u32[]{:S(2)}, u32[]{:S(2)}) collective-permute-start(f32[256,512]{1,0:T(8,128)S(1)} %get-tuple-element.52), channel_id=1, source_target_pairs={{0,8},{8,0},{1,9},{9,1},{2,10},{10,2},{3,11},{11,3},{4,12},{12,4},... | collective-permute-start | bytes 1572872 | tf_op jit(solution)/shard_map/ppermute | solution.py:388
  120.4 25.7 %all-to-all-start.3 = ((f32[32,8,512]{2,1,0:T(8,128)}), f32[32,8,512]{2,1,0:T(8,128)S(1)}, u32[]{:S(2)}, u32[]{:S(2)}) async-start(f32[32,8,512]{2,1,0:T(8,128)} %bitcast.7), calls=%async_computation.3 | async-start | bytes 1048576 | tf_op jit(solution)/shard_map/all_to_all | solution.py:384
  129.5 3.9 %collective-permute-start.9 = (f32[768,128]{1,0:T(8,128)S(1)}, f32[768,128]{1,0:T(8,128)S(1)}, u32[]{:S(2)}, u32[]{:S(2)}) collective-permute-start(f32[768,128]{1,0:T(8,128)S(1)} %bitcast.11), channel_id=1, source_target_pairs={{0,8},{8,0},{1,9},{9,1},{2,10},{10,2},{3,11},{11,3},{4,12},{12,4},... | collective-permute-start | bytes 1179656 | tf_op jit(solution)/shard_map/ppermute | solution.py:388
  142.2 22.2 %copy-start.1 = (f32[256,768]{1,0:T(8,128)}, f32[256,768]{1,0:T(8,128)S(1)}, u32[]{:S(2)}) copy-start(f32[256,768]{1,0:T(8,128)S(1)} %factor0.1.refs_0_.refs_2_) | copy-start | bytes 2359300
  142.2 10.6 %copy-start.5 = (f32[512,512]{1,0:T(8,128)S(1)}, f32[512,512]{1,0:T(8,128)}, u32[]{:S(2)}) copy-start(f32[512,512]{1,0:T(8,128)} %copy-done.4) | copy-start | bytes 3145732
  146.9 21.2 %all-to-all-start.5 = ((f32[32,8,512]{2,1,0:T(8,128)}), f32[32,8,512]{2,1,0:T(8,128)S(1)}, u32[]{:S(2)}, u32[]{:S(2)}) async-start(f32[32,8,512]{2,1,0:T(8,128)} %fold.1), calls=%async_computation.5 | async-start | bytes 1048576 | tf_op jit(solution)/shard_map/all_to_all | solution.py:384
  168.2 6.6 %copy-start.8 = (f32[32,8,512]{2,1,0:T(8,128)}, f32[32,8,512]{2,1,0:T(8,128)S(1)}, u32[]{:S(2)}) copy-start(f32[32,8,512]{2,1,0:T(8,128)S(1)} %all-to-all-done.5) | copy-start | bytes 1572868
  168.2 6.6 %collective-permute-start.10 = (f32[256,512]{1,0:T(8,128)S(1)}, f32[256,512]{1,0:T(8,128)S(1)}, u32[]{:S(2)}, u32[]{:S(2)}) collective-permute-start(f32[256,512]{1,0:T(8,128)S(1)} %bitcast.16), channel_id=1, source_target_pairs={{0,8},{8,0},{1,9},{9,1},{2,10},{10,2},{3,11},{11,3},{4,12},{12,4},... | collective-permute-start | bytes 1572872 | tf_op jit(solution)/shard_map/ppermute | solution.py:388
  (3 other events, 2.7 us)
